TPU v7x, 32 devices: a whole 2x2x4 slice. The times are simulated.
32 devices in a mesh: gx: 2 (over y), gy: 4 (over z), gz: 4 (over x, core).
Axes of the slice: x: 2, y: 2, z: 4, core: 2. Of those that a mesh axis runs over, the one named last changes fastest.
Arguments:
- history: float32 [56, 32, 32, 256], P(None, 'gz', 'gy', 'gx'), may hold values from -6 to 6
- start: float32 [4, 32, 32, 256], P(None, 'gz', 'gy', 'gx'), may hold values from -51 to 51
- diagonal: float32 [32, 32, 256], P('gz', 'gy', 'gx'), may hold values from 0.25 to 2
Outputs:
- new_basis: float32 [20, 32, 32, 256], P(None, 'gz', 'gy', 'gx')
- r_factor: float32 [20, 20], replicated
All inputs are finite; a program needn't handle non-finite values.
Results may differ from a plain program's by a relative error of at most 0.0003.
Values sent between devices are 32-bit elements; how exact they have to be, the bound alone decides.
No kernel may reach another device: no remote copies, remote signals or barrier semaphores. Data moves between devices by JAX's collectives and lax.ppermute only.
A program may use at most 64 MiB of HBM per device.

v0:
```python
import jax
import jax.numpy as jnp
from jax import lax
from jax.sharding import PartitionSpec as P

STEPS = 4
HIST = 56
COLS = 20


def with_halo(block, sides, width):
    for axis, dim in sides:
        count = lax.axis_size(axis)
        forward = [(i, i + 1) for i in range(count - 1)]
        backward = [(target, source) for source, target in forward]
        low = lax.ppermute(
            lax.slice_in_dim(block, block.shape[dim] - width, None, axis=dim), axis, forward
        )
        high = lax.ppermute(lax.slice_in_dim(block, 0, width, axis=dim), axis, backward)
        block = jnp.concatenate([low, block, high], axis=dim)
    return block


def crop_cells(array, margin):
    return array[
        ...,
        margin : array.shape[-3] - margin,
        margin : array.shape[-2] - margin,
        margin : array.shape[-1] - margin,
    ]


def scaled_from_padded(padded, diag_inner, mask_inner):
    center = crop_cells(padded, 1)
    beside = padded[:, 2:, 1:-1, 1:-1] + padded[:, :-2, 1:-1, 1:-1]
    beside = beside + padded[:, 1:-1, 2:, 1:-1] + padded[:, 1:-1, :-2, 1:-1]
    beside = beside + padded[:, 1:-1, 1:-1, 2:] + padded[:, 1:-1, 1:-1, :-2]
    return ((6.0 + diag_inner[None]) * center - beside - 7.0 * center) / 7.0 * mask_inner


def on_device(history, start, diagonal):
    depth_z, depth_y, depth_x = diagonal.shape

    def scaled_step(field):
        padded = with_halo(field, (("gx", 3), ("gy", 2), ("gz", 1)), 1)
        return scaled_from_padded(padded, diagonal, 1.0)

    blocks = [start, scaled_step(start)]
    for level in range(1, STEPS):
        blocks.append(2.0 * scaled_step(blocks[level]) - blocks[level - 1])
    basis = jnp.concatenate(blocks, axis=0)
    cell_total = float(
        depth_z
        * depth_y
        * depth_x
        * lax.axis_size("gx")
        * lax.axis_size("gy")
        * lax.axis_size("gz")
    )
    flat_basis = basis.reshape(COLS, -1)
    flat_hist = history.reshape(HIST, -1)
    highest = lax.Precision.HIGHEST
    local_coef = jnp.dot(
        flat_hist, flat_basis.T, precision=highest, preferred_element_type=jnp.float32
    )
    coef = lax.psum(local_coef, ("gx", "gy", "gz")) / cell_total
    projected = flat_basis - jnp.dot(
        coef.T, flat_hist, precision=highest, preferred_element_type=jnp.float32
    )
    local_gram = jnp.dot(
        projected, projected.T, precision=highest, preferred_element_type=jnp.float32
    )
    gram = lax.psum(local_gram, ("gx", "gy", "gz")) / cell_total
    lower = jnp.linalg.cholesky(gram)
    solved = lax.linalg.triangular_solve(lower, projected, left_side=True, lower=True)
    return (solved.reshape(basis.shape), lower.T)


def solution(mesh):
    return jax.shard_map(
        on_device,
        mesh=mesh,
        in_specs=(P(None, "gz", "gy", "gx"), P(None, "gz", "gy", "gx"), P("gz", "gy", "gx")),
        out_specs=(P(None, "gz", "gy", "gx"), P()),
        check_vma=False,
    )
```

profile of v0, /device:TPU:0, one launch (start us, length us, event | category | flops | bytes accessed | tf_op | source)
XLA Modules:
  0.0 201.8 jit_solution(4397125938922040660)
XLA Ops:
  1.8 1.3 collective-permute-start.1
  3.1 4.9 %collective-permute-start = (f32[4,8,8,1]{3,2,1,0:T(8,128)S(1)}, f32[4,8,8,1]{3,2,1,0:T(8,128)S(1)}, u32[]{:S(2)}, u32[]{:S(2)}) collective-permute-start(f32[4,8,8,1]{3,2,1,0:T(8,128)S(1)} %get-tuple-element.33), channel_id=1, source_target_pairs={{0,16},{1,17},{2,18},{3,19},{4,20},{5,21},{6,22},{7,23},{8,24},{9,... | collective-permute-start | bytes 3080 | tf_op jit(solution)/shard_map/ppermute | solution.py:16
  8.0 1.6 collective-permute-done.1
  12.0 1.3 collective-permute-start.3
  13.3 5.0 %collective-permute-start.2 = (f32[4,8,1,130]{3,2,1,0:T(1,128)S(1)}, f32[4,8,1,130]{3,2,1,0:T(1,128)S(1)}, u32[]{:S(2)}, u32[]{:S(2)}) collective-permute-start(f32[4,8,1,130]{3,2,1,0:T(1,128)S(1)} %get-tuple-element.25), channel_id=1, source_target_pairs={{0,4},{4,8},{8,12},{1,5},{5,9},{9,13},{2,6},{6,10},{10,14},{3,7},{... | collective-permute-start | bytes 49928 | tf_op jit(solution)/shard_map/ppermute | solution.py:16
  18.3 1.6 collective-permute-done.2
  20.7 1.3 collective-permute-start.4
  22.0 3.0 %collective-permute-start.5 = (f32[4,1,10,130]{3,2,1,0:T(8,128)S(1)}, f32[4,1,10,130]{3,2,1,0:T(8,128)S(1)}, u32[]{:S(2)}, u32[]{:S(2)}) collective-permute-start(f32[4,1,10,130]{3,2,1,0:T(8,128)S(1)} %get-tuple-element.17), channel_id=1, source_target_pairs={{0,1},{1,2},{2,3},{4,5},{5,6},{6,7},{8,9},{9,10},{10,11},{12,13},{... | collective-permute-start | bytes 62408 | tf_op jit(solution)/shard_map/ppermute | solution.py:16
  25.9 2.1 %broadcast_multiply_fusion = (f32[4,8,8,128]{3,2,1,0:T(8,128)S(1)}, f32[4,8,8,128]{3,2,1,0:T(8,128)S(1)}) fusion(f32[4,8,8,128]{3,2,1,0:T(8,128)} %param.4, f32[4,8,8,1]{3,2,1,0:T(8,128)S(1)} %collective-permute-done, f32[4,8,8,1]{3,2,1,0:T(8,128)S(1)} %collective-permute-done.1, f32[4,8,1,130]{3,2,1,0:T(1,128)S(1)} %collective-permute-done.2, ...), kind=kLoop, calls=%fused_computation.137 | loop fusion | flops 917504 | bytes 502912 | tf_op jit(solution)/shard_map/div | solution.py:38
  29.4 4.6 %collective-permute-start.6 = (f32[4,8,8,1]{3,2,1,0:T(8,128)S(1)}, f32[4,8,8,1]{3,2,1,0:T(8,128)S(1)}, u32[]{:S(2)}, u32[]{:S(2)}) collective-permute-start(f32[4,8,8,1]{3,2,1,0:T(8,128)S(1)} %get-tuple-element.31), channel_id=1, source_target_pairs={{0,16},{1,17},{2,18},{3,19},{4,20},{5,21},{6,22},{7,23},{8,24},{9,... | collective-permute-start | bytes 3080 | tf_op jit(solution)/shard_map/ppermute | solution.py:16
  34.0 1.3 collective-permute-done.7
  35.3 1.8 collective-permute-done.6
  38.6 4.9 %collective-permute-start.8 = (f32[4,8,1,130]{3,2,1,0:T(1,128)S(1)}, f32[4,8,1,130]{3,2,1,0:T(1,128)S(1)}, u32[]{:S(2)}, u32[]{:S(2)}) collective-permute-start(f32[4,8,1,130]{3,2,1,0:T(1,128)S(1)} %get-tuple-element.23), channel_id=1, source_target_pairs={{0,4},{4,8},{8,12},{1,5},{5,9},{9,13},{2,6},{6,10},{10,14},{3,7},{... | collective-permute-start | bytes 49928 | tf_op jit(solution)/shard_map/ppermute | solution.py:16
  43.6 1.6 collective-permute-done.8
  46.6 3.0 %collective-permute-start.11 = (f32[4,1,10,130]{3,2,1,0:T(8,128)S(1)}, f32[4,1,10,130]{3,2,1,0:T(8,128)S(1)}, u32[]{:S(2)}, u32[]{:S(2)}) collective-permute-start(f32[4,1,10,130]{3,2,1,0:T(8,128)S(1)} %get-tuple-element.15), channel_id=1, source_target_pairs={{0,1},{1,2},{2,3},{4,5},{5,6},{6,7},{8,9},{9,10},{10,11},{12,13},{... | collective-permute-start | bytes 62408 | tf_op jit(solution)/shard_map/ppermute | solution.py:16
  52.4 4.6 %collective-permute-start.12 = (f32[4,8,8,1]{3,2,1,0:T(8,128)S(1)}, f32[4,8,8,1]{3,2,1,0:T(8,128)S(1)}, u32[]{:S(2)}, u32[]{:S(2)}) collective-permute-start(f32[4,8,8,1]{3,2,1,0:T(8,128)S(1)} %get-tuple-element.29), channel_id=1, source_target_pairs={{0,16},{1,17},{2,18},{3,19},{4,20},{5,21},{6,22},{7,23},{8,24},{9,... | collective-permute-start | bytes 3080 | tf_op jit(solution)/shard_map/ppermute | solution.py:16
  58.0 1.5 collective-permute-done.12
  61.0 5.0 %collective-permute-start.14 = (f32[4,8,1,130]{3,2,1,0:T(1,128)S(1)}, f32[4,8,1,130]{3,2,1,0:T(1,128)S(1)}, u32[]{:S(2)}, u32[]{:S(2)}) collective-permute-start(f32[4,8,1,130]{3,2,1,0:T(1,128)S(1)} %get-tuple-element.21), channel_id=1, source_target_pairs={{0,4},{4,8},{8,12},{1,5},{5,9},{9,13},{2,6},{6,10},{10,14},{3,7},{... | collective-permute-start | bytes 49928 | tf_op jit(solution)/shard_map/ppermute | solution.py:16
  66.1 1.6 collective-permute-done.14
  67.8 1.4 collective-permute-start.16
  69.2 4.0 %collective-permute-start.17 = (f32[4,1,10,130]{3,2,1,0:T(8,128)S(1)}, f32[4,1,10,130]{3,2,1,0:T(8,128)S(1)}, u32[]{:S(2)}, u32[]{:S(2)}) collective-permute-start(f32[4,1,10,130]{3,2,1,0:T(8,128)S(1)} %get-tuple-element.13), channel_id=1, source_target_pairs={{0,1},{1,2},{2,3},{4,5},{5,6},{6,7},{8,9},{9,10},{10,11},{12,13},{... | collective-permute-start | bytes 62408 | tf_op jit(solution)/shard_map/ppermute | solution.py:16
  76.0 4.6 %collective-permute-start.18 = (f32[4,8,8,1]{3,2,1,0:T(8,128)S(1)}, f32[4,8,8,1]{3,2,1,0:T(8,128)S(1)}, u32[]{:S(2)}, u32[]{:S(2)}) collective-permute-start(f32[4,8,8,1]{3,2,1,0:T(8,128)S(1)} %get-tuple-element.27), channel_id=1, source_target_pairs={{0,16},{1,17},{2,18},{3,19},{4,20},{5,21},{6,22},{7,23},{8,24},{9,... | collective-permute-start | bytes 3080 | tf_op jit(solution)/shard_map/ppermute | solution.py:16
  81.5 1.5 collective-permute-done.18
  84.6 4.6 %collective-permute-start.20 = (f32[4,8,1,130]{3,2,1,0:T(1,128)S(1)}, f32[4,8,1,130]{3,2,1,0:T(1,128)S(1)}, u32[]{:S(2)}, u32[]{:S(2)}) collective-permute-start(f32[4,8,1,130]{3,2,1,0:T(1,128)S(1)} %get-tuple-element.19), channel_id=1, source_target_pairs={{0,4},{4,8},{8,12},{1,5},{5,9},{9,13},{2,6},{6,10},{10,14},{3,7},{... | collective-permute-start | bytes 49928 | tf_op jit(solution)/shard_map/ppermute | solution.py:16
  89.2 1.6 collective-permute-done.20
  92.2 5.6 %collective-permute-start.23 = (f32[4,1,10,130]{3,2,1,0:T(8,128)S(1)}, f32[4,1,10,130]{3,2,1,0:T(8,128)S(1)}, u32[]{:S(2)}, u32[]{:S(2)}) collective-permute-start(f32[4,1,10,130]{3,2,1,0:T(8,128)S(1)} %get-tuple-element.11), channel_id=1, source_target_pairs={{0,1},{1,2},{2,3},{4,5},{5,6},{6,7},{8,9},{9,10},{10,11},{12,13},{... | collective-permute-start | bytes 62408 | tf_op jit(solution)/shard_map/ppermute | solution.py:16
  99.1 2.7 %fusion.4 = f32[56,20]{0,1:T(8,128)S(1)} fusion(f32[56,8,8,128]{3,2,1,0:T(8,128)S(1)} %copy-done, f32[20,8,8,128]{3,2,1,0:T(8,128)S(1)} %fusion.15), kind=kOutput, calls=%fused_computation.5 | convolution fusion | flops 110100480 | bytes 2494848 | tf_op jit(solution)/shard_map/dot_general | solution.py:63
  101.9 48.3 %psum.14 = f32[56,20]{0,1:T(8,128)S(1)} all-reduce(f32[56,20]{0,1:T(8,128)S(1)} %fusion.4), channel_id=1, replica_groups=mesh['gx'=2,'gy'=4,'gz'=4] {'gx','gy','gz'}, use_global_device_ids=true, to_apply=%region_0.0 | all-reduce | flops 1120 | bytes 8960 | tf_op jit(solution)/shard_map/psum | solution.py:66
  150.7 2.0 convolution_subtract_fusion
  153.7 40.3 %psum.15 = f32[20,20]{0,1:T(8,128)S(1)} all-reduce(f32[20,20]{0,1:T(8,128)S(1)} %fusion.58), channel_id=1, replica_groups=mesh['gx'=2,'gy'=4,'gz'=4] {'gx','gy','gz'}, use_global_device_ids=true, to_apply=%region_1.0 | all-reduce | flops 400 | bytes 3200 | tf_op jit(solution)/shard_map/psum | solution.py:73
  194.1 1.8 cholesky.16
  198.0 1.5 custom-call.6
  (59 shorter events, 28.9 us)
Async XLA Ops:
  0.6 42.9 %copy-start.1 = (f32[4,8,8,128]{3,2,1,0:T(8,128)S(1)}, f32[4,8,8,128]{3,2,1,0:T(8,128)}, u32[]{:S(2)}) copy-start(f32[4,8,8,128]{3,2,1,0:T(8,128)} %param.4) | copy-start | bytes 393220
  1.8 7.7 %collective-permute-start.1 = (f32[4,8,8,1]{3,2,1,0:T(8,128)S(1)}, f32[4,8,8,1]{3,2,1,0:T(8,128)S(1)}, u32[]{:S(2)}, u32[]{:S(2)}) collective-permute-start(f32[4,8,8,1]{3,2,1,0:T(8,128)S(1)} %get-tuple-element.32), channel_id=1, source_target_pairs={{16,0},{17,1},{18,2},{19,3},{20,4},{21,5},{22,6},{23,7},{24,8},{25... | collective-permute-start | bytes 3080 | tf_op jit(solution)/shard_map/ppermute | solution.py:19
  3.1 7.6 %collective-permute-start = (f32[4,8,8,1]{3,2,1,0:T(8,128)S(1)}, f32[4,8,8,1]{3,2,1,0:T(8,128)S(1)}, u32[]{:S(2)}, u32[]{:S(2)}) collective-permute-start(f32[4,8,8,1]{3,2,1,0:T(8,128)S(1)} %get-tuple-element.33), channel_id=1, source_target_pairs={{0,16},{1,17},{2,18},{3,19},{4,20},{5,21},{6,22},{7,23},{8,24},{9,... | collective-permute-start | bytes 3080 | tf_op jit(solution)/shard_map/ppermute | solution.py:16
  12.0 6.3 %collective-permute-start.3 = (f32[4,8,1,130]{3,2,1,0:T(1,128)S(1)}, f32[4,8,1,130]{3,2,1,0:T(1,128)S(1)}, u32[]{:S(2)}, u32[]{:S(2)}) collective-permute-start(f32[4,8,1,130]{3,2,1,0:T(1,128)S(1)} %get-tuple-element.24), channel_id=1, source_target_pairs={{4,0},{8,4},{12,8},{5,1},{9,5},{13,9},{6,2},{10,6},{14,10},{7,3},{... | collective-permute-start | bytes 49928 | tf_op jit(solution)/shard_map/ppermute | solution.py:19
  13.3 6.6 %collective-permute-start.2 = (f32[4,8,1,130]{3,2,1,0:T(1,128)S(1)}, f32[4,8,1,130]{3,2,1,0:T(1,128)S(1)}, u32[]{:S(2)}, u32[]{:S(2)}) collective-permute-start(f32[4,8,1,130]{3,2,1,0:T(1,128)S(1)} %get-tuple-element.25), channel_id=1, source_target_pairs={{0,4},{4,8},{8,12},{1,5},{5,9},{9,13},{2,6},{6,10},{10,14},{3,7},{... | collective-permute-start | bytes 49928 | tf_op jit(solution)/shard_map/ppermute | solution.py:16
  20.7 5.1 %collective-permute-start.4 = (f32[4,1,10,130]{3,2,1,0:T(8,128)S(1)}, f32[4,1,10,130]{3,2,1,0:T(8,128)S(1)}, u32[]{:S(2)}, u32[]{:S(2)}) collective-permute-start(f32[4,1,10,130]{3,2,1,0:T(8,128)S(1)} %get-tuple-element.16), channel_id=1, source_target_pairs={{1,0},{2,1},{3,2},{5,4},{6,5},{7,6},{9,8},{10,9},{11,10},{13,12},{... | collective-permute-start | bytes 62408 | tf_op jit(solution)/shard_map/ppermute | solution.py:19
  22.0 3.9 %collective-permute-start.5 = (f32[4,1,10,130]{3,2,1,0:T(8,128)S(1)}, f32[4,1,10,130]{3,2,1,0:T(8,128)S(1)}, u32[]{:S(2)}, u32[]{:S(2)}) collective-permute-start(f32[4,1,10,130]{3,2,1,0:T(8,128)S(1)} %get-tuple-element.17), channel_id=1, source_target_pairs={{0,1},{1,2},{2,3},{4,5},{5,6},{6,7},{8,9},{9,10},{10,11},{12,13},{... | collective-permute-start | bytes 62408 | tf_op jit(solution)/shard_map/ppermute | solution.py:16
  28.1 7.2 %collective-permute-start.7 = (f32[4,8,8,1]{3,2,1,0:T(8,128)S(1)}, f32[4,8,8,1]{3,2,1,0:T(8,128)S(1)}, u32[]{:S(2)}, u32[]{:S(2)}) collective-permute-start(f32[4,8,8,1]{3,2,1,0:T(8,128)S(1)} %get-tuple-element.30), channel_id=1, source_target_pairs={{16,0},{17,1},{18,2},{19,3},{20,4},{21,5},{22,6},{23,7},{24,8},{25... | collective-permute-start | bytes 3080 | tf_op jit(solution)/shard_map/ppermute | solution.py:19
  29.4 7.6 %collective-permute-start.6 = (f32[4,8,8,1]{3,2,1,0:T(8,128)S(1)}, f32[4,8,8,1]{3,2,1,0:T(8,128)S(1)}, u32[]{:S(2)}, u32[]{:S(2)}) collective-permute-start(f32[4,8,8,1]{3,2,1,0:T(8,128)S(1)} %get-tuple-element.31), channel_id=1, source_target_pairs={{0,16},{1,17},{2,18},{3,19},{4,20},{5,21},{6,22},{7,23},{8,24},{9,... | collective-permute-start | bytes 3080 | tf_op jit(solution)/shard_map/ppermute | solution.py:16
  37.3 6.2 %collective-permute-start.9 = (f32[4,8,1,130]{3,2,1,0:T(1,128)S(1)}, f32[4,8,1,130]{3,2,1,0:T(1,128)S(1)}, u32[]{:S(2)}, u32[]{:S(2)}) collective-permute-start(f32[4,8,1,130]{3,2,1,0:T(1,128)S(1)} %get-tuple-element.22), channel_id=1, source_target_pairs={{4,0},{8,4},{12,8},{5,1},{9,5},{13,9},{6,2},{10,6},{14,10},{7,3},{... | collective-permute-start | bytes 49928 | tf_op jit(solution)/shard_map/ppermute | solution.py:19
  38.6 6.6 %collective-permute-start.8 = (f32[4,8,1,130]{3,2,1,0:T(1,128)S(1)}, f32[4,8,1,130]{3,2,1,0:T(1,128)S(1)}, u32[]{:S(2)}, u32[]{:S(2)}) collective-permute-start(f32[4,8,1,130]{3,2,1,0:T(1,128)S(1)} %get-tuple-element.23), channel_id=1, source_target_pairs={{0,4},{4,8},{8,12},{1,5},{5,9},{9,13},{2,6},{6,10},{10,14},{3,7},{... | collective-permute-start | bytes 49928 | tf_op jit(solution)/shard_map/ppermute | solution.py:16
  45.3 4.4 %collective-permute-start.10 = (f32[4,1,10,130]{3,2,1,0:T(8,128)S(1)}, f32[4,1,10,130]{3,2,1,0:T(8,128)S(1)}, u32[]{:S(2)}, u32[]{:S(2)}) collective-permute-start(f32[4,1,10,130]{3,2,1,0:T(8,128)S(1)} %get-tuple-element.14), channel_id=1, source_target_pairs={{1,0},{2,1},{3,2},{5,4},{6,5},{7,6},{9,8},{10,9},{11,10},{13,12},{... | collective-permute-start | bytes 62408 | tf_op jit(solution)/shard_map/ppermute | solution.py:19
  46.6 3.9 %collective-permute-start.11 = (f32[4,1,10,130]{3,2,1,0:T(8,128)S(1)}, f32[4,1,10,130]{3,2,1,0:T(8,128)S(1)}, u32[]{:S(2)}, u32[]{:S(2)}) collective-permute-start(f32[4,1,10,130]{3,2,1,0:T(8,128)S(1)} %get-tuple-element.15), channel_id=1, source_target_pairs={{0,1},{1,2},{2,3},{4,5},{5,6},{6,7},{8,9},{9,10},{10,11},{12,13},{... | collective-permute-start | bytes 62408 | tf_op jit(solution)/shard_map/ppermute | solution.py:16
  51.1 6.9 %collective-permute-start.13 = (f32[4,8,8,1]{3,2,1,0:T(8,128)S(1)}, f32[4,8,8,1]{3,2,1,0:T(8,128)S(1)}, u32[]{:S(2)}, u32[]{:S(2)}) collective-permute-start(f32[4,8,8,1]{3,2,1,0:T(8,128)S(1)} %get-tuple-element.28), channel_id=1, source_target_pairs={{16,0},{17,1},{18,2},{19,3},{20,4},{21,5},{22,6},{23,7},{24,8},{25... | collective-permute-start | bytes 3080 | tf_op jit(solution)/shard_map/ppermute | solution.py:19
  52.4 7.1 %collective-permute-start.12 = (f32[4,8,8,1]{3,2,1,0:T(8,128)S(1)}, f32[4,8,8,1]{3,2,1,0:T(8,128)S(1)}, u32[]{:S(2)}, u32[]{:S(2)}) collective-permute-start(f32[4,8,8,1]{3,2,1,0:T(8,128)S(1)} %get-tuple-element.29), channel_id=1, source_target_pairs={{0,16},{1,17},{2,18},{3,19},{4,20},{5,21},{6,22},{7,23},{8,24},{9,... | collective-permute-start | bytes 3080 | tf_op jit(solution)/shard_map/ppermute | solution.py:16
  59.7 6.3 %collective-permute-start.15 = (f32[4,8,1,130]{3,2,1,0:T(1,128)S(1)}, f32[4,8,1,130]{3,2,1,0:T(1,128)S(1)}, u32[]{:S(2)}, u32[]{:S(2)}) collective-permute-start(f32[4,8,1,130]{3,2,1,0:T(1,128)S(1)} %get-tuple-element.20), channel_id=1, source_target_pairs={{4,0},{8,4},{12,8},{5,1},{9,5},{13,9},{6,2},{10,6},{14,10},{7,3},{... | collective-permute-start | bytes 49928 | tf_op jit(solution)/shard_map/ppermute | solution.py:19
  61.0 6.6 %collective-permute-start.14 = (f32[4,8,1,130]{3,2,1,0:T(1,128)S(1)}, f32[4,8,1,130]{3,2,1,0:T(1,128)S(1)}, u32[]{:S(2)}, u32[]{:S(2)}) collective-permute-start(f32[4,8,1,130]{3,2,1,0:T(1,128)S(1)} %get-tuple-element.21), channel_id=1, source_target_pairs={{0,4},{4,8},{8,12},{1,5},{5,9},{9,13},{2,6},{6,10},{10,14},{3,7},{... | collective-permute-start | bytes 49928 | tf_op jit(solution)/shard_map/ppermute | solution.py:16
  67.8 31.4 %copy-start = (f32[56,8,8,128]{3,2,1,0:T(8,128)S(1)}, f32[56,8,8,128]{3,2,1,0:T(8,128)}, u32[]{:S(2)}) copy-start(f32[56,8,8,128]{3,2,1,0:T(8,128)} %param.3) | copy-start | bytes 5505028
  67.8 5.5 %collective-permute-start.16 = (f32[4,1,10,130]{3,2,1,0:T(8,128)S(1)}, f32[4,1,10,130]{3,2,1,0:T(8,128)S(1)}, u32[]{:S(2)}, u32[]{:S(2)}) collective-permute-start(f32[4,1,10,130]{3,2,1,0:T(8,128)S(1)} %get-tuple-element.12), channel_id=1, source_target_pairs={{1,0},{2,1},{3,2},{5,4},{6,5},{7,6},{9,8},{10,9},{11,10},{13,12},{... | collective-permute-start | bytes 62408 | tf_op jit(solution)/shard_map/ppermute | solution.py:19
  69.2 4.9 %collective-permute-start.17 = (f32[4,1,10,130]{3,2,1,0:T(8,128)S(1)}, f32[4,1,10,130]{3,2,1,0:T(8,128)S(1)}, u32[]{:S(2)}, u32[]{:S(2)}) collective-permute-start(f32[4,1,10,130]{3,2,1,0:T(8,128)S(1)} %get-tuple-element.13), channel_id=1, source_target_pairs={{0,1},{1,2},{2,3},{4,5},{5,6},{6,7},{8,9},{9,10},{10,11},{12,13},{... | collective-permute-start | bytes 62408 | tf_op jit(solution)/shard_map/ppermute | solution.py:16
  74.7 6.9 %collective-permute-start.19 = (f32[4,8,8,1]{3,2,1,0:T(8,128)S(1)}, f32[4,8,8,1]{3,2,1,0:T(8,128)S(1)}, u32[]{:S(2)}, u32[]{:S(2)}) collective-permute-start(f32[4,8,8,1]{3,2,1,0:T(8,128)S(1)} %get-tuple-element.26), channel_id=1, source_target_pairs={{16,0},{17,1},{18,2},{19,3},{20,4},{21,5},{22,6},{23,7},{24,8},{25... | collective-permute-start | bytes 3080 | tf_op jit(solution)/shard_map/ppermute | solution.py:19
  76.0 7.1 %collective-permute-start.18 = (f32[4,8,8,1]{3,2,1,0:T(8,128)S(1)}, f32[4,8,8,1]{3,2,1,0:T(8,128)S(1)}, u32[]{:S(2)}, u32[]{:S(2)}) collective-permute-start(f32[4,8,8,1]{3,2,1,0:T(8,128)S(1)} %get-tuple-element.27), channel_id=1, source_target_pairs={{0,16},{1,17},{2,18},{3,19},{4,20},{5,21},{6,22},{7,23},{8,24},{9,... | collective-permute-start | bytes 3080 | tf_op jit(solution)/shard_map/ppermute | solution.py:16
  83.3 5.9 %collective-permute-start.21 = (f32[4,8,1,130]{3,2,1,0:T(1,128)S(1)}, f32[4,8,1,130]{3,2,1,0:T(1,128)S(1)}, u32[]{:S(2)}, u32[]{:S(2)}) collective-permute-start(f32[4,8,1,130]{3,2,1,0:T(1,128)S(1)} %get-tuple-element.18), channel_id=1, source_target_pairs={{4,0},{8,4},{12,8},{5,1},{9,5},{13,9},{6,2},{10,6},{14,10},{7,3},{... | collective-permute-start | bytes 49928 | tf_op jit(solution)/shard_map/ppermute | solution.py:19
  84.6 6.1 %collective-permute-start.20 = (f32[4,8,1,130]{3,2,1,0:T(1,128)S(1)}, f32[4,8,1,130]{3,2,1,0:T(1,128)S(1)}, u32[]{:S(2)}, u32[]{:S(2)}) collective-permute-start(f32[4,8,1,130]{3,2,1,0:T(1,128)S(1)} %get-tuple-element.19), channel_id=1, source_target_pairs={{0,4},{4,8},{8,12},{1,5},{5,9},{9,13},{2,6},{6,10},{10,14},{3,7},{... | collective-permute-start | bytes 49928 | tf_op jit(solution)/shard_map/ppermute | solution.py:16
  90.9 6.9 %collective-permute-start.22 = (f32[4,1,10,130]{3,2,1,0:T(8,128)S(1)}, f32[4,1,10,130]{3,2,1,0:T(8,128)S(1)}, u32[]{:S(2)}, u32[]{:S(2)}) collective-permute-start(f32[4,1,10,130]{3,2,1,0:T(8,128)S(1)} %get-tuple-element.10), channel_id=1, source_target_pairs={{1,0},{2,1},{3,2},{5,4},{6,5},{7,6},{9,8},{10,9},{11,10},{13,12},{... | collective-permute-start | bytes 62408 | tf_op jit(solution)/shard_map/ppermute | solution.py:19
  92.2 6.5 %collective-permute-start.23 = (f32[4,1,10,130]{3,2,1,0:T(8,128)S(1)}, f32[4,1,10,130]{3,2,1,0:T(8,128)S(1)}, u32[]{:S(2)}, u32[]{:S(2)}) collective-permute-start(f32[4,1,10,130]{3,2,1,0:T(8,128)S(1)} %get-tuple-element.11), channel_id=1, source_target_pairs={{0,1},{1,2},{2,3},{4,5},{5,6},{6,7},{8,9},{9,10},{10,11},{12,13},{... | collective-permute-start | bytes 62408 | tf_op jit(solution)/shard_map/ppermute | solution.py:16
where the time goes:
time: 203 us; the launch traced here: 202 us
  blocking collectives  88.7 us (44%)
  starting transfers between devices  69.3 us (34%)
  waiting for transfers between devices  19.9 us (10%)
  other arithmetic  12.1 us (6%)
  matrix products  6.76 us (3%)
  local copies, waits for them, and re-layouts  3.91 us (2%)
    ppermute x12, starting transfers between devices, with_halo(): lax.ppermute(lax.slice_in_dim(block, block.shape[dim] - width, None, axis...  53.7 us
    psum x1, blocking collectives, on_device(): coef = lax.psum(local_coef, ('gx', 'gy', 'gz')) / cell_total  48.3 us
    psum x1, blocking collectives, on_device(): gram = lax.psum(local_gram, ('gx', 'gy', 'gz')) / cell_total  40.3 us
    ppermute x12, starting transfers between devices, with_halo(): lax.ppermute(lax.slice_in_dim(block, 0, width, axis=dim), axis, backward)  15.6 us
    ppermute x12, waiting for transfers between devices, with_halo(): lax.ppermute(lax.slice_in_dim(block, block.shape[dim] - width, None, axis...  15 us
    ppermute x12, waiting for transfers between devices, with_halo(): lax.ppermute(lax.slice_in_dim(block, 0, width, axis=dim), axis, backward)  4.92 us
  transfers between devices with their start and end apart: 24, of which 17 were waited for; matrix products, arithmetic and copies ran while one was open for 0% of the time, Pallas kernels for 0%

commit v1 on v0

v1 whole, which is shorter than its diff:
```python
import functools

import jax
import jax.numpy as jnp
from jax import lax
from jax.experimental import pallas as pl
from jax.experimental.pallas import tpu as pltpu
from jax.sharding import PartitionSpec as P

STEPS = 4
F32 = jnp.float32
BF16 = jnp.bfloat16
AXES = ("gx", "gy", "gz")
HIGHEST = lax.Precision.HIGHEST
Z, Y, X = 8, 8, 128
CELLS = Z * Y
SLOTS = 16
BPAD = 32
HPAD = 64


def roll(tile, shift, axis):
    shift %= tile.shape[axis]
    return pltpu.roll(tile, shift, axis) if shift else tile


def iotas():
    return (
        lax.broadcasted_iota(jnp.int32, (Y, X), 0),
        lax.broadcasted_iota(jnp.int32, (Y, X), 1),
    )


def is_even(axis):
    return lax.rem(lax.axis_index(axis), 2) == 0


def facing(axis, count, received):
    index = lax.axis_index(axis)
    even = lax.rem(index, 2) == 0
    low_there, high_there = index > 0, index < count - 1

    def pick(k):
        first = received[0][k]
        if len(received) == 1:
            return jnp.where(even, 0.0, first), jnp.where(even, first, 0.0)
        second = received[1][k]
        low = jnp.where(low_there, jnp.where(even, second, first), 0.0)
        high = jnp.where(high_there, jnp.where(even, first, second), 0.0)
        return low, high

    return pick


def swaps(arrays, axis, count):
    first = [(i, i ^ 1) for i in range(count)]
    second = [(i, (i + 1 if i % 2 else i - 1) % count) for i in range(count)]
    return [lax.ppermute(a, axis, pairs) for a, pairs in zip(arrays, (first, second))]


def pack_x(fields, start, diagonal, *sends):
    _, lane = iotas()
    even = is_even("gx")
    for f in range(fields + 1):
        to_high = jnp.zeros((Y, X), F32)
        to_low = to_high
        for z in range(Z):
            tile = start[f, z] if f < fields else diagonal[z]
            base = 8 * z
            to_high = jnp.where(
                (lane >= base + 1) & (lane < base + 5), roll(tile, base + 5, 1), to_high
            )
            to_low = jnp.where(
                (lane >= base + 3) & (lane < base + 7), roll(tile, base + 3, 1), to_low
            )
        sends[0][f] = jnp.where(even, to_high, to_low)
        if len(sends) > 1:
            sends[1][f] = jnp.where(even, to_low, to_high)


def pack_y(fields, count, ways, start, diagonal, *refs):
    received, (sides, *sends) = refs[:ways], refs[ways:]
    row, lane = iotas()
    column = lane & 7
    pick = facing("gx", count, received)
    even = is_even("gy")
    half = lane < X // 2

    def send(k, one, two):
        one_turned, two_turned = roll(one, 4, 0), roll(two, 4, 0)
        to_high = jnp.where(row < 4, one_turned, two)
        to_low = jnp.where(row < 4, one, two_turned)
        sends[0][k] = jnp.where(even, to_high, to_low)
        if len(sends) > 1:
            sends[1][k] = jnp.where(even, to_low, to_high)

    for f in range(fields + 1):
        tiles = [start[f, z] if f < fields else diagonal[z] for z in range(Z)]
        low, high = pick(f)
        side = jnp.where(half & (column >= 1) & (column <= 4), low, 0.0)
        side = jnp.where(
            jnp.logical_not(half) & (column >= 3) & (column <= 6), roll(high, 64, 1), side
        )
        for z in range(Z):
            base = 8 * z
            side = jnp.where(
                (lane >= base + 5) & (lane < base + 8), roll(tiles[z], base + 5, 1), side
            )
            side = jnp.where(
                (lane >= base + 64) & (lane < base + 67), roll(tiles[z], base + 67, 1), side
            )
        sides[f] = side
        for p in range(4):
            send(4 * f + p, tiles[p], tiles[p + 4])
    for f in range(0, fields + 1, 2):
        send(4 * (fields + 1) + f // 2, sides[f], sides[min(f + 1, fields)])


def pack_z(fields, count, ways, start, diagonal, sides, *refs):
    received, (beyond, beyond_sides, *sends) = refs[:ways], refs[ways:]
    row, lane = iotas()
    pick = facing("gy", count, received)
    even = is_even("gz")
    upper = row < 4

    def unpack(k):
        low, high = pick(k)
        return (
            jnp.where(upper, high, roll(low, 4, 0)),
            jnp.where(upper, roll(high, 4, 0), low),
        )

    for f in range(fields + 1):
        for p in range(4):
            beyond[f, p], beyond[f, p + 4] = unpack(4 * f + p)
    for f in range(0, fields + 1, 2):
        one, two = unpack(4 * (fields + 1) + f // 2)
        beyond_sides[f] = one
        if f < fields:
            beyond_sides[f + 1] = two

    inner = (row == 2) | (row == 3)
    quarter = (lane & 32) == 0
    for which, ref in enumerate(sends):
        up = even if which == 0 else jnp.logical_not(even)
        at = [None] + [jnp.where(up, Z - d, d - 1) for d in range(1, 5)]
        k = 0
        for f in range(fields):
            for d in range(1, 5):
                ref[k] = start[f, at[d]]
                k += 1
            ref[k] = beyond[f, at[1]]
            ref[k + 1] = jnp.where(inner, roll(beyond[f, at[3]], 3, 0), beyond[f, at[2]])
            k += 2
        for d in range(1, 4):
            ref[k] = diagonal[at[d]]
            k += 1
        ref[k] = jnp.where(inner, roll(beyond[fields, at[2]], 3, 0), beyond[fields, at[1]])
        k += 1
        for source in (sides, beyond_sides):
            for f in range(0, fields + 1, 2):
                one, two = source[f], source[min(f + 1, fields)]
                to_high = jnp.where(quarter, roll(one, -32, 1), two)
                to_low = jnp.where(quarter, one, roll(two, 32, 1))
                ref[k] = jnp.where(up, to_high, to_low)
                k += 1


def z_tiles(fields):
    return 6 * fields + 4 + 2 * ((fields + 2) // 2)


def powers(fields, count, ways, start, diagonal, sides, beyond, beyond_sides, *refs):
    received = refs[:ways]
    history_split, history_gram, split, sums = refs[ways : ways + 4]
    halo, center, ends, coef_a, coef_b = refs[ways + 4 :]
    columns = fields * (STEPS + 1)
    row, lane = iotas()
    pick = facing("gz", count, received)

    own = set(range(Z))
    k = 0
    for f in range(fields):
        for z in range(Z):
            center[pl.ds(f * CELLS + z * Y, Y), :] = start[f, z]
            halo[0, f, z, 1] = beyond[f, z]
        for d in range(1, 5):
            halo[0, f, SLOTS - d, 0], halo[0, f, Z - 1 + d, 0] = pick(k)
            k += 1
        halo[0, f, SLOTS - 1, 1], halo[0, f, Z, 1] = pick(k)
        low, high = pick(k + 1)
        halo[0, f, SLOTS - 2, 1], halo[0, f, Z + 1, 1] = low, high
        halo[0, f, SLOTS - 3, 1], halo[0, f, Z + 2, 1] = roll(low, -3, 0), roll(high, -3, 0)
        k += 2

    def coefficients(d):
        inside = d > 0.0
        return jnp.where(inside, (d - 1.0) * (1.0 / 7.0), 0.0), jnp.where(inside, 1.0 / 7.0, 0.0)

    for z in range(Z):
        coef_a[z, 0] = (diagonal[z] - 1.0) * (1.0 / 7.0)
        coef_a[z, 1], coef_b[z, 1] = coefficients(beyond[fields, z])
    for d in range(1, 4):
        low, high = pick(k)
        coef_a[SLOTS - d, 0], coef_b[SLOTS - d, 0] = coefficients(low)
        coef_a[Z - 1 + d, 0], coef_b[Z - 1 + d, 0] = coefficients(high)
        k += 1
    low, high = pick(k)
    k += 1
    coef_a[SLOTS - 1, 1], coef_b[SLOTS - 1, 1] = coefficients(low)
    coef_a[Z, 1], coef_b[Z, 1] = coefficients(high)
    coef_a[SLOTS - 2, 1], coef_b[SLOTS - 2, 1] = coefficients(roll(low, -3, 0))
    coef_a[Z + 1, 1], coef_b[Z + 1, 1] = coefficients(roll(high, -3, 0))

    end_coefs = {}
    for part, source in enumerate((sides, beyond_sides)):
        for f in range(0, fields + 1, 2):
            low, high = pick(k)
            k += 1
            for g in (f, f + 1):
                if g > fields:
                    continue
                shift = 32 * (g - f)
                mine = source[g]
                left = jnp.where(
                    lane < 64,
                    mine,
                    jnp.where(lane < 96, roll(high, 64 - shift, 1), roll(low, 96 - shift, 1)),
                )
                right = jnp.where(
                    lane < 64,
                    roll(mine, 64, 1),
                    jnp.where(lane < 96, roll(high, -shift, 1), roll(low, 32 - shift, 1)),
                )
                if g < fields:
                    ends[0, 0, g, part], ends[0, 1, g, part] = left, right
                else:
                    end_coefs[0, part], end_coefs[1, part] = coefficients(left), coefficients(right)

    def read(level, f, z, part):
        if part == 0 and z in own:
            return center[pl.ds((fields * level + f) * CELLS + z * Y, Y), :]
        return halo[level, f, z, part]

    def beside_y(mine, other):
        above, above_other = roll(mine, -1, 0), roll(other, -1, 0)
        below, below_other = roll(mine, 1, 0), roll(other, 1, 0)
        last, first = row == Y - 1, row == 0
        return (
            jnp.where(last, above_other, above) + jnp.where(first, below_other, below),
            jnp.where(last, above, above_other) + jnp.where(first, below, below_other),
        )

    for level in range(1, STEPS + 1):
        reach = STEPS - level
        for f in range(fields):
            joined = [
                jnp.where((lane & 7) <= 3, ends[level - 1, 1, f, p], ends[level - 1, 0, f, p])
                for p in range(2)
            ]
            for at in range(-reach, Z + reach):
                z, before, after = at % SLOTS, (at - 1) % SLOTS, (at + 1) % SLOTS
                distance = max(-at, at - Z + 1, 0)
                tiles = [read(level - 1, f, z, p) for p in range(2)]
                along_y = beside_y(*tiles)
                for part in range(2 if distance < reach else 1):
                    tile = tiles[part]
                    end = roll(joined[part], 124 - 8 * z, 1)
                    total = jnp.where(lane == 0, end, roll(tile, 1, 1))
                    total = total + jnp.where(lane == X - 1, end, roll(tile, -1, 1))
                    total = total + along_y[part]
                    total = total + read(level - 1, f, before, part)
                    total = total + read(level - 1, f, after, part)
                    if part == 0 and z in own:
                        value = coef_a[z, 0] * tile - (1.0 / 7.0) * total
                    else:
                        value = coef_a[z, part] * tile - coef_b[z, part] * total
                    if level > 1:
                        value = value + value - read(level - 2, f, z, part)
                    if part == 0 and z in own:
                        center[pl.ds((fields * level + f) * CELLS + z * Y, Y), :] = value
                    else:
                        halo[level, f, z, part] = value
            if level < STEPS:
                for side in range(2):
                    tiles = [ends[level - 1, side, f, p] for p in range(2)]
                    along_y = beside_y(*tiles)
                    for part in range(2):
                        tile = tiles[part]
                        total = roll(tile, 1, 1) + roll(tile, -1, 1) + along_y[part]
                        total = total + roll(tile, 8, 1) + roll(tile, -8, 1)
                        a, b = end_coefs[side, part]
                        value = a * tile - b * total
                        if level > 1:
                            value = value + value - ends[level - 2, side, f, part]
                        ends[level, side, f, part] = value

    center[pl.ds(columns * CELLS, (24 - columns) * CELLS), :] = jnp.zeros(
        ((24 - columns) * CELLS, X), F32
    )
    for cell in range(CELLS):
        high, low = split_rows(center[pl.ds(cell, 24, stride=CELLS), :], BPAD)
        split[0:BPAD, cell * X : (cell + 1) * X] = high
        split[BPAD : 2 * BPAD, cell * X : (cell + 1) * X] = low
    basis = product(split[...], split[...])
    cross = product(history_split[...], split[...])
    basis = join(join(basis, BPAD).T, BPAD)
    cross = join(join(cross, HPAD).T, BPAD).T
    sums[:, 0:HPAD] = history_gram[...]
    sums[:, HPAD : HPAD + BPAD] = cross
    sums[0:BPAD, HPAD + BPAD :] = basis
    sums[BPAD:, HPAD + BPAD :] = jnp.zeros((HPAD - BPAD, BPAD), F32)


def split_rows(rows, padded):
    rows = jnp.concatenate([rows, jnp.zeros((padded - rows.shape[0], rows.shape[1]), F32)], axis=0)
    high = rows.astype(BF16)
    return high, (rows - high.astype(F32)).astype(BF16)


def product(left, right):
    return lax.dot_general(left, right, (((1,), (1,)), ((), ())), preferred_element_type=F32)


def join(both, padded):
    return both[:padded] + both[padded:]


def history_kernel(count, history, split, gram):
    for cell in range(CELLS):
        high, low = split_rows(history[pl.ds(cell, count, stride=CELLS), :], HPAD)
        split[0:HPAD, cell * X : (cell + 1) * X] = high
        split[HPAD : 2 * HPAD, cell * X : (cell + 1) * X] = low
    gram[...] = join(join(product(split[...], split[...]), HPAD).T, HPAD)


def split_matrix(matrix):
    high = matrix.astype(BF16)
    return high, (matrix - high.astype(F32)).astype(BF16)


def finish(columns, cells, history_split, split, *refs):
    parts, (out, factor) = refs[:-2], refs[-2:]
    total = (parts[0][...] + parts[1][...]) + (parts[2][...] + parts[3][...])
    total = total * (1.0 / cells)
    history_gram = total[:, 0:HPAD]
    coef = total[:, HPAD : HPAD + BPAD]
    basis_gram = total[0:BPAD, HPAD + BPAD :]
    inner = jnp.dot(history_gram, coef, precision=HIGHEST, preferred_element_type=F32)
    gram = basis_gram + lax.dot_general(
        coef, inner - 2.0 * coef, (((0,), (0,)), ((), ())), precision=HIGHEST, preferred_element_type=F32
    )
    row = lax.broadcasted_iota(jnp.int32, (BPAD, X), 0)
    lane = lax.broadcasted_iota(jnp.int32, (BPAD, X), 1)
    work = jnp.concatenate(
        [gram, jnp.zeros((BPAD, X - BPAD), F32)], axis=1
    )
    work = jnp.where(lane == row + BPAD, 1.0, work)
    for k in range(columns):
        pivot_row = work[k : k + 1, :]
        scale = work[:, k : k + 1] / pivot_row[:, k : k + 1]
        work = work - jnp.where(row > k, scale, 0.0) * pivot_row
    pivots = jnp.sum(jnp.where(lane == row, work, 0.0), axis=1, keepdims=True)
    good = lax.broadcasted_iota(jnp.int32, (BPAD, 1), 0) < columns
    work = work * jnp.where(good, 1.0 / jnp.sqrt(jnp.where(good, pivots, 1.0)), 0.0)
    factor[...] = jnp.where(lane >= row, work, 0.0)[0:columns, 0:columns]
    inverse = work[:, BPAD : 2 * BPAD]
    onto_history = -lax.dot_general(
        inverse, coef, (((1,), (1,)), ((), ())), precision=HIGHEST, preferred_element_type=F32
    )
    history_high, history_low = split_matrix(onto_history)
    basis_high, basis_low = split_matrix(inverse)
    left = jnp.concatenate(
        [
            jnp.concatenate([history_high, history_high, basis_high, basis_high], axis=1),
            jnp.concatenate(
                [history_low, jnp.zeros_like(history_low), basis_low, jnp.zeros_like(basis_low)], axis=1
            ),
        ],
        axis=0,
    )
    width = 4 * X
    for c in range(CELLS * X // width):
        at = slice(c * width, (c + 1) * width)
        right = jnp.concatenate([history_split[:, at], split[:, at]], axis=0)
        result = join(jnp.dot(left, right, preferred_element_type=F32), BPAD)
        for j in range(width // X):
            out[pl.ds(c * (width // X) + j, columns, stride=CELLS), :] = result[
                0:columns, j * X : (j + 1) * X
            ]


def call(kernel, outs, flops, bytes_accessed, scratch=()):
    return pl.pallas_call(
        kernel,
        out_shape=[jax.ShapeDtypeStruct(shape, dtype) for shape, dtype in outs],
        scratch_shapes=list(scratch),
        compiler_params=pltpu.CompilerParams(vmem_limit_bytes=40 * 1024 * 1024),
        cost_estimate=pl.CostEstimate(flops=flops, bytes_accessed=bytes_accessed, transcendentals=0),
    )


def exchange_sums(array, sizes, bits):
    count = sizes[0] * sizes[1] * sizes[2]
    arrays = [array]
    for mask in range(1, 1 << len(bits)):
        flip = sum(bit for i, bit in enumerate(bits) if mask >> i & 1)
        arrays.append(lax.ppermute(array, AXES, [(i, i ^ flip) for i in range(count)]))
    return arrays


def on_device(sizes, history, start, diagonal):
    fields, history_count = start.shape[0], history.shape[0]
    columns = fields * (STEPS + 1)
    all_fields = fields + 1
    count = dict(zip(AXES, sizes))
    ways = {axis: 1 if size == 2 else 2 for axis, size in count.items()}
    cells = Z * Y * X * sizes[0] * sizes[1] * sizes[2]
    tile = Y * X * 4

    with jax.named_scope("history_products"):
        history_split, history_gram = call(
            functools.partial(history_kernel, history_count),
            [((2 * HPAD, CELLS * X), BF16), ((HPAD, HPAD), F32)],
            2 * 128 * 128 * CELLS * X,
            history.size * 4 * 2,
        )(history.reshape(history_count * CELLS, X))

    with jax.named_scope("halo_x"):
        sends = call(
            functools.partial(pack_x, fields),
            [((all_fields, Y, X), F32)] * ways["gx"],
            1000,
            start.size * 4,
        )(start, diagonal)
        received = swaps(sends, "gx", count["gx"])
    with jax.named_scope("halo_y"):
        y_tiles = 4 * all_fields + (all_fields + 1) // 2
        sides, *sends = call(
            functools.partial(pack_y, fields, count["gx"], ways["gx"]),
            [((all_fields, Y, X), F32)] + [((y_tiles, Y, X), F32)] * ways["gy"],
            1000,
            start.size * 4,
        )(start, diagonal, *received)
        received = swaps(sends, "gy", count["gy"])
    with jax.named_scope("halo_z"):
        beyond, beyond_sides, *sends = call(
            functools.partial(pack_z, fields, count["gy"], ways["gy"]),
            [((all_fields, Z, Y, X), F32), ((all_fields, Y, X), F32)]
            + [((z_tiles(fields), Y, X), F32)] * ways["gz"],
            1000,
            start.size * 4,
        )(start, diagonal, sides, *received)
        received = swaps(sends, "gz", count["gz"])
    with jax.named_scope("matrix_powers"):
        split, sums = call(
            functools.partial(powers, fields, count["gz"], ways["gz"]),
            [((2 * BPAD, CELLS * X), BF16), ((HPAD, X), F32)],
            2 * 192 * 64 * CELLS * X,
            start.size * 4,
            [
                pltpu.VMEM((STEPS, fields, SLOTS, 2, Y, X), F32),
                pltpu.VMEM((24 * CELLS, X), F32),
                pltpu.VMEM((STEPS, 2, fields, 2, Y, X), F32),
                pltpu.VMEM((SLOTS, 2, Y, X), F32),
                pltpu.VMEM((SLOTS, 2, Y, X), F32),
            ],
        )(start, diagonal, sides, beyond, beyond_sides, *received, history_split, history_gram)
    with jax.named_scope("sum_over_devices"):
        devices = sizes[0] * sizes[1] * sizes[2]
        bits = []
        for axis, stride in (("gz", 1), ("gx", sizes[1] * sizes[2]), ("gy", sizes[2])):
            bits += [stride << b for b in range(count[axis].bit_length() - 1)]
        first, rest = bits[: 1 + (len(bits) - 1) % 2], bits[1 + (len(bits) - 1) % 2 :]
        for bit in first:
            pair = exchange_sums(sums, sizes, [bit])
            sums = pair[0] + pair[1]
        while rest:
            parts = exchange_sums(sums, sizes, rest[:2])
            rest = rest[2:]
            if rest:
                sums = (parts[0] + parts[1]) + (parts[2] + parts[3])
    with jax.named_scope("orthonormalize"):
        out, factor = call(
            functools.partial(finish, columns, cells),
            [((columns * CELLS, X), F32), ((columns, columns), F32)],
            2 * 192 * 64 * CELLS * X,
            columns * CELLS * X * 4,
        )(history_split, split, *parts)
    return out.reshape(columns, Z, Y, X), factor


def solution(mesh):
    sizes = tuple(mesh.shape[axis] for axis in AXES)
    return jax.shard_map(
        functools.partial(on_device, sizes),
        mesh=mesh,
        in_specs=(P(None, "gz", "gy", "gx"), P(None, "gz", "gy", "gx"), P("gz", "gy", "gx")),
        out_specs=(P(None, "gz", "gy", "gx"), P()),
        check_vma=False,
    )
```

time: 203 us -> 44.2 us (0.22)
  blocking collectives: 88.7 us -> 0 us
  starting transfers between devices: 69.3 us -> 17.7 us
  other arithmetic: 12.1 us -> 0.01 us
  Pallas kernels: 0 us -> 9.02 us
  matrix products: 6.76 us -> 0 us
  waiting for transfers between devices: 19.9 us -> 13.3 us
    psum x2 -> x0, blocking collectives: 88.7 us -> none  [the longest x1 48.3 us: on_device(): coef = lax.psum(local_coef, ('gx', 'gy', 'gz')) / cell_total]
    ppermute x24 -> x12, starting transfers between devices: 69.3 us -> 17.7 us  [the longest x5 9.33 us: swaps(): lax.ppermute(a, axis, pairs)]
    pallas_call x0 -> x6, Pallas kernels: none -> 9.02 us  [the longest x1 4.23 us: on_device(): call(functools.partial(finish, columns, cells), [((columns * CELLS, X), F...]
    ppermute x24 -> x12, waiting for transfers between devices: 19.9 us -> 13.3 us  [the longest x7 7.25 us: exchange_sums(): lax.ppermute(array, AXES, [(i, i ^ flip) for i in range(count)])]
    dot_general x3 -> x0, matrix products: 5.67 us -> none  [the longest x1 2.73 us: on_device(): jnp.dot(flat_hist, flat_basis.T, precision=highest, preferred_element_typ...]
    another operation x4 -> x0, other arithmetic: 4.02 us -> none  [the longest x3 2.49 us: on_device(): lower = jnp.linalg.cholesky(gram)]
    concatenate x5 -> x0, other arithmetic: 2.49 us -> none  [the longest x4 2.05 us: with_halo(): block = jnp.concatenate([low, block, high], axis=dim)]
    div x3 -> x0, other arithmetic: 2.12 us -> none  [the longest x1 2.11 us: scaled_from_padded(): ((6.0 + diag_inner[None]) * center - beside - 7.0 * center) / 7.0]
  transfers between devices with their start and end apart: 24 -> 12, of which waited for: 17 -> 10; matrix products, arithmetic and copies ran while one was open for 0% -> 0% of each run, Pallas kernels for 0% -> 4%
where the time goes in v1:
time: 44.2 us; the launch traced here: 43.9 us
  starting transfers between devices  17.7 us (40%)
  waiting for transfers between devices  13.3 us (30%)
  Pallas kernels  9.02 us (20%)
  local copies, waits for them, and re-layouts  3.16 us (7%)
  between operations  0.71 us (2%)
    ppermute x5, starting transfers between devices, swaps(): lax.ppermute(a, axis, pairs)  9.33 us
    ppermute x7, starting transfers between devices, exchange_sums(): lax.ppermute(array, AXES, [(i, i ^ flip) for i in range(count)])  8.4 us
    ppermute x7, waiting for transfers between devices, exchange_sums(): lax.ppermute(array, AXES, [(i, i ^ flip) for i in range(count)])  7.25 us
    ppermute x5, waiting for transfers between devices, swaps(): lax.ppermute(a, axis, pairs)  6.05 us
    pallas_call x1, Pallas kernels, on_device(): call(functools.partial(finish, columns, cells), [((columns * CELLS, X), F...  4.23 us
    unnamed x10, local copies, waits for them, and re-layouts  3.16 us
    pallas_call x1, Pallas kernels, on_device(): call(functools.partial(powers, fields, count['gz'], ways['gz']), [((2 * B...  2.43 us
    pallas_call x1, Pallas kernels, on_device(): call(functools.partial(history_kernel, history_count), [((2 * HPAD, CELLS...  1.95 us
  transfers between devices with their start and end apart: 12, of which 10 were waited for; matrix products, arithmetic and copies ran while one was open for 0% of the time, Pallas kernels for 4%

profile of v1, /device:TPU:0, one launch (start us, length us, event | category | flops | bytes accessed | tf_op | source)
XLA Modules:
  0.0 43.9 jit_solution(3452468627115497917)
XLA Ops:
  0.6 0.9 %copy-done = f32[4,8,8,128]{3,2,1,0:T(8,128)S(1)} copy-done((f32[4,8,8,128]{3,2,1,0:T(8,128)S(1)}, f32[4,8,8,128]{3,2,1,0:T(8,128)}, u32[]{:S(2)}) %copy-start) | copy-done | bytes 131096
  1.5 0.8 %copy-done.3 = f32[8,8,128]{2,1,0:T(8,128)S(1)} copy-done((f32[8,8,128]{2,1,0:T(8,128)S(1)}, f32[8,8,128]{2,1,0:T(8,128)}, u32[]{:S(2)}) %copy-start.3) | copy-done | bytes 32792
  2.3 0.1 halo_x.1
  2.4 3.0 %collective-permute-start = (f32[5,8,128]{2,1,0:T(8,128)S(1)}, f32[5,8,128]{2,1,0:T(8,128)S(1)}, u32[]{:S(2)}, u32[]{:S(2)}) collective-permute-start(f32[5,8,128]{2,1,0:T(8,128)S(1)} %halo_x.1), channel_id=1, source_target_pairs={{0,16},{16,0},{1,17},{17,1},{2,18},{18,2},{3,19},{19,3},{4,20},{20... | collective-permute-start | bytes 61448 | tf_op jit(solution)/shard_map/halo_x/ppermute | solution.py:58
  5.5 1.8 %collective-permute-done.refs_0_ = f32[5,8,128]{2,1,0:T(8,128)S(1)} collective-permute-done((f32[5,8,128]{2,1,0:T(8,128)S(1)}, f32[5,8,128]{2,1,0:T(8,128)S(1)}, u32[]{:S(2)}, u32[]{:S(2)}) %collective-permute-start) | collective-permute-done | bytes 20512 | tf_op jit(solution)/shard_map/halo_x/ppermute | solution.py:58
  7.2 0.2 halo_y.1
  7.4 2.1 %collective-permute-start.1 = (f32[23,8,128]{2,1,0:T(8,128)S(1)}, f32[23,8,128]{2,1,0:T(8,128)S(1)}, u32[]{:S(2)}, u32[]{:S(2)}) collective-permute-start(f32[23,8,128]{2,1,0:T(8,128)S(1)} %get-tuple-element.17), channel_id=1, source_target_pairs={{0,4},{4,0},{8,12},{12,8},{1,5},{5,1},{9,13},{13,9},{2,6},{6,2},{1... | collective-permute-start | bytes 282632 | tf_op jit(solution)/shard_map/halo_y/ppermute | solution.py:58
  9.6 2.5 %collective-permute-start.2 = (f32[23,8,128]{2,1,0:T(8,128)S(1)}, f32[23,8,128]{2,1,0:T(8,128)S(1)}, u32[]{:S(2)}, u32[]{:S(2)}) collective-permute-start(f32[23,8,128]{2,1,0:T(8,128)S(1)} %get-tuple-element.18), channel_id=1, source_target_pairs={{0,12},{4,8},{8,4},{12,0},{1,13},{5,9},{9,5},{13,1},{2,14},{6,10},... | collective-permute-start | bytes 282632 | tf_op jit(solution)/shard_map/halo_y/ppermute | solution.py:58
  12.0 0.5 %collective-permute-done.1.refs_0_ = f32[23,8,128]{2,1,0:T(8,128)S(1)} collective-permute-done((f32[23,8,128]{2,1,0:T(8,128)S(1)}, f32[23,8,128]{2,1,0:T(8,128)S(1)}, u32[]{:S(2)}, u32[]{:S(2)}) %collective-permute-start.1) | collective-permute-done | bytes 94240 | tf_op jit(solution)/shard_map/halo_y/ppermute | solution.py:58
  12.6 3.4 %collective-permute-done.2.refs_1_ = f32[23,8,128]{2,1,0:T(8,128)S(1)} collective-permute-done((f32[23,8,128]{2,1,0:T(8,128)S(1)}, f32[23,8,128]{2,1,0:T(8,128)S(1)}, u32[]{:S(2)}, u32[]{:S(2)}) %collective-permute-start.2) | collective-permute-done | bytes 94240 | tf_op jit(solution)/shard_map/halo_y/ppermute | solution.py:58
  15.9 0.1 halo_z.1
  16.0 0.1 collective-permute-start.3
  16.1 1.6 %collective-permute-start.4 = (f32[34,8,128]{2,1,0:T(8,128)S(1)}, f32[34,8,128]{2,1,0:T(8,128)S(1)}, u32[]{:S(2)}, u32[]{:S(2)}) collective-permute-start(f32[34,8,128]{2,1,0:T(8,128)S(1)} %get-tuple-element.22), channel_id=1, source_target_pairs={{0,3},{1,2},{2,1},{3,0},{4,7},{5,6},{6,5},{7,4},{8,11},{9,10},{10,... | collective-permute-start | bytes 417800 | tf_op jit(solution)/shard_map/halo_z/ppermute | solution.py:58
  17.7 1.5 %copy-done.2 = f32[56,8,8,128]{3,2,1,0:T(8,128)S(1)} copy-done((f32[56,8,8,128]{3,2,1,0:T(8,128)S(1)}, f32[56,8,8,128]{3,2,1,0:T(8,128)}, u32[]{:S(2)}) %copy-start.2) | copy-done | bytes 1835032
  19.2 2.0 %history_products.1 = (bf16[128,8192]{1,0:T(8,128)(2,1)S(1)}, f32[64,64]{1,0:T(8,128)S(1)}) custom-call(f32[3584,128]{1,0:T(8,128)S(1)} %bitcast.2), custom_call_target="tpu_custom_call" | custom-call | flops 268435456 | bytes 3670016 | tf_op jit(solution)/shard_map/history_products/pallas_call | solution.py:422
  21.2 0.0 collective-permute-done.3.refs_0_
  21.2 0.4 collective-permute-done.4.refs_1_
  21.6 2.4 %matrix_powers.1 = (bf16[64,8192]{1,0:T(8,128)(2,1)S(1)}, f32[64,128]{1,0:T(8,128)S(1)}) custom-call(f32[4,8,8,128]{3,2,1,0:T(8,128)S(1)} %copy-done.1, f32[8,8,128]{2,1,0:T(8,128)S(1)} %copy-done.4, f32[5,8,128]{2,1,0:T(8,128)S(1)} %get-tuple-element.16.sides, f32[5,8,8,128]{3,2,1,0:T(8,128)S(1)} %get-tuple-element.19.beyond, ...), custom_call_target="tpu_custom_call" | custom-call | flops 201326592 | bytes 131072 | tf_op jit(solution)/shard_map/matrix_powers/pallas_call | solution.py:456
  24.0 0.5 %collective-permute-start.5 = (f32[64,128]{1,0:T(8,128)S(1)}, f32[64,128]{1,0:T(8,128)S(1)}, u32[]{:S(2)}, u32[]{:S(2)}) collective-permute-start(f32[64,128]{1,0:T(8,128)S(1)} %get-tuple-element.25), channel_id=1, source_target_pairs={{0,1},{1,0},{2,3},{3,2},{4,5},{5,4},{6,7},{7,6},{8,9},{9,8},{10,11... | collective-permute-start | bytes 98312 | tf_op jit(solution)/shard_map/sum_over_devices/ppermute | solution.py:408
  24.5 0.9 %collective-permute-done.5 = f32[64,128]{1,0:T(8,128)S(1)} collective-permute-done((f32[64,128]{1,0:T(8,128)S(1)}, f32[64,128]{1,0:T(8,128)S(1)}, u32[]{:S(2)}, u32[]{:S(2)}) %collective-permute-start.5) | collective-permute-done | bytes 32800 | tf_op jit(solution)/shard_map/sum_over_devices/ppermute | solution.py:408
  25.3 2.4 %collective-permute-start.8 = (f32[64,128]{1,0:T(8,128)S(1)}, f32[64,128]{1,0:T(8,128)S(1)}, u32[]{:S(2)}, u32[]{:S(2)}) collective-permute-start(f32[64,128]{1,0:T(8,128)S(1)} %add.12), channel_id=1, source_target_pairs={{0,18},{1,19},{2,16},{3,17},{4,22},{5,23},{6,20},{7,21},{8,26},{9,... | collective-permute-start | bytes 98312 | tf_op jit(solution)/shard_map/sum_over_devices/ppermute | solution.py:408
  27.8 0.5 %collective-permute-start.7 = (f32[64,128]{1,0:T(8,128)S(1)}, f32[64,128]{1,0:T(8,128)S(1)}, u32[]{:S(2)}, u32[]{:S(2)}) collective-permute-start(f32[64,128]{1,0:T(8,128)S(1)} %add.12), channel_id=1, source_target_pairs={{0,16},{1,17},{2,18},{3,19},{4,20},{5,21},{6,22},{7,23},{8,24},{9,... | collective-permute-start | bytes 98312 | tf_op jit(solution)/shard_map/sum_over_devices/ppermute | solution.py:408
  28.3 0.5 %collective-permute-start.6 = (f32[64,128]{1,0:T(8,128)S(1)}, f32[64,128]{1,0:T(8,128)S(1)}, u32[]{:S(2)}, u32[]{:S(2)}) collective-permute-start(f32[64,128]{1,0:T(8,128)S(1)} %add.12), channel_id=1, source_target_pairs={{0,2},{1,3},{2,0},{3,1},{4,6},{5,7},{6,4},{7,5},{8,10},{9,11},{10,... | collective-permute-start | bytes 98312 | tf_op jit(solution)/shard_map/sum_over_devices/ppermute | solution.py:408
  28.8 1.3 %collective-permute-done.8 = f32[64,128]{1,0:T(8,128)S(1)} collective-permute-done((f32[64,128]{1,0:T(8,128)S(1)}, f32[64,128]{1,0:T(8,128)S(1)}, u32[]{:S(2)}, u32[]{:S(2)}) %collective-permute-start.8) | collective-permute-done | bytes 32800 | tf_op jit(solution)/shard_map/sum_over_devices/ppermute | solution.py:408
  30.2 1.5 %collective-permute-done.7 = f32[64,128]{1,0:T(8,128)S(1)} collective-permute-done((f32[64,128]{1,0:T(8,128)S(1)}, f32[64,128]{1,0:T(8,128)S(1)}, u32[]{:S(2)}, u32[]{:S(2)}) %collective-permute-start.7) | collective-permute-done | bytes 32800 | tf_op jit(solution)/shard_map/sum_over_devices/ppermute | solution.py:408
  31.7 0.5 %collective-permute-done.6 = f32[64,128]{1,0:T(8,128)S(1)} collective-permute-done((f32[64,128]{1,0:T(8,128)S(1)}, f32[64,128]{1,0:T(8,128)S(1)}, u32[]{:S(2)}, u32[]{:S(2)}) %collective-permute-start.6) | collective-permute-done | bytes 32800 | tf_op jit(solution)/shard_map/sum_over_devices/ppermute | solution.py:408
  32.2 2.6 %collective-permute-start.11 = (f32[64,128]{1,0:T(8,128)S(1)}, f32[64,128]{1,0:T(8,128)S(1)}, u32[]{:S(2)}, u32[]{:S(2)}) collective-permute-start(f32[64,128]{1,0:T(8,128)S(1)} %add_add_fusion.refs_0_), channel_id=1, source_target_pairs={{0,12},{1,13},{2,14},{3,15},{4,8},{5,9},{6,10},{7,11},{8,4},{9,5},... | collective-permute-start | bytes 98312 | tf_op jit(solution)/shard_map/sum_over_devices/ppermute | solution.py:408
  34.9 1.8 %collective-permute-start.9 = (f32[64,128]{1,0:T(8,128)S(1)}, f32[64,128]{1,0:T(8,128)S(1)}, u32[]{:S(2)}, u32[]{:S(2)}) collective-permute-start(f32[64,128]{1,0:T(8,128)S(1)} %add_add_fusion.refs_0_), channel_id=1, source_target_pairs={{0,4},{1,5},{2,6},{3,7},{4,0},{5,1},{6,2},{7,3},{8,12},{9,13},{10,... | collective-permute-start | bytes 98312 | tf_op jit(solution)/shard_map/sum_over_devices/ppermute | solution.py:408
  36.7 1.4 %collective-permute-done.11.refs_3_ = f32[64,128]{1,0:T(8,128)S(1)} collective-permute-done((f32[64,128]{1,0:T(8,128)S(1)}, f32[64,128]{1,0:T(8,128)S(1)}, u32[]{:S(2)}, u32[]{:S(2)}) %collective-permute-start.11) | collective-permute-done | bytes 32800 | tf_op jit(solution)/shard_map/sum_over_devices/ppermute | solution.py:408
  38.1 1.6 %collective-permute-done.10.refs_2_ = f32[64,128]{1,0:T(8,128)S(1)} collective-permute-done((f32[64,128]{1,0:T(8,128)S(1)}, f32[64,128]{1,0:T(8,128)S(1)}, u32[]{:S(2)}, u32[]{:S(2)}) %collective-permute-start.10) | collective-permute-done | bytes 32800 | tf_op jit(solution)/shard_map/sum_over_devices/ppermute | solution.py:408
  39.7 0.0 collective-permute-done.9.refs_1_
  39.7 4.2 %orthonormalize.1 = (f32[1280,128]{1,0:T(8,128)}, f32[20,20]{1,0:T(8,128)}) custom-call(bf16[128,8192]{1,0:T(8,128)(2,1)S(1)} %get-tuple-element.15.refs_2_.history_split, bf16[64,8192]{1,0:T(8,128)(2,1)S(1)} %get-tuple-element.24.split, f32[64,128]{1,0:T(8,128)S(1)} %add_add_fusion.refs_0_, f32[64,128]{1,0:T(8,128)S(1)} %collective-permute-done.9.refs_1_, ...), custom_call_target="tpu_custom_call" | custom-call | flops 201326592 | bytes 655360 | tf_op jit(solution)/shard_map/orthonormalize/pallas_call | solution.py:484
  (10 shorter events, 0.0 us)
Async XLA Ops:
  0.6 0.9 %copy-start = (f32[4,8,8,128]{3,2,1,0:T(8,128)S(1)}, f32[4,8,8,128]{3,2,1,0:T(8,128)}, u32[]{:S(2)}) copy-start(f32[4,8,8,128]{3,2,1,0:T(8,128)} %start.7) | copy-start | bytes 393220
  1.5 0.8 %copy-start.3 = (f32[8,8,128]{2,1,0:T(8,128)S(1)}, f32[8,8,128]{2,1,0:T(8,128)}, u32[]{:S(2)}) copy-start(f32[8,8,128]{2,1,0:T(8,128)} %diagonal.7) | copy-start | bytes 98308
  2.3 19.3 %copy-start.1 = (f32[4,8,8,128]{3,2,1,0:T(8,128)S(1)}, f32[4,8,8,128]{3,2,1,0:T(8,128)}, u32[]{:S(2)}) copy-start(f32[4,8,8,128]{3,2,1,0:T(8,128)} %start.7) | copy-start | bytes 393220
  2.3 19.3 %copy-start.4 = (f32[8,8,128]{2,1,0:T(8,128)S(1)}, f32[8,8,128]{2,1,0:T(8,128)}, u32[]{:S(2)}) copy-start(f32[8,8,128]{2,1,0:T(8,128)} %diagonal.7) | copy-start | bytes 98308
  2.4 4.8 %collective-permute-start = (f32[5,8,128]{2,1,0:T(8,128)S(1)}, f32[5,8,128]{2,1,0:T(8,128)S(1)}, u32[]{:S(2)}, u32[]{:S(2)}) collective-permute-start(f32[5,8,128]{2,1,0:T(8,128)S(1)} %halo_x.1), channel_id=1, source_target_pairs={{0,16},{16,0},{1,17},{17,1},{2,18},{18,2},{3,19},{19,3},{4,20},{20... | collective-permute-start | bytes 61448 | tf_op jit(solution)/shard_map/halo_x/ppermute | solution.py:58
  7.4 5.2 %collective-permute-start.1 = (f32[23,8,128]{2,1,0:T(8,128)S(1)}, f32[23,8,128]{2,1,0:T(8,128)S(1)}, u32[]{:S(2)}, u32[]{:S(2)}) collective-permute-start(f32[23,8,128]{2,1,0:T(8,128)S(1)} %get-tuple-element.17), channel_id=1, source_target_pairs={{0,4},{4,0},{8,12},{12,8},{1,5},{5,1},{9,13},{13,9},{2,6},{6,2},{1... | collective-permute-start | bytes 282632 | tf_op jit(solution)/shard_map/halo_y/ppermute | solution.py:58
  9.6 6.4 %collective-permute-start.2 = (f32[23,8,128]{2,1,0:T(8,128)S(1)}, f32[23,8,128]{2,1,0:T(8,128)S(1)}, u32[]{:S(2)}, u32[]{:S(2)}) collective-permute-start(f32[23,8,128]{2,1,0:T(8,128)S(1)} %get-tuple-element.18), channel_id=1, source_target_pairs={{0,12},{4,8},{8,4},{12,0},{1,13},{5,9},{9,5},{13,1},{2,14},{6,10},... | collective-permute-start | bytes 282632 | tf_op jit(solution)/shard_map/halo_y/ppermute | solution.py:58
  16.0 5.2 %collective-permute-start.3 = (f32[34,8,128]{2,1,0:T(8,128)S(1)}, f32[34,8,128]{2,1,0:T(8,128)S(1)}, u32[]{:S(2)}, u32[]{:S(2)}) collective-permute-start(f32[34,8,128]{2,1,0:T(8,128)S(1)} %get-tuple-element.21), channel_id=1, source_target_pairs={{0,1},{1,0},{2,3},{3,2},{4,5},{5,4},{6,7},{7,6},{8,9},{9,8},{10,11... | collective-permute-start | bytes 417800 | tf_op jit(solution)/shard_map/halo_z/ppermute | solution.py:58
  16.1 5.5 %collective-permute-start.4 = (f32[34,8,128]{2,1,0:T(8,128)S(1)}, f32[34,8,128]{2,1,0:T(8,128)S(1)}, u32[]{:S(2)}, u32[]{:S(2)}) collective-permute-start(f32[34,8,128]{2,1,0:T(8,128)S(1)} %get-tuple-element.22), channel_id=1, source_target_pairs={{0,3},{1,2},{2,1},{3,0},{4,7},{5,6},{6,5},{7,4},{8,11},{9,10},{10,... | collective-permute-start | bytes 417800 | tf_op jit(solution)/shard_map/halo_z/ppermute | solution.py:58
  17.7 1.5 %copy-start.2 = (f32[56,8,8,128]{3,2,1,0:T(8,128)S(1)}, f32[56,8,8,128]{3,2,1,0:T(8,128)}, u32[]{:S(2)}) copy-start(f32[56,8,8,128]{3,2,1,0:T(8,128)} %param.3) | copy-start | bytes 5505028
  24.0 1.3 %collective-permute-start.5 = (f32[64,128]{1,0:T(8,128)S(1)}, f32[64,128]{1,0:T(8,128)S(1)}, u32[]{:S(2)}, u32[]{:S(2)}) collective-permute-start(f32[64,128]{1,0:T(8,128)S(1)} %get-tuple-element.25), channel_id=1, source_target_pairs={{0,1},{1,0},{2,3},{3,2},{4,5},{5,4},{6,7},{7,6},{8,9},{9,8},{10,11... | collective-permute-start | bytes 98312 | tf_op jit(solution)/shard_map/sum_over_devices/ppermute | solution.py:408
  25.3 4.8 %collective-permute-start.8 = (f32[64,128]{1,0:T(8,128)S(1)}, f32[64,128]{1,0:T(8,128)S(1)}, u32[]{:S(2)}, u32[]{:S(2)}) collective-permute-start(f32[64,128]{1,0:T(8,128)S(1)} %add.12), channel_id=1, source_target_pairs={{0,18},{1,19},{2,16},{3,17},{4,22},{5,23},{6,20},{7,21},{8,26},{9,... | collective-permute-start | bytes 98312 | tf_op jit(solution)/shard_map/sum_over_devices/ppermute | solution.py:408
  27.8 3.9 %collective-permute-start.7 = (f32[64,128]{1,0:T(8,128)S(1)}, f32[64,128]{1,0:T(8,128)S(1)}, u32[]{:S(2)}, u32[]{:S(2)}) collective-permute-start(f32[64,128]{1,0:T(8,128)S(1)} %add.12), channel_id=1, source_target_pairs={{0,16},{1,17},{2,18},{3,19},{4,20},{5,21},{6,22},{7,23},{8,24},{9,... | collective-permute-start | bytes 98312 | tf_op jit(solution)/shard_map/sum_over_devices/ppermute | solution.py:408
  28.3 3.9 %collective-permute-start.6 = (f32[64,128]{1,0:T(8,128)S(1)}, f32[64,128]{1,0:T(8,128)S(1)}, u32[]{:S(2)}, u32[]{:S(2)}) collective-permute-start(f32[64,128]{1,0:T(8,128)S(1)} %add.12), channel_id=1, source_target_pairs={{0,2},{1,3},{2,0},{3,1},{4,6},{5,7},{6,4},{7,5},{8,10},{9,11},{10,... | collective-permute-start | bytes 98312 | tf_op jit(solution)/shard_map/sum_over_devices/ppermute | solution.py:408
  32.2 5.9 %collective-permute-start.11 = (f32[64,128]{1,0:T(8,128)S(1)}, f32[64,128]{1,0:T(8,128)S(1)}, u32[]{:S(2)}, u32[]{:S(2)}) collective-permute-start(f32[64,128]{1,0:T(8,128)S(1)} %add_add_fusion.refs_0_), channel_id=1, source_target_pairs={{0,12},{1,13},{2,14},{3,15},{4,8},{5,9},{6,10},{7,11},{8,4},{9,5},... | collective-permute-start | bytes 98312 | tf_op jit(solution)/shard_map/sum_over_devices/ppermute | solution.py:408
  34.9 4.8 %collective-permute-start.10 = (f32[64,128]{1,0:T(8,128)S(1)}, f32[64,128]{1,0:T(8,128)S(1)}, u32[]{:S(2)}, u32[]{:S(2)}) collective-permute-start(f32[64,128]{1,0:T(8,128)S(1)} %add_add_fusion.refs_0_), channel_id=1, source_target_pairs={{0,8},{1,9},{2,10},{3,11},{4,12},{5,13},{6,14},{7,15},{8,0},{9,1},... | collective-permute-start | bytes 98312 | tf_op jit(solution)/shard_map/sum_over_devices/ppermute | solution.py:408
  34.9 4.8 %collective-permute-start.9 = (f32[64,128]{1,0:T(8,128)S(1)}, f32[64,128]{1,0:T(8,128)S(1)}, u32[]{:S(2)}, u32[]{:S(2)}) collective-permute-start(f32[64,128]{1,0:T(8,128)S(1)} %add_add_fusion.refs_0_), channel_id=1, source_target_pairs={{0,4},{1,5},{2,6},{3,7},{4,0},{5,1},{6,2},{7,3},{8,12},{9,13},{10,... | collective-permute-start | bytes 98312 | tf_op jit(solution)/shard_map/sum_over_devices/ppermute | solution.py:408

commit v2 on v1

--- a/solution.py
+++ b/solution.py
@@ -14,9 +14,12 @@
 HIGHEST = lax.Precision.HIGHEST
 Z, Y, X = 8, 8, 128
 CELLS = Z * Y
+HALF = CELLS // 2
 SLOTS = 16
 BPAD = 32
+BROWS = 24
 HPAD = 64
+ROWS = 56
 
 
 def roll(tile, shift, axis):
@@ -52,13 +55,24 @@
     return pick
 
 
-def swaps(arrays, axis, count):
+def swaps(arrays, axis, count, around=True):
     first = [(i, i ^ 1) for i in range(count)]
     second = [(i, (i + 1 if i % 2 else i - 1) % count) for i in range(count)]
+    if not around:
+        second = second[1:-1]
     return [lax.ppermute(a, axis, pairs) for a, pairs in zip(arrays, (first, second))]
 
 
-def pack_x(fields, start, diagonal, *sends):
+def pack_x(fields, start_there, diagonal_there, start, diagonal, *refs):
+    sends, done = refs[:-1], refs[-1]
+    copies = [
+        pltpu.make_async_copy(start_there, start, done.at[0]),
+        pltpu.make_async_copy(diagonal_there, diagonal, done.at[1]),
+    ]
+    for copy in copies:
+        copy.start()
+    for copy in copies:
+        copy.wait()
     _, lane = iotas()
     even = is_even("gx")
     for f in range(fields + 1):
@@ -78,7 +92,7 @@
             sends[1][f] = jnp.where(even, to_low, to_high)
 
 
-def pack_y(fields, count, ways, start, diagonal, *refs):
+def pack_y(fields, count, ways, start, diagonal, _, *refs):
     received, (sides, *sends) = refs[:ways], refs[ways:]
     row, lane = iotas()
     column = lane & 7
@@ -116,7 +130,7 @@
         send(4 * (fields + 1) + f // 2, sides[f], sides[min(f + 1, fields)])
 
 
-def pack_z(fields, count, ways, start, diagonal, sides, *refs):
+def pack_z(fields, count, ways, start, diagonal, _, sides, *refs):
     received, (beyond, beyond_sides, *sends) = refs[:ways], refs[ways:]
     row, lane = iotas()
     pick = facing("gy", count, received)
@@ -172,8 +186,12 @@
 
 def powers(fields, count, ways, start, diagonal, sides, beyond, beyond_sides, *refs):
     received = refs[:ways]
-    history_split, history_gram, split, sums = refs[ways : ways + 4]
-    halo, center, ends, coef_a, coef_b = refs[ways + 4 :]
+    history_splits, history_grams, (split, sums) = (
+        refs[ways : ways + 2],
+        refs[ways + 2 : ways + 4],
+        refs[ways + 4 : ways + 6],
+    )
+    halo, center, ends, coef_a, coef_b = refs[ways + 6 :]
     columns = fields * (STEPS + 1)
     row, lane = iotas()
     pick = facing("gz", count, received)
@@ -295,21 +313,22 @@
                             value = value + value - ends[level - 2, side, f, part]
                         ends[level, side, f, part] = value
 
-    center[pl.ds(columns * CELLS, (24 - columns) * CELLS), :] = jnp.zeros(
-        ((24 - columns) * CELLS, X), F32
+    center[pl.ds(columns * CELLS, (BROWS - columns) * CELLS), :] = jnp.zeros(
+        ((BROWS - columns) * CELLS, X), F32
     )
     for cell in range(CELLS):
-        high, low = split_rows(center[pl.ds(cell, 24, stride=CELLS), :], BPAD)
+        high, low = split_rows(center[pl.ds(cell, BROWS, stride=CELLS), :], BPAD)
         split[0:BPAD, cell * X : (cell + 1) * X] = high
         split[BPAD : 2 * BPAD, cell * X : (cell + 1) * X] = low
-    basis = product(split[...], split[...])
-    cross = product(history_split[...], split[...])
-    basis = join(join(basis, BPAD).T, BPAD)
-    cross = join(join(cross, HPAD).T, BPAD).T
-    sums[:, 0:HPAD] = history_gram[...]
-    sums[:, HPAD : HPAD + BPAD] = cross
-    sums[0:BPAD, HPAD + BPAD :] = basis
-    sums[BPAD:, HPAD + BPAD :] = jnp.zeros((HPAD - BPAD, BPAD), F32)
+    basis = join_lanes(join(product(split[...], split[...]), BPAD), BPAD)
+    cross = product(split[:, : HALF * X], history_splits[0][...])
+    cross = cross + product(split[:, HALF * X :], history_splits[1][...])
+    cross = join_lanes(join(cross, BPAD), HPAD)
+    sums[:, 0:HPAD] = (history_grams[0][...] + history_grams[1][...])[:ROWS]
+    sums[0:BROWS, HPAD:] = cross[:BROWS]
+    sums[BROWS : 2 * BROWS, HPAD : HPAD + BPAD] = basis[:BROWS]
+    sums[BROWS : 2 * BROWS, HPAD + BPAD :] = jnp.zeros((BROWS, X - HPAD - BPAD), F32)
+    sums[2 * BROWS :, HPAD:] = jnp.zeros((ROWS - 2 * BROWS, X - HPAD), F32)
 
 
 def split_rows(rows, padded):
@@ -326,12 +345,16 @@
     return both[:padded] + both[padded:]
 
 
-def history_kernel(count, history, split, gram):
-    for cell in range(CELLS):
-        high, low = split_rows(history[pl.ds(cell, count, stride=CELLS), :], HPAD)
+def join_lanes(both, padded):
+    return both[:, :padded] + both[:, padded:]
+
+
+def history_kernel(count, first, history, split, gram):
+    for cell in range(HALF):
+        high, low = split_rows(history[pl.ds(first + cell, count, stride=CELLS), :], HPAD)
         split[0:HPAD, cell * X : (cell + 1) * X] = high
         split[HPAD : 2 * HPAD, cell * X : (cell + 1) * X] = low
-    gram[...] = join(join(product(split[...], split[...]), HPAD).T, HPAD)
+    gram[...] = join_lanes(join(product(split[...], split[...]), HPAD), HPAD)
 
 
 def split_matrix(matrix):
@@ -339,37 +362,47 @@
     return high, (matrix - high.astype(F32)).astype(BF16)
 
 
-def finish(columns, cells, history_split, split, *refs):
+def reciprocal(value):
+    guess = pl.reciprocal(value, approx=True)
+    guess = guess * (2.0 - value * guess)
+    return guess * (2.0 - value * guess)
+
+
+def finish(columns, cells, first_half, second_half, split, *refs):
     parts, (out, factor) = refs[:-2], refs[-2:]
     total = (parts[0][...] + parts[1][...]) + (parts[2][...] + parts[3][...])
     total = total * (1.0 / cells)
-    history_gram = total[:, 0:HPAD]
-    coef = total[:, HPAD : HPAD + BPAD]
-    basis_gram = total[0:BPAD, HPAD + BPAD :]
-    inner = jnp.dot(history_gram, coef, precision=HIGHEST, preferred_element_type=F32)
+    history_gram = jnp.concatenate([total[:, 0:HPAD], jnp.zeros((HPAD - ROWS, HPAD), F32)], axis=0)
+    coef = total[0:BROWS, HPAD:]
+    basis_gram = total[BROWS : 2 * BROWS, HPAD : HPAD + BPAD]
+    inner = jnp.dot(coef, history_gram, precision=HIGHEST, preferred_element_type=F32) - 2.0 * coef
+    inner = jnp.concatenate([inner, jnp.zeros((BPAD - BROWS, HPAD), F32)], axis=0)
     gram = basis_gram + lax.dot_general(
-        coef, inner - 2.0 * coef, (((0,), (0,)), ((), ())), precision=HIGHEST, preferred_element_type=F32
-    )
-    row = lax.broadcasted_iota(jnp.int32, (BPAD, X), 0)
-    lane = lax.broadcasted_iota(jnp.int32, (BPAD, X), 1)
-    work = jnp.concatenate(
-        [gram, jnp.zeros((BPAD, X - BPAD), F32)], axis=1
-    )
+        coef, inner, (((1,), (1,)), ((), ())), precision=HIGHEST, preferred_element_type=F32
+    )
+    row = lax.broadcasted_iota(jnp.int32, (BROWS, X), 0)
+    lane = lax.broadcasted_iota(jnp.int32, (BROWS, X), 1)
+    work = jnp.concatenate([gram, jnp.zeros((BROWS, X - BPAD - HPAD), F32), coef], axis=1)
     work = jnp.where(lane == row + BPAD, 1.0, work)
-    for k in range(columns):
-        pivot_row = work[k : k + 1, :]
-        scale = work[:, k : k + 1] / pivot_row[:, k : k + 1]
-        work = work - jnp.where(row > k, scale, 0.0) * pivot_row
+    panel = columns
+    for start in range(0, columns, panel):
+        spread = [
+            jnp.broadcast_to(work[:, k : k + 1], (BROWS, X)) for k in range(start, start + panel)
+        ]
+        for j in range(panel):
+            k = start + j
+            scale = spread[j] * reciprocal(spread[j][k : k + 1, :])
+            scale = jnp.where(row > k, scale, 0.0)
+            for later in range(j + 1, panel):
+                spread[later] = spread[later] - scale * spread[later][k : k + 1, :]
+            work = work - scale * work[k : k + 1, :]
     pivots = jnp.sum(jnp.where(lane == row, work, 0.0), axis=1, keepdims=True)
-    good = lax.broadcasted_iota(jnp.int32, (BPAD, 1), 0) < columns
+    good = lax.broadcasted_iota(jnp.int32, (BROWS, 1), 0) < columns
     work = work * jnp.where(good, 1.0 / jnp.sqrt(jnp.where(good, pivots, 1.0)), 0.0)
     factor[...] = jnp.where(lane >= row, work, 0.0)[0:columns, 0:columns]
-    inverse = work[:, BPAD : 2 * BPAD]
-    onto_history = -lax.dot_general(
-        inverse, coef, (((1,), (1,)), ((), ())), precision=HIGHEST, preferred_element_type=F32
-    )
-    history_high, history_low = split_matrix(onto_history)
-    basis_high, basis_low = split_matrix(inverse)
+    work = jnp.concatenate([work, jnp.zeros((BPAD - BROWS, X), F32)], axis=0)
+    history_high, history_low = split_matrix(-work[:, X - HPAD :])
+    basis_high, basis_low = split_matrix(work[:, BPAD : 2 * BPAD])
     left = jnp.concatenate(
         [
             jnp.concatenate([history_high, history_high, basis_high, basis_high], axis=1),
@@ -381,8 +414,14 @@
     )
     width = 4 * X
     for c in range(CELLS * X // width):
-        at = slice(c * width, (c + 1) * width)
-        right = jnp.concatenate([history_split[:, at], split[:, at]], axis=0)
+        half, base = (first_half, 0) if c * width < HALF * X else (second_half, HALF * X)
+        right = jnp.concatenate(
+            [
+                half[:, c * width - base : (c + 1) * width - base],
+                split[:, c * width : (c + 1) * width],
+            ],
+            axis=0,
+        )
         result = join(jnp.dot(left, right, preferred_element_type=F32), BPAD)
         for j in range(width // X):
             out[pl.ds(c * (width // X) + j, columns, stride=CELLS), :] = result[
@@ -390,9 +429,10 @@
             ]
 
 
-def call(kernel, outs, flops, bytes_accessed, scratch=()):
+def call(kernel, outs, flops, bytes_accessed, scratch=(), **specs):
     return pl.pallas_call(
         kernel,
+        **specs,
         out_shape=[jax.ShapeDtypeStruct(shape, dtype) for shape, dtype in outs],
         scratch_shapes=list(scratch),
         compiler_params=pltpu.CompilerParams(vmem_limit_bytes=40 * 1024 * 1024),
@@ -418,22 +458,27 @@
     cells = Z * Y * X * sizes[0] * sizes[1] * sizes[2]
     tile = Y * X * 4
 
-    with jax.named_scope("history_products"):
-        history_split, history_gram = call(
-            functools.partial(history_kernel, history_count),
-            [((2 * HPAD, CELLS * X), BF16), ((HPAD, HPAD), F32)],
-            2 * 128 * 128 * CELLS * X,
-            history.size * 4 * 2,
-        )(history.reshape(history_count * CELLS, X))
+    def history_products(half):
+        with jax.named_scope("history_products"):
+            return call(
+                functools.partial(history_kernel, history_count, half * HALF),
+                [((2 * HPAD, HALF * X), BF16), ((HPAD, HPAD), F32)],
+                128 * 128 * CELLS * X,
+                history.size * 2,
+            )(history.reshape(history_count * CELLS, X))
 
     with jax.named_scope("halo_x"):
-        sends = call(
+        there = pl.BlockSpec(memory_space=pltpu.HBM)
+        start, diagonal, *sends = call(
             functools.partial(pack_x, fields),
-            [((all_fields, Y, X), F32)] * ways["gx"],
+            [(start.shape, F32), (diagonal.shape, F32)] + [((all_fields, Y, X), F32)] * ways["gx"],
             1000,
             start.size * 4,
+            [pltpu.SemaphoreType.DMA((2,))],
+            in_specs=[there, there],
         )(start, diagonal)
         received = swaps(sends, "gx", count["gx"])
+    first_split, first_gram = history_products(0)
     with jax.named_scope("halo_y"):
         y_tiles = 4 * all_fields + (all_fields + 1) // 2
         sides, *sends = call(
@@ -441,8 +486,9 @@
             [((all_fields, Y, X), F32)] + [((y_tiles, Y, X), F32)] * ways["gy"],
             1000,
             start.size * 4,
-        )(start, diagonal, *received)
-        received = swaps(sends, "gy", count["gy"])
+        )(start, diagonal, first_gram, *received)
+        received = swaps(sends, "gy", count["gy"], False)
+    second_split, second_gram = history_products(1)
     with jax.named_scope("halo_z"):
         beyond, beyond_sides, *sends = call(
             functools.partial(pack_z, fields, count["gy"], ways["gy"]),
@@ -450,22 +496,33 @@
             + [((z_tiles(fields), Y, X), F32)] * ways["gz"],
             1000,
             start.size * 4,
-        )(start, diagonal, sides, *received)
+        )(start, diagonal, second_gram, sides, *received)
         received = swaps(sends, "gz", count["gz"])
     with jax.named_scope("matrix_powers"):
         split, sums = call(
             functools.partial(powers, fields, count["gz"], ways["gz"]),
-            [((2 * BPAD, CELLS * X), BF16), ((HPAD, X), F32)],
+            [((2 * BPAD, CELLS * X), BF16), ((ROWS, X), F32)],
             2 * 192 * 64 * CELLS * X,
             start.size * 4,
             [
                 pltpu.VMEM((STEPS, fields, SLOTS, 2, Y, X), F32),
-                pltpu.VMEM((24 * CELLS, X), F32),
+                pltpu.VMEM((BROWS * CELLS, X), F32),
                 pltpu.VMEM((STEPS, 2, fields, 2, Y, X), F32),
                 pltpu.VMEM((SLOTS, 2, Y, X), F32),
                 pltpu.VMEM((SLOTS, 2, Y, X), F32),
             ],
-        )(start, diagonal, sides, beyond, beyond_sides, *received, history_split, history_gram)
+        )(
+            start,
+            diagonal,
+            sides,
+            beyond,
+            beyond_sides,
+            *received,
+            first_split,
+            second_split,
+            first_gram,
+            second_gram,
+        )
     with jax.named_scope("sum_over_devices"):
         devices = sizes[0] * sizes[1] * sizes[2]
         bits = []
@@ -486,7 +543,7 @@
             [((columns * CELLS, X), F32), ((columns, columns), F32)],
             2 * 192 * 64 * CELLS * X,
             columns * CELLS * X * 4,
-        )(history_split, split, *parts)
+        )(first_split, second_split, split, *parts)
     return out.reshape(columns, Z, Y, X), factor
 
 

time: 44.2 us -> 42.4 us (0.959)
  Pallas kernels: 9.02 us -> 8.02 us
  waiting for transfers between devices: 13.3 us -> 12.7 us
    ppermute x5, starting transfers between devices: 9.33 us -> 7 us  [swaps(): lax.ppermute(a, axis, pairs)]
    ppermute x7, starting transfers between devices: 8.4 us -> 10.6 us  [exchange_sums(): lax.ppermute(array, AXES, [(i, i ^ flip) for i in range(count)])]
    pallas_call x1, Pallas kernels: 4.23 us -> 2.81 us  [on_device(): call(functools.partial(finish, columns, cells), [((columns * CELLS, X), F...]
    ppermute x5, waiting for transfers between devices: 6.05 us -> 5.1 us  [swaps(): lax.ppermute(a, axis, pairs)]
    pallas_call x2 -> x3, Pallas kernels: 2.1 us -> 2.51 us  [the longest x2 2.17 us: history_products(): call(functools.partial(history_kernel, history_count, half * HALF), [((2...]
    unnamed x10 -> x8, local copies, waits for them, and re-layouts: 3.16 us -> 3.16 us
  transfers between devices with their start and end apart: 12 -> 12, of which waited for: 10 -> 8; matrix products, arithmetic and copies ran while one was open for 0% -> 0% of each run, Pallas kernels for 4% -> 5%
where the time goes in v2:
time: 42.4 us; the launch traced here: 42.2 us
  starting transfers between devices  17.6 us (42%)
  waiting for transfers between devices  12.7 us (30%)
  Pallas kernels  8.02 us (19%)
  local copies, waits for them, and re-layouts  3.16 us (7%)
  between operations  0.72 us (2%)
    ppermute x7, starting transfers between devices, exchange_sums(): lax.ppermute(array, AXES, [(i, i ^ flip) for i in range(count)])  10.6 us
    ppermute x7, waiting for transfers between devices, exchange_sums(): lax.ppermute(array, AXES, [(i, i ^ flip) for i in range(count)])  7.58 us
    ppermute x5, starting transfers between devices, swaps(): lax.ppermute(a, axis, pairs)  7 us
    ppermute x5, waiting for transfers between devices, swaps(): lax.ppermute(a, axis, pairs)  5.1 us
    unnamed x8, local copies, waits for them, and re-layouts  3.16 us
    pallas_call x1, Pallas kernels, on_device(): call(functools.partial(finish, columns, cells), [((columns * CELLS, X), F...  2.81 us
    pallas_call x1, Pallas kernels, on_device(): call(functools.partial(powers, fields, count['gz'], ways['gz']), [((2 * B...  2.44 us
    pallas_call x2, Pallas kernels, history_products(): call(functools.partial(history_kernel, history_count, half * HALF), [((2...  2.17 us
  transfers between devices with their start and end apart: 12, of which 8 were waited for; matrix products, arithmetic and copies ran while one was open for 0% of the time, Pallas kernels for 5%

profile of v2, /device:TPU:0, one launch (start us, length us, event | category | flops | bytes accessed | tf_op | source)
XLA Modules:
  0.0 42.2 jit_solution(17387789653620634760)
XLA Ops:
  0.6 0.9 %copy-done.2 = f32[4,8,8,128]{3,2,1,0:T(8,128)S(1)} copy-done((f32[4,8,8,128]{3,2,1,0:T(8,128)S(1)}, f32[4,8,8,128]{3,2,1,0:T(8,128)}, u32[]{:S(2)}) %copy-start.2) | copy-done | bytes 131096
  1.5 0.8 %copy-done.3 = f32[8,8,128]{2,1,0:T(8,128)S(1)} copy-done((f32[8,8,128]{2,1,0:T(8,128)S(1)}, f32[8,8,128]{2,1,0:T(8,128)}, u32[]{:S(2)}) %copy-start.3) | copy-done | bytes 32792
  2.3 0.3 halo_x.1
  2.7 3.0 %collective-permute-start = (f32[5,8,128]{2,1,0:T(8,128)S(1)}, f32[5,8,128]{2,1,0:T(8,128)S(1)}, u32[]{:S(2)}, u32[]{:S(2)}) collective-permute-start(f32[5,8,128]{2,1,0:T(8,128)S(1)} %get-tuple-element.25), channel_id=1, source_target_pairs={{0,16},{16,0},{1,17},{17,1},{2,18},{18,2},{3,19},{19,3},{4,20},{20... | collective-permute-start | bytes 61448 | tf_op jit(solution)/shard_map/halo_x/ppermute | solution.py:63
  5.7 1.5 %copy-done = f32[56,8,8,128]{3,2,1,0:T(8,128)S(1)} copy-done((f32[56,8,8,128]{3,2,1,0:T(8,128)S(1)}, f32[56,8,8,128]{3,2,1,0:T(8,128)}, u32[]{:S(2)}) %copy-start) | copy-done | bytes 1835032
  7.2 1.1 %history_products.2 = (bf16[128,4096]{1,0:T(8,128)(2,1)S(1)}, f32[64,64]{1,0:T(8,128)S(1)}) custom-call(f32[3584,128]{1,0:T(8,128)S(1)} %bitcast.2), custom_call_target="tpu_custom_call" | custom-call | flops 134217728 | bytes 917504 | tf_op jit(solution)/shard_map/history_products/pallas_call | solution.py:463
  8.3 0.0 collective-permute-done.refs_0_
  8.3 0.2 halo_y.1
  8.5 1.6 %collective-permute-start.1 = (f32[23,8,128]{2,1,0:T(8,128)S(1)}, f32[23,8,128]{2,1,0:T(8,128)S(1)}, u32[]{:S(2)}, u32[]{:S(2)}) collective-permute-start(f32[23,8,128]{2,1,0:T(8,128)S(1)} %get-tuple-element.28), channel_id=1, source_target_pairs={{0,4},{4,0},{8,12},{12,8},{1,5},{5,1},{9,13},{13,9},{2,6},{6,2},{1... | collective-permute-start | bytes 282632 | tf_op jit(solution)/shard_map/halo_y/ppermute | solution.py:63
  10.1 0.7 %collective-permute-start.2 = (f32[23,8,128]{2,1,0:T(8,128)S(1)}, f32[23,8,128]{2,1,0:T(8,128)S(1)}, u32[]{:S(2)}, u32[]{:S(2)}) collective-permute-start(f32[23,8,128]{2,1,0:T(8,128)S(1)} %get-tuple-element.29), channel_id=1, source_target_pairs={{4,8},{8,4},{5,9},{9,5},{6,10},{10,6},{7,11},{11,7},{20,24},{24,20... | collective-permute-start | bytes 282632 | tf_op jit(solution)/shard_map/halo_y/ppermute | solution.py:63
  10.8 1.1 %history_products.3 = (bf16[128,4096]{1,0:T(8,128)(2,1)S(1)}, f32[64,64]{1,0:T(8,128)S(1)}) custom-call(f32[3584,128]{1,0:T(8,128)S(1)} %bitcast.3), custom_call_target="tpu_custom_call" | custom-call | flops 134217728 | bytes 917504 | tf_op jit(solution)/shard_map/history_products/pallas_call | solution.py:463
  11.9 1.2 %collective-permute-done.1.refs_0_ = f32[23,8,128]{2,1,0:T(8,128)S(1)} collective-permute-done((f32[23,8,128]{2,1,0:T(8,128)S(1)}, f32[23,8,128]{2,1,0:T(8,128)S(1)}, u32[]{:S(2)}, u32[]{:S(2)}) %collective-permute-start.1) | collective-permute-done | bytes 94240 | tf_op jit(solution)/shard_map/halo_y/ppermute | solution.py:63
  13.1 0.0 collective-permute-done.2.refs_1_
  13.1 0.1 halo_z.1
  13.2 0.1 collective-permute-start.3
  13.3 1.6 %collective-permute-start.4 = (f32[34,8,128]{2,1,0:T(8,128)S(1)}, f32[34,8,128]{2,1,0:T(8,128)S(1)}, u32[]{:S(2)}, u32[]{:S(2)}) collective-permute-start(f32[34,8,128]{2,1,0:T(8,128)S(1)} %get-tuple-element.33), channel_id=1, source_target_pairs={{0,3},{1,2},{2,1},{3,0},{4,7},{5,6},{6,5},{7,4},{8,11},{9,10},{10,... | collective-permute-start | bytes 417800 | tf_op jit(solution)/shard_map/halo_z/ppermute | solution.py:63
  14.9 3.9 %collective-permute-done.4.refs_1_ = f32[34,8,128]{2,1,0:T(8,128)S(1)} collective-permute-done((f32[34,8,128]{2,1,0:T(8,128)S(1)}, f32[34,8,128]{2,1,0:T(8,128)S(1)}, u32[]{:S(2)}, u32[]{:S(2)}) %collective-permute-start.4) | collective-permute-done | bytes 139296 | tf_op jit(solution)/shard_map/halo_z/ppermute | solution.py:63
  18.7 2.4 %matrix_powers.1 = (bf16[64,8192]{1,0:T(8,128)(2,1)S(1)}, f32[56,128]{1,0:T(8,128)S(1)}) custom-call(f32[4,8,8,128]{3,2,1,0:T(8,128)S(1)} %get-tuple-element.22.start, f32[8,8,128]{2,1,0:T(8,128)S(1)} %get-tuple-element.23.diagonal, f32[5,8,128]{2,1,0:T(8,128)S(1)} %get-tuple-element.26.sides, f32[5,8,8,128]{3,2,1,0:T(8,128)S(1)} %get-tuple-element.30.beyond, ...), custom_call_target="tpu_custom_call" | custom-call | flops 201326592 | bytes 131072 | tf_op jit(solution)/shard_map/matrix_powers/pallas_call | solution.py:502
  21.2 0.4 collective-permute-start.5
  21.6 0.9 %collective-permute-done.5 = f32[56,128]{1,0:T(8,128)S(1)} collective-permute-done((f32[56,128]{1,0:T(8,128)S(1)}, f32[56,128]{1,0:T(8,128)S(1)}, u32[]{:S(2)}, u32[]{:S(2)}) %collective-permute-start.5) | collective-permute-done | bytes 28704 | tf_op jit(solution)/shard_map/sum_over_devices/ppermute | solution.py:448
  22.5 2.1 %collective-permute-start.8 = (f32[56,128]{1,0:T(8,128)S(1)}, f32[56,128]{1,0:T(8,128)S(1)}, u32[]{:S(2)}, u32[]{:S(2)}) collective-permute-start(f32[56,128]{1,0:T(8,128)S(1)} %add.12), channel_id=1, source_target_pairs={{0,18},{1,19},{2,16},{3,17},{4,22},{5,23},{6,20},{7,21},{8,26},{9,... | collective-permute-start | bytes 86024 | tf_op jit(solution)/shard_map/sum_over_devices/ppermute | solution.py:448
  24.6 0.9 %collective-permute-start.7 = (f32[56,128]{1,0:T(8,128)S(1)}, f32[56,128]{1,0:T(8,128)S(1)}, u32[]{:S(2)}, u32[]{:S(2)}) collective-permute-start(f32[56,128]{1,0:T(8,128)S(1)} %add.12), channel_id=1, source_target_pairs={{0,16},{1,17},{2,18},{3,19},{4,20},{5,21},{6,22},{7,23},{8,24},{9,... | collective-permute-start | bytes 86024 | tf_op jit(solution)/shard_map/sum_over_devices/ppermute | solution.py:448
  25.4 0.5 %collective-permute-start.6 = (f32[56,128]{1,0:T(8,128)S(1)}, f32[56,128]{1,0:T(8,128)S(1)}, u32[]{:S(2)}, u32[]{:S(2)}) collective-permute-start(f32[56,128]{1,0:T(8,128)S(1)} %add.12), channel_id=1, source_target_pairs={{0,2},{1,3},{2,0},{3,1},{4,6},{5,7},{6,4},{7,5},{8,10},{9,11},{10,... | collective-permute-start | bytes 86024 | tf_op jit(solution)/shard_map/sum_over_devices/ppermute | solution.py:448
  25.9 1.3 %collective-permute-done.8 = f32[56,128]{1,0:T(8,128)S(1)} collective-permute-done((f32[56,128]{1,0:T(8,128)S(1)}, f32[56,128]{1,0:T(8,128)S(1)}, u32[]{:S(2)}, u32[]{:S(2)}) %collective-permute-start.8) | collective-permute-done | bytes 28704 | tf_op jit(solution)/shard_map/sum_over_devices/ppermute | solution.py:448
  27.2 1.2 %collective-permute-done.7 = f32[56,128]{1,0:T(8,128)S(1)} collective-permute-done((f32[56,128]{1,0:T(8,128)S(1)}, f32[56,128]{1,0:T(8,128)S(1)}, u32[]{:S(2)}, u32[]{:S(2)}) %collective-permute-start.7) | collective-permute-done | bytes 28704 | tf_op jit(solution)/shard_map/sum_over_devices/ppermute | solution.py:448
  28.4 0.9 %collective-permute-done.6 = f32[56,128]{1,0:T(8,128)S(1)} collective-permute-done((f32[56,128]{1,0:T(8,128)S(1)}, f32[56,128]{1,0:T(8,128)S(1)}, u32[]{:S(2)}, u32[]{:S(2)}) %collective-permute-start.6) | collective-permute-done | bytes 28704 | tf_op jit(solution)/shard_map/sum_over_devices/ppermute | solution.py:448
  29.3 3.7 %collective-permute-start.11 = (f32[56,128]{1,0:T(8,128)S(1)}, f32[56,128]{1,0:T(8,128)S(1)}, u32[]{:S(2)}, u32[]{:S(2)}) collective-permute-start(f32[56,128]{1,0:T(8,128)S(1)} %add_add_fusion.refs_0_), channel_id=1, source_target_pairs={{0,12},{1,13},{2,14},{3,15},{4,8},{5,9},{6,10},{7,11},{8,4},{9,5},... | collective-permute-start | bytes 86024 | tf_op jit(solution)/shard_map/sum_over_devices/ppermute | solution.py:448
  33.0 2.5 %collective-permute-start.10 = (f32[56,128]{1,0:T(8,128)S(1)}, f32[56,128]{1,0:T(8,128)S(1)}, u32[]{:S(2)}, u32[]{:S(2)}) collective-permute-start(f32[56,128]{1,0:T(8,128)S(1)} %add_add_fusion.refs_0_), channel_id=1, source_target_pairs={{0,8},{1,9},{2,10},{3,11},{4,12},{5,13},{6,14},{7,15},{8,0},{9,1},... | collective-permute-start | bytes 86024 | tf_op jit(solution)/shard_map/sum_over_devices/ppermute | solution.py:448
  35.5 0.5 %collective-permute-start.9 = (f32[56,128]{1,0:T(8,128)S(1)}, f32[56,128]{1,0:T(8,128)S(1)}, u32[]{:S(2)}, u32[]{:S(2)}) collective-permute-start(f32[56,128]{1,0:T(8,128)S(1)} %add_add_fusion.refs_0_), channel_id=1, source_target_pairs={{0,4},{1,5},{2,6},{3,7},{4,0},{5,1},{6,2},{7,3},{8,12},{9,13},{10,... | collective-permute-start | bytes 86024 | tf_op jit(solution)/shard_map/sum_over_devices/ppermute | solution.py:448
  36.0 1.9 %collective-permute-done.10.refs_2_ = f32[56,128]{1,0:T(8,128)S(1)} collective-permute-done((f32[56,128]{1,0:T(8,128)S(1)}, f32[56,128]{1,0:T(8,128)S(1)}, u32[]{:S(2)}, u32[]{:S(2)}) %collective-permute-start.10) | collective-permute-done | bytes 28704 | tf_op jit(solution)/shard_map/sum_over_devices/ppermute | solution.py:448
  37.9 1.5 %collective-permute-done.9.refs_1_ = f32[56,128]{1,0:T(8,128)S(1)} collective-permute-done((f32[56,128]{1,0:T(8,128)S(1)}, f32[56,128]{1,0:T(8,128)S(1)}, u32[]{:S(2)}, u32[]{:S(2)}) %collective-permute-start.9) | collective-permute-done | bytes 28704 | tf_op jit(solution)/shard_map/sum_over_devices/ppermute | solution.py:448
  39.4 2.8 %orthonormalize.1 = (f32[1280,128]{1,0:T(8,128)}, f32[20,20]{1,0:T(8,128)}) custom-call(bf16[128,4096]{1,0:T(8,128)(2,1)S(1)} %get-tuple-element.20.refs_2_.first_half, bf16[128,4096]{1,0:T(8,128)(2,1)S(1)} %get-tuple-element.21.refs_3_.second_half, bf16[64,8192]{1,0:T(8,128)(2,1)S(1)} %get-tuple-element.34.split, f32[56,128]{1,0:T(8,128)S(1)} %add_add_fusion.refs_0_, ...), custom_call_target="tpu_custom_call" | custom-call | flops 201326592 | bytes 655360 | tf_op jit(solution)/shard_map/orthonormalize/pallas_call | solution.py:541
  (9 shorter events, 0.0 us)
Async XLA Ops:
  0.6 0.9 %copy-start.2 = (f32[4,8,8,128]{3,2,1,0:T(8,128)S(1)}, f32[4,8,8,128]{3,2,1,0:T(8,128)}, u32[]{:S(2)}) copy-start(f32[4,8,8,128]{3,2,1,0:T(8,128)} %start_there.1) | copy-start | bytes 393220
  1.5 0.8 %copy-start.3 = (f32[8,8,128]{2,1,0:T(8,128)S(1)}, f32[8,8,128]{2,1,0:T(8,128)}, u32[]{:S(2)}) copy-start(f32[8,8,128]{2,1,0:T(8,128)} %diagonal_there.1) | copy-start | bytes 98308
  2.7 5.6 %collective-permute-start = (f32[5,8,128]{2,1,0:T(8,128)S(1)}, f32[5,8,128]{2,1,0:T(8,128)S(1)}, u32[]{:S(2)}, u32[]{:S(2)}) collective-permute-start(f32[5,8,128]{2,1,0:T(8,128)S(1)} %get-tuple-element.25), channel_id=1, source_target_pairs={{0,16},{16,0},{1,17},{17,1},{2,18},{18,2},{3,19},{19,3},{4,20},{20... | collective-permute-start | bytes 61448 | tf_op jit(solution)/shard_map/halo_x/ppermute | solution.py:63
  5.7 1.5 %copy-start = (f32[56,8,8,128]{3,2,1,0:T(8,128)S(1)}, f32[56,8,8,128]{3,2,1,0:T(8,128)}, u32[]{:S(2)}) copy-start(f32[56,8,8,128]{3,2,1,0:T(8,128)} %param.3) | copy-start | bytes 5505028
  7.2 3.6 %copy-start.1 = (f32[56,8,8,128]{3,2,1,0:T(8,128)S(1)}, f32[56,8,8,128]{3,2,1,0:T(8,128)}, u32[]{:S(2)}) copy-start(f32[56,8,8,128]{3,2,1,0:T(8,128)} %param.3) | copy-start | bytes 5505028
  8.5 4.6 %collective-permute-start.1 = (f32[23,8,128]{2,1,0:T(8,128)S(1)}, f32[23,8,128]{2,1,0:T(8,128)S(1)}, u32[]{:S(2)}, u32[]{:S(2)}) collective-permute-start(f32[23,8,128]{2,1,0:T(8,128)S(1)} %get-tuple-element.28), channel_id=1, source_target_pairs={{0,4},{4,0},{8,12},{12,8},{1,5},{5,1},{9,13},{13,9},{2,6},{6,2},{1... | collective-permute-start | bytes 282632 | tf_op jit(solution)/shard_map/halo_y/ppermute | solution.py:63
  10.1 3.0 %collective-permute-start.2 = (f32[23,8,128]{2,1,0:T(8,128)S(1)}, f32[23,8,128]{2,1,0:T(8,128)S(1)}, u32[]{:S(2)}, u32[]{:S(2)}) collective-permute-start(f32[23,8,128]{2,1,0:T(8,128)S(1)} %get-tuple-element.29), channel_id=1, source_target_pairs={{4,8},{8,4},{5,9},{9,5},{6,10},{10,6},{7,11},{11,7},{20,24},{24,20... | collective-permute-start | bytes 282632 | tf_op jit(solution)/shard_map/halo_y/ppermute | solution.py:63
  13.2 1.7 %collective-permute-start.3 = (f32[34,8,128]{2,1,0:T(8,128)S(1)}, f32[34,8,128]{2,1,0:T(8,128)S(1)}, u32[]{:S(2)}, u32[]{:S(2)}) collective-permute-start(f32[34,8,128]{2,1,0:T(8,128)S(1)} %get-tuple-element.32), channel_id=1, source_target_pairs={{0,1},{1,0},{2,3},{3,2},{4,5},{5,4},{6,7},{7,6},{8,9},{9,8},{10,11... | collective-permute-start | bytes 417800 | tf_op jit(solution)/shard_map/halo_z/ppermute | solution.py:63
  13.3 5.5 %collective-permute-start.4 = (f32[34,8,128]{2,1,0:T(8,128)S(1)}, f32[34,8,128]{2,1,0:T(8,128)S(1)}, u32[]{:S(2)}, u32[]{:S(2)}) collective-permute-start(f32[34,8,128]{2,1,0:T(8,128)S(1)} %get-tuple-element.33), channel_id=1, source_target_pairs={{0,3},{1,2},{2,1},{3,0},{4,7},{5,6},{6,5},{7,4},{8,11},{9,10},{10,... | collective-permute-start | bytes 417800 | tf_op jit(solution)/shard_map/halo_z/ppermute | solution.py:63
  21.2 1.3 %collective-permute-start.5 = (f32[56,128]{1,0:T(8,128)S(1)}, f32[56,128]{1,0:T(8,128)S(1)}, u32[]{:S(2)}, u32[]{:S(2)}) collective-permute-start(f32[56,128]{1,0:T(8,128)S(1)} %get-tuple-element.35), channel_id=1, source_target_pairs={{0,1},{1,0},{2,3},{3,2},{4,5},{5,4},{6,7},{7,6},{8,9},{9,8},{10,11... | collective-permute-start | bytes 86024 | tf_op jit(solution)/shard_map/sum_over_devices/ppermute | solution.py:448
  22.5 4.8 %collective-permute-start.8 = (f32[56,128]{1,0:T(8,128)S(1)}, f32[56,128]{1,0:T(8,128)S(1)}, u32[]{:S(2)}, u32[]{:S(2)}) collective-permute-start(f32[56,128]{1,0:T(8,128)S(1)} %add.12), channel_id=1, source_target_pairs={{0,18},{1,19},{2,16},{3,17},{4,22},{5,23},{6,20},{7,21},{8,26},{9,... | collective-permute-start | bytes 86024 | tf_op jit(solution)/shard_map/sum_over_devices/ppermute | solution.py:448
  24.6 3.9 %collective-permute-start.7 = (f32[56,128]{1,0:T(8,128)S(1)}, f32[56,128]{1,0:T(8,128)S(1)}, u32[]{:S(2)}, u32[]{:S(2)}) collective-permute-start(f32[56,128]{1,0:T(8,128)S(1)} %add.12), channel_id=1, source_target_pairs={{0,16},{1,17},{2,18},{3,19},{4,20},{5,21},{6,22},{7,23},{8,24},{9,... | collective-permute-start | bytes 86024 | tf_op jit(solution)/shard_map/sum_over_devices/ppermute | solution.py:448
  25.4 3.9 %collective-permute-start.6 = (f32[56,128]{1,0:T(8,128)S(1)}, f32[56,128]{1,0:T(8,128)S(1)}, u32[]{:S(2)}, u32[]{:S(2)}) collective-permute-start(f32[56,128]{1,0:T(8,128)S(1)} %add.12), channel_id=1, source_target_pairs={{0,2},{1,3},{2,0},{3,1},{4,6},{5,7},{6,4},{7,5},{8,10},{9,11},{10,... | collective-permute-start | bytes 86024 | tf_op jit(solution)/shard_map/sum_over_devices/ppermute | solution.py:448
  29.3 6.7 %collective-permute-start.11 = (f32[56,128]{1,0:T(8,128)S(1)}, f32[56,128]{1,0:T(8,128)S(1)}, u32[]{:S(2)}, u32[]{:S(2)}) collective-permute-start(f32[56,128]{1,0:T(8,128)S(1)} %add_add_fusion.refs_0_), channel_id=1, source_target_pairs={{0,12},{1,13},{2,14},{3,15},{4,8},{5,9},{6,10},{7,11},{8,4},{9,5},... | collective-permute-start | bytes 86024 | tf_op jit(solution)/shard_map/sum_over_devices/ppermute | solution.py:448
  33.0 4.9 %collective-permute-start.10 = (f32[56,128]{1,0:T(8,128)S(1)}, f32[56,128]{1,0:T(8,128)S(1)}, u32[]{:S(2)}, u32[]{:S(2)}) collective-permute-start(f32[56,128]{1,0:T(8,128)S(1)} %add_add_fusion.refs_0_), channel_id=1, source_target_pairs={{0,8},{1,9},{2,10},{3,11},{4,12},{5,13},{6,14},{7,15},{8,0},{9,1},... | collective-permute-start | bytes 86024 | tf_op jit(solution)/shard_map/sum_over_devices/ppermute | solution.py:448
  35.5 3.9 %collective-permute-start.9 = (f32[56,128]{1,0:T(8,128)S(1)}, f32[56,128]{1,0:T(8,128)S(1)}, u32[]{:S(2)}, u32[]{:S(2)}) collective-permute-start(f32[56,128]{1,0:T(8,128)S(1)} %add_add_fusion.refs_0_), channel_id=1, source_target_pairs={{0,4},{1,5},{2,6},{3,7},{4,0},{5,1},{6,2},{7,3},{8,12},{9,13},{10,... | collective-permute-start | bytes 86024 | tf_op jit(solution)/shard_map/sum_over_devices/ppermute | solution.py:448

commit v3 on v2

--- a/solution.py
+++ b/solution.py
@@ -1,4 +1,5 @@
 import functools
+import itertools
 
 import jax
 import jax.numpy as jnp
@@ -15,6 +16,7 @@
 Z, Y, X = 8, 8, 128
 CELLS = Z * Y
 HALF = CELLS // 2
+PIECE = 16
 SLOTS = 16
 BPAD = 32
 BROWS = 24
@@ -55,12 +57,26 @@
     return pick
 
 
-def swaps(arrays, axis, count, around=True):
-    first = [(i, i ^ 1) for i in range(count)]
-    second = [(i, (i + 1 if i % 2 else i - 1) % count) for i in range(count)]
-    if not around:
-        second = second[1:-1]
-    return [lax.ppermute(a, axis, pairs) for a, pairs in zip(arrays, (first, second))]
+def swaps(arrays, sizes, axis):
+    first, second = [], []
+    dimension = AXES.index(axis)
+    aside = 0 if dimension == 2 else 2
+    for place in itertools.product(*map(range, sizes)):
+        at = place[dimension]
+
+        def pair(dimension, to):
+            other = place[:dimension] + (to,) + place[dimension + 1 :]
+            return tuple(
+                (p[0] * sizes[1] + p[1]) * sizes[2] + p[2] for p in (place, other)
+            )
+
+        first.append(pair(dimension, at ^ 1))
+        beyond = at + 1 if at % 2 else at - 1
+        if 0 <= beyond < sizes[dimension]:
+            second.append(pair(dimension, beyond))
+        else:
+            second.append(pair(aside, place[aside] ^ 1))
+    return [lax.ppermute(a, AXES, pairs) for a, pairs in zip(arrays, (first, second))]
 
 
 def pack_x(fields, start_there, diagonal_there, start, diagonal, *refs):
@@ -130,7 +146,7 @@
         send(4 * (fields + 1) + f // 2, sides[f], sides[min(f + 1, fields)])
 
 
-def pack_z(fields, count, ways, start, diagonal, _, sides, *refs):
+def pack_z(fields, count, ways, start, diagonal, _, __, sides, *refs):
     received, (beyond, beyond_sides, *sends) = refs[:ways], refs[ways:]
     row, lane = iotas()
     pick = facing("gy", count, received)
@@ -349,9 +365,15 @@
     return both[:, :padded] + both[:, padded:]
 
 
-def history_kernel(count, first, history, split, gram):
+def load_history(first, history, here, done):
+    copy = pltpu.make_async_copy(history.at[:, pl.ds(first, Z // 2)], here, done)
+    copy.start()
+    copy.wait()
+
+
+def history_kernel(count, history, split, gram):
     for cell in range(HALF):
-        high, low = split_rows(history[pl.ds(first + cell, count, stride=CELLS), :], HPAD)
+        high, low = split_rows(history[pl.ds(cell, count, stride=HALF), :], HPAD)
         split[0:HPAD, cell * X : (cell + 1) * X] = high
         split[HPAD : 2 * HPAD, cell * X : (cell + 1) * X] = low
     gram[...] = join_lanes(join(product(split[...], split[...]), HPAD), HPAD)
@@ -369,7 +391,7 @@
 
 
 def finish(columns, cells, first_half, second_half, split, *refs):
-    parts, (out, factor) = refs[:-2], refs[-2:]
+    parts, (out, factor, staged, factor_staged, done) = refs[:-5], refs[-5:]
     total = (parts[0][...] + parts[1][...]) + (parts[2][...] + parts[3][...])
     total = total * (1.0 / cells)
     history_gram = jnp.concatenate([total[:, 0:HPAD], jnp.zeros((HPAD - ROWS, HPAD), F32)], axis=0)
@@ -399,7 +421,9 @@
     pivots = jnp.sum(jnp.where(lane == row, work, 0.0), axis=1, keepdims=True)
     good = lax.broadcasted_iota(jnp.int32, (BROWS, 1), 0) < columns
     work = work * jnp.where(good, 1.0 / jnp.sqrt(jnp.where(good, pivots, 1.0)), 0.0)
-    factor[...] = jnp.where(lane >= row, work, 0.0)[0:columns, 0:columns]
+    factor_staged[...] = jnp.where(lane >= row, work, 0.0)[0:columns, 0:columns]
+    copies = [pltpu.make_async_copy(factor_staged, factor, done.at[0])]
+    copies[0].start()
     work = jnp.concatenate([work, jnp.zeros((BPAD - BROWS, X), F32)], axis=0)
     history_high, history_low = split_matrix(-work[:, X - HPAD :])
     basis_high, basis_low = split_matrix(work[:, BPAD : 2 * BPAD])
@@ -413,8 +437,10 @@
         axis=0,
     )
     width = 4 * X
-    for c in range(CELLS * X // width):
-        half, base = (first_half, 0) if c * width < HALF * X else (second_half, HALF * X)
+    inside = width // X
+    blocks = staged.reshape(columns, CELLS, X)
+    for c in range(CELLS // inside):
+        half, base = (first_half, 0) if c * inside < HALF else (second_half, HALF * X)
         right = jnp.concatenate(
             [
                 half[:, c * width - base : (c + 1) * width - base],
@@ -423,30 +449,46 @@
             axis=0,
         )
         result = join(jnp.dot(left, right, preferred_element_type=F32), BPAD)
-        for j in range(width // X):
-            out[pl.ds(c * (width // X) + j, columns, stride=CELLS), :] = result[
+        for j in range(inside):
+            staged[pl.ds(c * inside + j, columns, stride=CELLS), :] = result[
                 0:columns, j * X : (j + 1) * X
             ]
-
-
-def call(kernel, outs, flops, bytes_accessed, scratch=(), **specs):
+        cells_done = (c + 1) * inside
+        if cells_done % PIECE == 0:
+            piece = pl.ds(cells_done - PIECE, PIECE)
+            copies.append(
+                pltpu.make_async_copy(
+                    blocks.at[:, piece, :], out.at[:, piece, :], done.at[len(copies)]
+                )
+            )
+            copies[-1].start()
+    for copy in copies:
+        copy.wait()
+
+
+def call(
+    kernel,
+    outs,
+    flops,
+    bytes_accessed,
+    scratch=(),
+    limit=40 * 1024 * 1024,
+    place=jax.ShapeDtypeStruct,
+    **specs,
+):
     return pl.pallas_call(
         kernel,
         **specs,
-        out_shape=[jax.ShapeDtypeStruct(shape, dtype) for shape, dtype in outs],
+        out_shape=[place(shape, dtype) for shape, dtype in outs],
         scratch_shapes=list(scratch),
-        compiler_params=pltpu.CompilerParams(vmem_limit_bytes=40 * 1024 * 1024),
+        compiler_params=pltpu.CompilerParams(vmem_limit_bytes=limit),
         cost_estimate=pl.CostEstimate(flops=flops, bytes_accessed=bytes_accessed, transcendentals=0),
     )
 
 
-def exchange_sums(array, sizes, bits):
-    count = sizes[0] * sizes[1] * sizes[2]
-    arrays = [array]
-    for mask in range(1, 1 << len(bits)):
-        flip = sum(bit for i, bit in enumerate(bits) if mask >> i & 1)
-        arrays.append(lax.ppermute(array, AXES, [(i, i ^ flip) for i in range(count)]))
-    return arrays
+def exchange_sums(array, sizes, flips):
+    devices = range(sizes[0] * sizes[1] * sizes[2])
+    return [array] + [lax.ppermute(array, AXES, [(i, i ^ flip) for i in devices]) for flip in flips]
 
 
 def on_device(sizes, history, start, diagonal):
@@ -458,27 +500,45 @@
     cells = Z * Y * X * sizes[0] * sizes[1] * sizes[2]
     tile = Y * X * 4
 
-    def history_products(half):
+    there = pl.BlockSpec(memory_space=pltpu.HBM)
+    anywhere = pl.BlockSpec(memory_space=pl.ANY)
+    here = pl.BlockSpec(memory_space=pltpu.VMEM)
+
+    def history_half(half):
+        with jax.named_scope("load_history"):
+            return call(
+                functools.partial(load_history, half * (Z // 2)),
+                [((history_count, Z // 2, Y, X), F32)],
+                1000,
+                history.size * 4,
+                [pltpu.SemaphoreType.DMA],
+                None,
+                pltpu.VMEM,
+                in_specs=[there],
+            )(history)[0].reshape(history_count * HALF, X)
+
+    def history_products(rows):
         with jax.named_scope("history_products"):
             return call(
-                functools.partial(history_kernel, history_count, half * HALF),
+                functools.partial(history_kernel, history_count),
                 [((2 * HPAD, HALF * X), BF16), ((HPAD, HPAD), F32)],
                 128 * 128 * CELLS * X,
                 history.size * 2,
-            )(history.reshape(history_count * CELLS, X))
+            )(rows)
 
     with jax.named_scope("halo_x"):
-        there = pl.BlockSpec(memory_space=pltpu.HBM)
         start, diagonal, *sends = call(
             functools.partial(pack_x, fields),
             [(start.shape, F32), (diagonal.shape, F32)] + [((all_fields, Y, X), F32)] * ways["gx"],
             1000,
             start.size * 4,
             [pltpu.SemaphoreType.DMA((2,))],
+            None,
+            pltpu.VMEM,
             in_specs=[there, there],
         )(start, diagonal)
-        received = swaps(sends, "gx", count["gx"])
-    first_split, first_gram = history_products(0)
+        received = swaps(sends, sizes, "gx")
+    first_rows = history_half(0)
     with jax.named_scope("halo_y"):
         y_tiles = 4 * all_fields + (all_fields + 1) // 2
         sides, *sends = call(
@@ -486,9 +546,11 @@
             [((all_fields, Y, X), F32)] + [((y_tiles, Y, X), F32)] * ways["gy"],
             1000,
             start.size * 4,
-        )(start, diagonal, first_gram, *received)
-        received = swaps(sends, "gy", count["gy"], False)
-    second_split, second_gram = history_products(1)
+            in_specs=[here, here, anywhere] + [here] * ways["gx"],
+        )(start, diagonal, first_rows, *received)
+        received = swaps(sends, sizes, "gy")
+    second_rows = history_half(1)
+    first_split, first_gram = history_products(first_rows)
     with jax.named_scope("halo_z"):
         beyond, beyond_sides, *sends = call(
             functools.partial(pack_z, fields, count["gy"], ways["gy"]),
@@ -496,8 +558,10 @@
             + [((z_tiles(fields), Y, X), F32)] * ways["gz"],
             1000,
             start.size * 4,
-        )(start, diagonal, second_gram, sides, *received)
-        received = swaps(sends, "gz", count["gz"])
+            in_specs=[here, here, here, anywhere, here] + [here] * ways["gy"],
+        )(start, diagonal, first_gram, second_rows, sides, *received)
+        received = swaps(sends, sizes, "gz")
+    second_split, second_gram = history_products(second_rows)
     with jax.named_scope("matrix_powers"):
         split, sums = call(
             functools.partial(powers, fields, count["gz"], ways["gz"]),
@@ -524,25 +588,31 @@
             second_gram,
         )
     with jax.named_scope("sum_over_devices"):
-        devices = sizes[0] * sizes[1] * sizes[2]
         bits = []
         for axis, stride in (("gz", 1), ("gx", sizes[1] * sizes[2]), ("gy", sizes[2])):
             bits += [stride << b for b in range(count[axis].bit_length() - 1)]
-        first, rest = bits[: 1 + (len(bits) - 1) % 2], bits[1 + (len(bits) - 1) % 2 :]
-        for bit in first:
+        alone = 1 + (len(bits) - 1) % 2
+        for bit in bits[:alone]:
             pair = exchange_sums(sums, sizes, [bit])
             sums = pair[0] + pair[1]
-        while rest:
-            parts = exchange_sums(sums, sizes, rest[:2])
-            rest = rest[2:]
-            if rest:
+        for k in range(alone, len(bits), 2):
+            if k > alone:
                 sums = (parts[0] + parts[1]) + (parts[2] + parts[3])
+            one, two = bits[k : k + 2]
+            flips = [one, two ^ 1, one ^ two ^ 1] if k + 2 == len(bits) else [one ^ 1, two ^ 1, one ^ two]
+            parts = exchange_sums(sums, sizes, flips)
     with jax.named_scope("orthonormalize"):
         out, factor = call(
             functools.partial(finish, columns, cells),
-            [((columns * CELLS, X), F32), ((columns, columns), F32)],
+            [((columns, CELLS, X), F32), ((columns, columns), F32)],
             2 * 192 * 64 * CELLS * X,
             columns * CELLS * X * 4,
+            [
+                pltpu.VMEM((columns * CELLS, X), F32),
+                pltpu.VMEM((columns, columns), F32),
+                pltpu.SemaphoreType.DMA((CELLS // PIECE + 1,)),
+            ],
+            out_specs=[pl.BlockSpec(memory_space=pltpu.HBM)] * 2,
         )(first_split, second_split, split, *parts)
     return out.reshape(columns, Z, Y, X), factor
 

time: 42.4 us -> 37.6 us (0.89)
  local copies, waits for them, and re-layouts: 3.16 us -> 0 us
  Pallas kernels: 8.02 us -> 11 us
  waiting for transfers between devices: 12.7 us -> 10.3 us
  starting transfers between devices: 17.6 us -> 15.3 us
    unnamed x8 -> x0, local copies, waits for them, and re-layouts: 3.16 us -> none
    ppermute x12, waiting for transfers between devices: 12.7 us -> 10.3 us  [the longest x7 7.32 us: exchange_sums(): lax.ppermute(array, AXES, [(i, i ^ flip) for i in devices])]
    ppermute x12, starting transfers between devices: 17.6 us -> 15.3 us  [the longest x7 8.02 us: exchange_sums(): lax.ppermute(array, AXES, [(i, i ^ flip) for i in devices])]
    pallas_call x3 -> x5, Pallas kernels: 4.97 us -> 7.23 us  [the longest x1 2.68 us: on_device(): call(functools.partial(finish, columns, cells), [((columns, CELLS, X), F3...]
    pallas_call x1, Pallas kernels: 0.35 us -> 1.08 us  [on_device(): call(functools.partial(pack_x, fields), [(start.shape, F32), (diagonal.sh...]
  transfers between devices with their start and end apart: 12 -> 12, of which waited for: 8 -> 9; matrix products, arithmetic and copies ran while one was open for 0% -> 0% of each run, Pallas kernels for 5% -> 12%
where the time goes in v3:
time: 37.6 us; the launch traced here: 37.4 us
  starting transfers between devices  15.3 us (41%)
  Pallas kernels  11 us (29%)
  waiting for transfers between devices  10.3 us (27%)
  between operations  0.71 us (2%)
    ppermute x7, starting transfers between devices, exchange_sums(): lax.ppermute(array, AXES, [(i, i ^ flip) for i in devices])  8.02 us
    ppermute x7, waiting for transfers between devices, exchange_sums(): lax.ppermute(array, AXES, [(i, i ^ flip) for i in devices])  7.32 us
    ppermute x5, starting transfers between devices, swaps(): lax.ppermute(a, AXES, pairs)  7.28 us
    ppermute x5, waiting for transfers between devices, swaps(): lax.ppermute(a, AXES, pairs)  3.02 us
    pallas_call x1, Pallas kernels, on_device(): call(functools.partial(finish, columns, cells), [((columns, CELLS, X), F3...  2.68 us
    pallas_call x1, Pallas kernels, on_device(): call(functools.partial(powers, fields, count['gz'], ways['gz']), [((2 * B...  2.43 us
    pallas_call x2, Pallas kernels, history_half(): call(functools.partial(load_history, half * (Z // 2)), [((history_count,...  2.37 us
    pallas_call x2, Pallas kernels, history_products(): call(functools.partial(history_kernel, history_count), [((2 * HPAD, HALF...  2.17 us
  transfers between devices with their start and end apart: 12, of which 9 were waited for; matrix products, arithmetic and copies ran while one was open for 0% of the time, Pallas kernels for 12%

profile of v3, /device:TPU:0, one launch (start us, length us, event | category | flops | bytes accessed | tf_op | source)
XLA Modules:
  0.0 37.4 jit_solution(15600516010641033494)
XLA Ops:
  0.6 1.1 %halo_x.1 = (f32[4,8,8,128]{3,2,1,0:T(8,128)S(1)}, f32[8,8,128]{2,1,0:T(8,128)S(1)}, f32[5,8,128]{2,1,0:T(8,128)S(1)}) custom-call(f32[4,8,8,128]{3,2,1,0:T(8,128)} %start_there.1, f32[8,8,128]{2,1,0:T(8,128)} %diagonal_there.1), custom_call_target="tpu_custom_call" | custom-call | flops 1000 | bytes 131072 | tf_op jit(solution)/shard_map/halo_x/pallas_call | solution.py:530
  1.7 3.0 %collective-permute-start = (f32[5,8,128]{2,1,0:T(8,128)S(1)}, f32[5,8,128]{2,1,0:T(8,128)S(1)}, u32[]{:S(2)}, u32[]{:S(2)}) collective-permute-start(f32[5,8,128]{2,1,0:T(8,128)S(1)} %get-tuple-element.24), channel_id=1, source_target_pairs={{0,16},{1,17},{2,18},{3,19},{4,20},{5,21},{6,22},{7,23},{8,24},{9,... | collective-permute-start | bytes 61448 | tf_op jit(solution)/shard_map/halo_x/ppermute | solution.py:79
  4.7 1.2 %load_history.2 = f32[56,4,8,128]{3,2,1,0:T(8,128)S(1)} custom-call(f32[56,8,8,128]{3,2,1,0:T(8,128)} %history.3), custom_call_target="tpu_custom_call" | custom-call | flops 1000 | bytes 1835008 | tf_op jit(solution)/shard_map/load_history/pallas_call | solution.py:509
  5.9 0.6 %collective-permute-done.refs_0_ = f32[5,8,128]{2,1,0:T(8,128)S(1)} collective-permute-done((f32[5,8,128]{2,1,0:T(8,128)S(1)}, f32[5,8,128]{2,1,0:T(8,128)S(1)}, u32[]{:S(2)}, u32[]{:S(2)}) %collective-permute-start) | collective-permute-done | bytes 20512 | tf_op jit(solution)/shard_map/halo_x/ppermute | solution.py:79
  6.5 0.2 halo_y.1
  6.7 2.1 %collective-permute-start.1 = (f32[23,8,128]{2,1,0:T(8,128)S(1)}, f32[23,8,128]{2,1,0:T(8,128)S(1)}, u32[]{:S(2)}, u32[]{:S(2)}) collective-permute-start(f32[23,8,128]{2,1,0:T(8,128)S(1)} %get-tuple-element.27), channel_id=1, source_target_pairs={{0,4},{1,5},{2,6},{3,7},{4,0},{5,1},{6,2},{7,3},{8,12},{9,13},{10,... | collective-permute-start | bytes 282632 | tf_op jit(solution)/shard_map/halo_y/ppermute | solution.py:79
  8.8 1.2 %load_history.3 = f32[56,4,8,128]{3,2,1,0:T(8,128)S(1)} custom-call(f32[56,8,8,128]{3,2,1,0:T(8,128)} %history.3), custom_call_target="tpu_custom_call" | custom-call | flops 1000 | bytes 1835008 | tf_op jit(solution)/shard_map/load_history/pallas_call | solution.py:509
  10.0 1.1 %history_products.2 = (bf16[128,4096]{1,0:T(8,128)(2,1)S(1)}, f32[64,64]{1,0:T(8,128)S(1)}) custom-call(f32[1792,128]{1,0:T(8,128)S(1)} %bitcast.6), custom_call_target="tpu_custom_call" | custom-call | flops 134217728 | bytes 917504 | tf_op jit(solution)/shard_map/history_products/pallas_call | solution.py:522
  11.1 0.2 collective-permute-done.1.refs_0_
  11.4 0.0 collective-permute-done.2.refs_1_
  11.4 0.1 halo_z.1
  11.5 0.3 collective-permute-start.3
  11.8 1.8 %collective-permute-start.4 = (f32[34,8,128]{2,1,0:T(8,128)S(1)}, f32[34,8,128]{2,1,0:T(8,128)S(1)}, u32[]{:S(2)}, u32[]{:S(2)}) collective-permute-start(f32[34,8,128]{2,1,0:T(8,128)S(1)} %get-tuple-element.32), channel_id=1, source_target_pairs={{0,16},{1,2},{2,1},{3,19},{4,20},{5,6},{6,5},{7,23},{8,24},{9,10},... | collective-permute-start | bytes 417800 | tf_op jit(solution)/shard_map/halo_z/ppermute | solution.py:79
  13.6 1.1 %history_products.3 = (bf16[128,4096]{1,0:T(8,128)(2,1)S(1)}, f32[64,64]{1,0:T(8,128)S(1)}) custom-call(f32[1792,128]{1,0:T(8,128)S(1)} %bitcast.4), custom_call_target="tpu_custom_call" | custom-call | flops 134217728 | bytes 917504 | tf_op jit(solution)/shard_map/history_products/pallas_call | solution.py:522
  14.7 0.0 collective-permute-done.3.refs_0_
  14.7 2.2 %collective-permute-done.4.refs_1_ = f32[34,8,128]{2,1,0:T(8,128)S(1)} collective-permute-done((f32[34,8,128]{2,1,0:T(8,128)S(1)}, f32[34,8,128]{2,1,0:T(8,128)S(1)}, u32[]{:S(2)}, u32[]{:S(2)}) %collective-permute-start.4) | collective-permute-done | bytes 139296 | tf_op jit(solution)/shard_map/halo_z/ppermute | solution.py:79
  16.9 2.4 %matrix_powers.1 = (bf16[64,8192]{1,0:T(8,128)(2,1)S(1)}, f32[56,128]{1,0:T(8,128)S(1)}) custom-call(f32[4,8,8,128]{3,2,1,0:T(8,128)S(1)} %get-tuple-element.22.start, f32[8,8,128]{2,1,0:T(8,128)S(1)} %get-tuple-element.23.diagonal, f32[5,8,128]{2,1,0:T(8,128)S(1)} %get-tuple-element.25.sides, f32[5,8,8,128]{3,2,1,0:T(8,128)S(1)} %get-tuple-element.29.beyond, ...), custom_call_target="tpu_custom_call" | custom-call | flops 201326592 | bytes 131072 | tf_op jit(solution)/shard_map/matrix_powers/pallas_call | solution.py:566
  19.3 0.0 collective-permute-start.5
  19.4 1.2 %collective-permute-done.5 = f32[56,128]{1,0:T(8,128)S(1)} collective-permute-done((f32[56,128]{1,0:T(8,128)S(1)}, f32[56,128]{1,0:T(8,128)S(1)}, u32[]{:S(2)}, u32[]{:S(2)}) %collective-permute-start.5) | collective-permute-done | bytes 28704 | tf_op jit(solution)/shard_map/sum_over_devices/ppermute | solution.py:491
  20.6 2.1 %collective-permute-start.8 = (f32[56,128]{1,0:T(8,128)S(1)}, f32[56,128]{1,0:T(8,128)S(1)}, u32[]{:S(2)}, u32[]{:S(2)}) collective-permute-start(f32[56,128]{1,0:T(8,128)S(1)} %add.12), channel_id=1, source_target_pairs={{0,18},{1,19},{2,16},{3,17},{4,22},{5,23},{6,20},{7,21},{8,26},{9,... | collective-permute-start | bytes 86024 | tf_op jit(solution)/shard_map/sum_over_devices/ppermute | solution.py:491
  22.7 0.0 collective-permute-start.7
  22.7 1.1 %collective-permute-start.6 = (f32[56,128]{1,0:T(8,128)S(1)}, f32[56,128]{1,0:T(8,128)S(1)}, u32[]{:S(2)}, u32[]{:S(2)}) collective-permute-start(f32[56,128]{1,0:T(8,128)S(1)} %add.12), channel_id=1, source_target_pairs={{0,3},{1,2},{2,1},{3,0},{4,7},{5,6},{6,5},{7,4},{8,11},{9,10},{10,... | collective-permute-start | bytes 86024 | tf_op jit(solution)/shard_map/sum_over_devices/ppermute | solution.py:491
  23.8 1.6 %collective-permute-done.8 = f32[56,128]{1,0:T(8,128)S(1)} collective-permute-done((f32[56,128]{1,0:T(8,128)S(1)}, f32[56,128]{1,0:T(8,128)S(1)}, u32[]{:S(2)}, u32[]{:S(2)}) %collective-permute-start.8) | collective-permute-done | bytes 28704 | tf_op jit(solution)/shard_map/sum_over_devices/ppermute | solution.py:491
  25.3 0.9 %collective-permute-done.7 = f32[56,128]{1,0:T(8,128)S(1)} collective-permute-done((f32[56,128]{1,0:T(8,128)S(1)}, f32[56,128]{1,0:T(8,128)S(1)}, u32[]{:S(2)}, u32[]{:S(2)}) %collective-permute-start.7) | collective-permute-done | bytes 28704 | tf_op jit(solution)/shard_map/sum_over_devices/ppermute | solution.py:491
  26.2 0.0 collective-permute-done.6
  26.2 3.6 %collective-permute-start.11 = (f32[56,128]{1,0:T(8,128)S(1)}, f32[56,128]{1,0:T(8,128)S(1)}, u32[]{:S(2)}, u32[]{:S(2)}) collective-permute-start(f32[56,128]{1,0:T(8,128)S(1)} %add_add_fusion.refs_0_), channel_id=1, source_target_pairs={{0,13},{1,12},{2,15},{3,14},{4,9},{5,8},{6,11},{7,10},{8,5},{9,4},... | collective-permute-start | bytes 86024 | tf_op jit(solution)/shard_map/sum_over_devices/ppermute | solution.py:491
  29.9 0.6 %collective-permute-start.10 = (f32[56,128]{1,0:T(8,128)S(1)}, f32[56,128]{1,0:T(8,128)S(1)}, u32[]{:S(2)}, u32[]{:S(2)}) collective-permute-start(f32[56,128]{1,0:T(8,128)S(1)} %add_add_fusion.refs_0_), channel_id=1, source_target_pairs={{0,9},{1,8},{2,11},{3,10},{4,13},{5,12},{6,15},{7,14},{8,1},{9,0},... | collective-permute-start | bytes 86024 | tf_op jit(solution)/shard_map/sum_over_devices/ppermute | solution.py:491
  30.5 0.5 %collective-permute-start.9 = (f32[56,128]{1,0:T(8,128)S(1)}, f32[56,128]{1,0:T(8,128)S(1)}, u32[]{:S(2)}, u32[]{:S(2)}) collective-permute-start(f32[56,128]{1,0:T(8,128)S(1)} %add_add_fusion.refs_0_), channel_id=1, source_target_pairs={{0,4},{1,5},{2,6},{3,7},{4,0},{5,1},{6,2},{7,3},{8,12},{9,13},{10,... | collective-permute-start | bytes 86024 | tf_op jit(solution)/shard_map/sum_over_devices/ppermute | solution.py:491
  31.0 0.5 %collective-permute-done.11.refs_3_ = f32[56,128]{1,0:T(8,128)S(1)} collective-permute-done((f32[56,128]{1,0:T(8,128)S(1)}, f32[56,128]{1,0:T(8,128)S(1)}, u32[]{:S(2)}, u32[]{:S(2)}) %collective-permute-start.11) | collective-permute-done | bytes 28704 | tf_op jit(solution)/shard_map/sum_over_devices/ppermute | solution.py:491
  31.5 2.6 %collective-permute-done.10.refs_2_ = f32[56,128]{1,0:T(8,128)S(1)} collective-permute-done((f32[56,128]{1,0:T(8,128)S(1)}, f32[56,128]{1,0:T(8,128)S(1)}, u32[]{:S(2)}, u32[]{:S(2)}) %collective-permute-start.10) | collective-permute-done | bytes 28704 | tf_op jit(solution)/shard_map/sum_over_devices/ppermute | solution.py:491
  34.1 0.6 %collective-permute-done.9.refs_1_ = f32[56,128]{1,0:T(8,128)S(1)} collective-permute-done((f32[56,128]{1,0:T(8,128)S(1)}, f32[56,128]{1,0:T(8,128)S(1)}, u32[]{:S(2)}, u32[]{:S(2)}) %collective-permute-start.9) | collective-permute-done | bytes 28704 | tf_op jit(solution)/shard_map/sum_over_devices/ppermute | solution.py:491
  34.7 2.7 %orthonormalize.1 = (f32[20,64,128]{2,1,0:T(8,128)}, f32[20,20]{1,0:T(8,128)}) custom-call(bf16[128,4096]{1,0:T(8,128)(2,1)S(1)} %get-tuple-element.20.refs_2_.first_half, bf16[128,4096]{1,0:T(8,128)(2,1)S(1)} %get-tuple-element.21.refs_3_.second_half, bf16[64,8192]{1,0:T(8,128)(2,1)S(1)} %get-tuple-element.34.split, f32[56,128]{1,0:T(8,128)S(1)} %add_add_fusion.refs_0_, ...), custom_call_target="tpu_custom_call" | custom-call | flops 201326592 | bytes 655360 | tf_op jit(solution)/shard_map/orthonormalize/pallas_call | solution.py:605
  (3 shorter events, 0.0 us)
Async XLA Ops:
  1.7 4.8 %collective-permute-start = (f32[5,8,128]{2,1,0:T(8,128)S(1)}, f32[5,8,128]{2,1,0:T(8,128)S(1)}, u32[]{:S(2)}, u32[]{:S(2)}) collective-permute-start(f32[5,8,128]{2,1,0:T(8,128)S(1)} %get-tuple-element.24), channel_id=1, source_target_pairs={{0,16},{1,17},{2,18},{3,19},{4,20},{5,21},{6,22},{7,23},{8,24},{9,... | collective-permute-start | bytes 61448 | tf_op jit(solution)/shard_map/halo_x/ppermute | solution.py:79
  6.7 4.7 %collective-permute-start.1 = (f32[23,8,128]{2,1,0:T(8,128)S(1)}, f32[23,8,128]{2,1,0:T(8,128)S(1)}, u32[]{:S(2)}, u32[]{:S(2)}) collective-permute-start(f32[23,8,128]{2,1,0:T(8,128)S(1)} %get-tuple-element.27), channel_id=1, source_target_pairs={{0,4},{1,5},{2,6},{3,7},{4,0},{5,1},{6,2},{7,3},{8,12},{9,13},{10,... | collective-permute-start | bytes 282632 | tf_op jit(solution)/shard_map/halo_y/ppermute | solution.py:79
  8.8 2.6 %collective-permute-start.2 = (f32[23,8,128]{2,1,0:T(8,128)S(1)}, f32[23,8,128]{2,1,0:T(8,128)S(1)}, u32[]{:S(2)}, u32[]{:S(2)}) collective-permute-start(f32[23,8,128]{2,1,0:T(8,128)S(1)} %get-tuple-element.28), channel_id=1, source_target_pairs={{0,1},{1,0},{2,3},{3,2},{4,8},{5,9},{6,10},{7,11},{8,4},{9,5},{10,... | collective-permute-start | bytes 282632 | tf_op jit(solution)/shard_map/halo_y/ppermute | solution.py:79
  11.5 3.2 %collective-permute-start.3 = (f32[34,8,128]{2,1,0:T(8,128)S(1)}, f32[34,8,128]{2,1,0:T(8,128)S(1)}, u32[]{:S(2)}, u32[]{:S(2)}) collective-permute-start(f32[34,8,128]{2,1,0:T(8,128)S(1)} %get-tuple-element.31), channel_id=1, source_target_pairs={{0,1},{1,0},{2,3},{3,2},{4,5},{5,4},{6,7},{7,6},{8,9},{9,8},{10,11... | collective-permute-start | bytes 417800 | tf_op jit(solution)/shard_map/halo_z/ppermute | solution.py:79
  11.8 5.1 %collective-permute-start.4 = (f32[34,8,128]{2,1,0:T(8,128)S(1)}, f32[34,8,128]{2,1,0:T(8,128)S(1)}, u32[]{:S(2)}, u32[]{:S(2)}) collective-permute-start(f32[34,8,128]{2,1,0:T(8,128)S(1)} %get-tuple-element.32), channel_id=1, source_target_pairs={{0,16},{1,2},{2,1},{3,19},{4,20},{5,6},{6,5},{7,23},{8,24},{9,10},... | collective-permute-start | bytes 417800 | tf_op jit(solution)/shard_map/halo_z/ppermute | solution.py:79
  19.3 1.2 %collective-permute-start.5 = (f32[56,128]{1,0:T(8,128)S(1)}, f32[56,128]{1,0:T(8,128)S(1)}, u32[]{:S(2)}, u32[]{:S(2)}) collective-permute-start(f32[56,128]{1,0:T(8,128)S(1)} %get-tuple-element.35), channel_id=1, source_target_pairs={{0,1},{1,0},{2,3},{3,2},{4,5},{5,4},{6,7},{7,6},{8,9},{9,8},{10,11... | collective-permute-start | bytes 86024 | tf_op jit(solution)/shard_map/sum_over_devices/ppermute | solution.py:491
  20.6 4.8 %collective-permute-start.8 = (f32[56,128]{1,0:T(8,128)S(1)}, f32[56,128]{1,0:T(8,128)S(1)}, u32[]{:S(2)}, u32[]{:S(2)}) collective-permute-start(f32[56,128]{1,0:T(8,128)S(1)} %add.12), channel_id=1, source_target_pairs={{0,18},{1,19},{2,16},{3,17},{4,22},{5,23},{6,20},{7,21},{8,26},{9,... | collective-permute-start | bytes 86024 | tf_op jit(solution)/shard_map/sum_over_devices/ppermute | solution.py:491
  22.7 3.5 %collective-permute-start.7 = (f32[56,128]{1,0:T(8,128)S(1)}, f32[56,128]{1,0:T(8,128)S(1)}, u32[]{:S(2)}, u32[]{:S(2)}) collective-permute-start(f32[56,128]{1,0:T(8,128)S(1)} %add.12), channel_id=1, source_target_pairs={{0,17},{1,16},{2,19},{3,18},{4,21},{5,20},{6,23},{7,22},{8,25},{9,... | collective-permute-start | bytes 86024 | tf_op jit(solution)/shard_map/sum_over_devices/ppermute | solution.py:491
  22.7 3.5 %collective-permute-start.6 = (f32[56,128]{1,0:T(8,128)S(1)}, f32[56,128]{1,0:T(8,128)S(1)}, u32[]{:S(2)}, u32[]{:S(2)}) collective-permute-start(f32[56,128]{1,0:T(8,128)S(1)} %add.12), channel_id=1, source_target_pairs={{0,3},{1,2},{2,1},{3,0},{4,7},{5,6},{6,5},{7,4},{8,11},{9,10},{10,... | collective-permute-start | bytes 86024 | tf_op jit(solution)/shard_map/sum_over_devices/ppermute | solution.py:491
  26.2 5.2 %collective-permute-start.11 = (f32[56,128]{1,0:T(8,128)S(1)}, f32[56,128]{1,0:T(8,128)S(1)}, u32[]{:S(2)}, u32[]{:S(2)}) collective-permute-start(f32[56,128]{1,0:T(8,128)S(1)} %add_add_fusion.refs_0_), channel_id=1, source_target_pairs={{0,13},{1,12},{2,15},{3,14},{4,9},{5,8},{6,11},{7,10},{8,5},{9,4},... | collective-permute-start | bytes 86024 | tf_op jit(solution)/shard_map/sum_over_devices/ppermute | solution.py:491
  29.9 4.2 %collective-permute-start.10 = (f32[56,128]{1,0:T(8,128)S(1)}, f32[56,128]{1,0:T(8,128)S(1)}, u32[]{:S(2)}, u32[]{:S(2)}) collective-permute-start(f32[56,128]{1,0:T(8,128)S(1)} %add_add_fusion.refs_0_), channel_id=1, source_target_pairs={{0,9},{1,8},{2,11},{3,10},{4,13},{5,12},{6,15},{7,14},{8,1},{9,0},... | collective-permute-start | bytes 86024 | tf_op jit(solution)/shard_map/sum_over_devices/ppermute | solution.py:491
  30.5 4.2 %collective-permute-start.9 = (f32[56,128]{1,0:T(8,128)S(1)}, f32[56,128]{1,0:T(8,128)S(1)}, u32[]{:S(2)}, u32[]{:S(2)}) collective-permute-start(f32[56,128]{1,0:T(8,128)S(1)} %add_add_fusion.refs_0_), channel_id=1, source_target_pairs={{0,4},{1,5},{2,6},{3,7},{4,0},{5,1},{6,2},{7,3},{8,12},{9,13},{10,... | collective-permute-start | bytes 86024 | tf_op jit(solution)/shard_map/sum_over_devices/ppermute | solution.py:491

commit v4 on v3

v4 whole, which is shorter than its diff:
```python
import functools
import itertools

import jax
import jax.numpy as jnp
from jax import lax
from jax.experimental import pallas as pl
from jax.experimental.pallas import tpu as pltpu
from jax.sharding import PartitionSpec as P

STEPS = 4
F32 = jnp.float32
BF16 = jnp.bfloat16
AXES = ("gx", "gy", "gz")
HIGHEST = lax.Precision.HIGHEST
Z, Y, X = 8, 8, 128
CELLS = Z * Y
PIECE = 16
SLOTS = 16
BPAD = 32
BROWS = 24
HPAD = 64
ROWS = 56


def roll(tile, shift, axis):
    shift %= tile.shape[axis]
    return pltpu.roll(tile, shift, axis) if shift else tile


def iotas():
    return (
        lax.broadcasted_iota(jnp.int32, (Y, X), 0),
        lax.broadcasted_iota(jnp.int32, (Y, X), 1),
    )


def is_even(axis):
    return lax.rem(lax.axis_index(axis), 2) == 0


def facing(axis, count, received):
    index = lax.axis_index(axis)
    even = lax.rem(index, 2) == 0
    low_there, high_there = index > 0, index < count - 1

    def pick(k):
        first = received[0][k]
        if len(received) == 1:
            return jnp.where(even, 0.0, first), jnp.where(even, first, 0.0)
        second = received[1][k]
        low = jnp.where(low_there, jnp.where(even, second, first), 0.0)
        high = jnp.where(high_there, jnp.where(even, first, second), 0.0)
        return low, high

    return pick


def swaps(arrays, sizes, axis):
    first, second = [], []
    dimension = AXES.index(axis)
    aside = 0 if dimension == 2 else 2
    for place in itertools.product(*map(range, sizes)):
        at = place[dimension]

        def pair(dimension, to):
            other = place[:dimension] + (to,) + place[dimension + 1 :]
            return tuple(
                (p[0] * sizes[1] + p[1]) * sizes[2] + p[2] for p in (place, other)
            )

        first.append(pair(dimension, at ^ 1))
        beyond = at + 1 if at % 2 else at - 1
        if 0 <= beyond < sizes[dimension]:
            second.append(pair(dimension, beyond))
        else:
            second.append(pair(aside, place[aside] ^ 1))
    return [lax.ppermute(a, AXES, pairs) for a, pairs in zip(arrays, (first, second))]


def choose(right, there, here):
    return (there if right else here) if isinstance(right, bool) else jnp.where(right, there, here)


def turn(tile, right, there, here):
    if isinstance(right, bool):
        return roll(tile, there if right else here, 1)
    return pltpu.roll(tile, jnp.where(right, there % X, here % X), 1)


def ends_of(count):
    return [is_even("gx")] if count == 2 else [False, True]


def pack_y(fields, start_there, diagonal_there, start, diagonal, *refs):
    sends, done = refs[:-1], refs[-1]
    copies = [
        pltpu.make_async_copy(start_there, start, done.at[0]),
        pltpu.make_async_copy(diagonal_there, diagonal, done.at[1]),
    ]
    for copy in copies:
        copy.start()
    for copy in copies:
        copy.wait()
    row, _ = iotas()
    even = is_even("gy")
    for f in range(fields + 1):
        for p in range(4):
            one, two = (start[f, z] if f < fields else diagonal[z] for z in (p, p + 4))
            to_high = jnp.where(row < 4, roll(one, 4, 0), two)
            to_low = jnp.where(row < 4, one, roll(two, 4, 0))
            sends[0][4 * f + p] = jnp.where(even, to_high, to_low)
            if len(sends) > 1:
                sends[1][4 * f + p] = jnp.where(even, to_low, to_high)


def pack_z(fields, count, ways, start, diagonal, _, *refs):
    received, (beyond, *sends) = refs[:ways], refs[ways:]
    row, _ = iotas()
    pick = facing("gy", count, received)
    even = is_even("gz")
    for f in range(fields + 1):
        for p in range(4):
            low, high = pick(4 * f + p)
            beyond[f, p] = jnp.where(row < 4, high, roll(low, 4, 0))
            beyond[f, p + 4] = jnp.where(row < 4, roll(high, 4, 0), low)
    inner = (row == 2) | (row == 3)
    for which, ref in enumerate(sends):
        up = even if which == 0 else jnp.logical_not(even)
        at = [None] + [jnp.where(up, Z - d, d - 1) for d in range(1, 5)]
        k = 0
        for f in range(fields):
            for d in range(1, 5):
                ref[k] = start[f, at[d]]
                k += 1
            ref[k] = beyond[f, at[1]]
            ref[k + 1] = jnp.where(inner, roll(beyond[f, at[3]], 3, 0), beyond[f, at[2]])
            k += 2
        for d in range(1, 4):
            ref[k] = diagonal[at[d]]
            k += 1
        ref[k] = jnp.where(inner, roll(beyond[fields, at[2]], 3, 0), beyond[fields, at[1]])


def z_tiles(fields):
    return 6 * fields + 4


def known(fields, f):
    depth = 4 if f < fields else 3
    for at in range(-depth, Z + depth):
        distance = max(-at, at - Z + 1, 0)
        for part in range(2 if distance < depth else 1):
            yield at % SLOTS, part


def pack_x(fields, count, ways, start, diagonal, _, beyond, *refs):
    received, (wide, *sends) = refs[:ways], refs[ways:]
    _, lane = iotas()
    pick = facing("gz", count, received)
    even = is_even("gx")
    k = 0
    for f in range(fields + 1):
        depth = 4 if f < fields else 3
        for z in range(Z):
            wide[f, z, 0] = start[f, z] if f < fields else diagonal[z]
            wide[f, z, 1] = beyond[f, z]
        for d in range(1, depth + 1):
            wide[f, SLOTS - d, 0], wide[f, Z - 1 + d, 0] = pick(k)
            k += 1
        if f < fields:
            wide[f, SLOTS - 1, 1], wide[f, Z, 1] = pick(k)
            k += 1
        low, high = pick(k)
        k += 1
        wide[f, SLOTS - depth + 2, 1], wide[f, Z + depth - 3, 1] = low, high
        wide[f, SLOTS - depth + 1, 1], wide[f, Z + depth - 2, 1] = roll(low, -3, 0), roll(high, -3, 0)
    for which, ref in enumerate(sends):
        up = even if which == 0 else jnp.logical_not(even)
        for k in range(x_tiles(fields)):
            ref[k] = jnp.zeros((Y, X), F32)
        for f in range(fields + 1):
            for z, part in known(fields, f):
                index, column = divmod(2 * f + part, 4)
                base = 16 * (z % 8) + 4 * column
                moved = turn(wide[f, z, part], up, base + 4, base)
                k = 2 * index + z // 8
                ref[k] = jnp.where((lane >= base) & (lane < base + 4), moved, ref[k])


def x_tiles(fields):
    return 2 * ((2 * (fields + 1) + 3) // 4)


def coefficients(d):
    inside = d > 0.0
    return jnp.where(inside, (d - 1.0) * (1.0 / 7.0), 0.0), jnp.where(inside, 1.0 / 7.0, 0.0)


def beside_y(mine, other):
    row, _ = iotas()
    above, above_other = roll(mine, -1, 0), roll(other, -1, 0)
    below, below_other = roll(mine, 1, 0), roll(other, 1, 0)
    last, first = row == Y - 1, row == 0
    return (
        jnp.where(last, above_other, above) + jnp.where(first, below_other, below),
        jnp.where(last, above, above_other) + jnp.where(first, below, below_other),
    )


def powers(fields, count, wide, history_split, history_gram, center, own, sums, *refs):
    halo, coef_a, coef_b, split = refs
    columns = fields * (STEPS + 1)
    _, lane = iotas()
    inside = set(range(Z))
    ends = ends_of(count)

    for z, part in known(fields, fields):
        if part == 0 and z in inside:
            coef_a[z, 0] = (wide[fields, z, 0] - 1.0) * (1.0 / 7.0)
        else:
            coef_a[z, part], coef_b[z, part] = coefficients(wide[fields, z, part])

    def read(level, f, z, part):
        if level == 0:
            return wide[f, z, part]
        if part == 0 and z in inside:
            return center[pl.ds((fields * level + f) * CELLS + z * Y, Y), :]
        return halo[level - 1, f, z, part]

    for f in range(fields):
        for z in range(Z):
            center[pl.ds(f * CELLS + z * Y, Y), :] = wide[f, z, 0]
    for level in range(1, STEPS + 1):
        reach = STEPS - level
        for f in range(fields):
            for at in range(-reach, Z + reach):
                z, before, after = at % SLOTS, (at - 1) % SLOTS, (at + 1) % SLOTS
                distance = max(-at, at - Z + 1, 0)
                tiles = [read(level - 1, f, z, p) for p in range(2)]
                along_y = beside_y(*tiles)
                for part in range(2 if distance < reach else 1):
                    tile = tiles[part]
                    total = jnp.where(lane == 0, 0.0, roll(tile, 1, 1))
                    total = total + jnp.where(lane == X - 1, 0.0, roll(tile, -1, 1))
                    total = total + along_y[part]
                    total = total + read(level - 1, f, before, part)
                    total = total + read(level - 1, f, after, part)
                    own_cells = part == 0 and z in inside
                    b = 1.0 / 7.0 if own_cells else coef_b[z, part]
                    value = coef_a[z, part] * tile - b * total
                    if level > 1:
                        value = value + value - read(level - 2, f, z, part)
                    if own_cells:
                        center[pl.ds((fields * level + f) * CELLS + z * Y, Y), :] = value
                    else:
                        halo[level - 1, f, z, part] = value
    center[pl.ds(columns * CELLS, (BROWS - columns) * CELLS), :] = jnp.zeros(
        ((BROWS - columns) * CELLS, X), F32
    )

    lanes = lax.broadcasted_iota(jnp.int32, (BROWS, X), 1)
    taken = [(lanes >= first) & (lanes < first + 4) for first in (choose(r, X - 4, 0) for r in ends)]
    for cell in range(CELLS):
        rows = center[pl.ds(cell, BROWS, stride=CELLS), :]
        for mask in taken:
            rows = jnp.where(mask, 0.0, rows)
        high, low = split_rows(rows, BPAD)
        split[0:BPAD, cell * X : (cell + 1) * X] = high
        split[BPAD : 2 * BPAD, cell * X : (cell + 1) * X] = low
    write_sums(sums, split[...], history_split[...])
    sums[:, 0:HPAD] = history_gram[0:ROWS]

    for e, right in enumerate(ends):
        for f in range(fields + 1):
            tiles = [[jnp.zeros((Y, X), F32)] * 2 for _ in range(2)]
            for z, part in known(fields, f):
                base = 16 * (z % 8)
                first = choose(right, base, base + 4)
                moved = turn(wide[f, z, part], right, base + 8, base + 4)
                tiles[part][z // 8] = jnp.where(
                    (lane >= first) & (lane < first + 8), moved, tiles[part][z // 8]
                )
            for part in range(2):
                for t in range(2):
                    own[e, f, part, t] = tiles[part][t]


def write_sums(sums, split, history_split):
    basis = join_lanes(join(product(split, split), BPAD), BPAD)
    cross = join_lanes(join(product(split, history_split), BPAD), HPAD)
    sums[0:BROWS, HPAD:] = cross[:BROWS]
    sums[BROWS : 2 * BROWS, HPAD : HPAD + BPAD] = basis[:BROWS]
    sums[BROWS : 2 * BROWS, HPAD + BPAD :] = jnp.zeros((BROWS, X - HPAD - BPAD), F32)
    sums[2 * BROWS :, HPAD:] = jnp.zeros((ROWS - 2 * BROWS, X - HPAD), F32)


def powers_at_ends(fields, count, ways, own, history_ends, before, *refs):
    received, (sums, patch, work, split) = refs[:ways], refs[ways:]
    columns = fields * (STEPS + 1)
    _, lane = iotas()
    column = lane & 15
    pick = facing("gx", count, received) if count > 2 else None
    ends = ends_of(count)
    taken = (column >= 4) & (column < 8)

    for e, right in enumerate(ends):

        def halo_of(k):
            return received[0][k] if count == 2 else pick(k)[e]

        first = choose(right, 8, 0)
        from_halo = (column >= first) & (column < first + 4)
        coefs = {}
        for f in range(fields + 1):
            for part in range(2):
                index, c = divmod(2 * f + part, 4)
                for t in range(2):
                    moved = turn(halo_of(2 * index + t), right, 8 - 4 * c, -4 * c)
                    tile = jnp.where(from_halo, moved, own[e, f, part, t])
                    if f < fields:
                        work[0, f, part, t] = tile
                    else:
                        coefs[part, t] = coefficients(tile)
        for level in range(1, STEPS + 1):
            for f in range(fields):
                tiles = [[work[level - 1, f, p, t] for t in range(2)] for p in range(2)]
                along_y = [beside_y(tiles[0][t], tiles[1][t]) for t in range(2)]
                for part, t in ((0, 0), (0, 1), (1, 0), (1, 1)):
                    if (level == STEPS and (part or t)) or (level == STEPS - 1 and part and t):
                        continue
                    tile = tiles[part][t]
                    nexts = [roll(tiles[part][i], -16, 1) for i in (t, 1 - t)]
                    lasts = [roll(tiles[part][i], 16, 1) for i in (t, 1 - t)]
                    total = roll(tile, 1, 1) + roll(tile, -1, 1) + along_y[t][part]
                    total = total + jnp.where(lane >= X - 16, nexts[1], nexts[0])
                    total = total + jnp.where(lane < 16, lasts[1], lasts[0])
                    a, b = coefs[part, t]
                    value = a * tile - b * total
                    if level > 1:
                        value = value + value - work[level - 2, f, part, t]
                    work[level, f, part, t] = value
        for level in range(STEPS + 1):
            for f in range(fields):
                k = fields * level + f
                patch[e, k * Y : (k + 1) * Y, :] = jnp.where(taken, work[level, f, 0, 0], 0.0)
        patch[e, columns * Y :, :] = jnp.zeros(((BROWS - columns) * Y, X), F32)
        for y in range(Y):
            high, low = split_rows(patch[e, pl.ds(y, BROWS, stride=Y), :], BPAD)
            at = (e * Y + y) * X
            split[0:BPAD, at : at + X] = high
            split[BPAD : 2 * BPAD, at : at + X] = low
    write_sums(sums, split[...], history_ends[...])
    sums[:, 0:HPAD] = before[:, 0:HPAD]
    sums[:, HPAD:] = sums[:, HPAD:] + before[:, HPAD:]


def patch_and_split(fields, count, center, patch, split, whole):
    _, lane = iotas()
    for k in range(BROWS):
        for z in range(Z):
            tile = center[pl.ds(k * CELLS + z * Y, Y), :]
            if fields <= k < fields * (STEPS + 1):
                for e, right in enumerate(ends_of(count)):
                    base = 16 * z + 4
                    moved = turn(patch[e, k * Y : (k + 1) * Y, :], right, X - 4 - base, -base)
                    first = choose(right, X - 4, 0)
                    tile = jnp.where((lane >= first) & (lane < first + 4), moved, tile)
            whole[pl.ds(k * CELLS + z * Y, Y), :] = tile
    for cell in range(CELLS):
        high, low = split_rows(whole[pl.ds(cell, BROWS, stride=CELLS), :], BPAD)
        split[0:BPAD, cell * X : (cell + 1) * X] = high
        split[BPAD : 2 * BPAD, cell * X : (cell + 1) * X] = low


def split_rows(rows, padded):
    rows = jnp.concatenate([rows, jnp.zeros((padded - rows.shape[0], rows.shape[1]), F32)], axis=0)
    high = rows.astype(BF16)
    return high, (rows - high.astype(F32)).astype(BF16)


def product(left, right):
    return lax.dot_general(left, right, (((1,), (1,)), ((), ())), preferred_element_type=F32)


def join(both, padded):
    return both[:padded] + both[padded:]


def join_lanes(both, padded):
    return both[:, :padded] + both[:, padded:]


def load_history(history, here, done):
    copy = pltpu.make_async_copy(history, here, done)
    copy.start()
    copy.wait()


def pack_history(count, ends_count, history, split, packed):
    _, lane = iotas()
    for e, right in enumerate(ends_of(ends_count)):
        for h in range(count):
            tile = jnp.zeros((Y, X), F32)
            for z in range(Z):
                base = 16 * z + 4
                moved = turn(history[pl.ds(h * CELLS + z * Y, Y), :], right, base + 4, base)
                tile = jnp.where((lane >= base) & (lane < base + 4), moved, tile)
            packed[pl.ds(h * Y, Y), :] = tile
        for y in range(Y):
            high, low = split_rows(packed[pl.ds(y, count, stride=Y), :], HPAD)
            at = (e * Y + y) * X
            split[0:HPAD, at : at + X] = high
            split[HPAD : 2 * HPAD, at : at + X] = low


def history_kernel(count, history, split, gram):
    for cell in range(CELLS):
        high, low = split_rows(history[pl.ds(cell, count, stride=CELLS), :], HPAD)
        split[0:HPAD, cell * X : (cell + 1) * X] = high
        split[HPAD : 2 * HPAD, cell * X : (cell + 1) * X] = low
    gram[...] = join_lanes(join(product(split[...], split[...]), HPAD), HPAD)


def split_matrix(matrix):
    high = matrix.astype(BF16)
    return high, (matrix - high.astype(F32)).astype(BF16)


def reciprocal(value):
    guess = pl.reciprocal(value, approx=True)
    guess = guess * (2.0 - value * guess)
    return guess * (2.0 - value * guess)


def finish(columns, cells, history_split, split, *refs):
    parts, (out, factor, staged, factor_staged, done) = refs[:-5], refs[-5:]
    total = (parts[0][...] + parts[1][...]) + (parts[2][...] + parts[3][...])
    total = total * (1.0 / cells)
    history_gram = jnp.concatenate([total[:, 0:HPAD], jnp.zeros((HPAD - ROWS, HPAD), F32)], axis=0)
    coef = total[0:BROWS, HPAD:]
    basis_gram = total[BROWS : 2 * BROWS, HPAD : HPAD + BPAD]
    inner = jnp.dot(coef, history_gram, precision=HIGHEST, preferred_element_type=F32) - 2.0 * coef
    inner = jnp.concatenate([inner, jnp.zeros((BPAD - BROWS, HPAD), F32)], axis=0)
    gram = basis_gram + lax.dot_general(
        coef, inner, (((1,), (1,)), ((), ())), precision=HIGHEST, preferred_element_type=F32
    )
    row = lax.broadcasted_iota(jnp.int32, (BROWS, X), 0)
    lane = lax.broadcasted_iota(jnp.int32, (BROWS, X), 1)
    work = jnp.concatenate([gram, jnp.zeros((BROWS, X - BPAD - HPAD), F32), coef], axis=1)
    work = jnp.where(lane == row + BPAD, 1.0, work)
    panel = columns
    for start in range(0, columns, panel):
        spread = [
            jnp.broadcast_to(work[:, k : k + 1], (BROWS, X)) for k in range(start, start + panel)
        ]
        for j in range(panel):
            k = start + j
            scale = spread[j] * reciprocal(spread[j][k : k + 1, :])
            scale = jnp.where(row > k, scale, 0.0)
            for later in range(j + 1, panel):
                spread[later] = spread[later] - scale * spread[later][k : k + 1, :]
            work = work - scale * work[k : k + 1, :]
    pivots = jnp.sum(jnp.where(lane == row, work, 0.0), axis=1, keepdims=True)
    good = lax.broadcasted_iota(jnp.int32, (BROWS, 1), 0) < columns
    work = work * jnp.where(good, 1.0 / jnp.sqrt(jnp.where(good, pivots, 1.0)), 0.0)
    factor_staged[...] = jnp.where(lane >= row, work, 0.0)[0:columns, 0:columns]
    copies = [pltpu.make_async_copy(factor_staged, factor, done.at[0])]
    copies[0].start()
    work = jnp.concatenate([work, jnp.zeros((BPAD - BROWS, X), F32)], axis=0)
    history_high, history_low = split_matrix(-work[:, X - HPAD :])
    basis_high, basis_low = split_matrix(work[:, BPAD : 2 * BPAD])
    left = jnp.concatenate(
        [
            jnp.concatenate([history_high, history_high, basis_high, basis_high], axis=1),
            jnp.concatenate(
                [history_low, jnp.zeros_like(history_low), basis_low, jnp.zeros_like(basis_low)], axis=1
            ),
        ],
        axis=0,
    )
    width = 4 * X
    inside = width // X
    blocks = staged.reshape(columns, CELLS, X)
    for c in range(CELLS // inside):
        right = jnp.concatenate(
            [
                history_split[:, c * width : (c + 1) * width],
                split[:, c * width : (c + 1) * width],
            ],
            axis=0,
        )
        result = join(jnp.dot(left, right, preferred_element_type=F32), BPAD)
        for j in range(inside):
            staged[pl.ds(c * inside + j, columns, stride=CELLS), :] = result[
                0:columns, j * X : (j + 1) * X
            ]
        cells_done = (c + 1) * inside
        if cells_done % PIECE == 0:
            piece = pl.ds(cells_done - PIECE, PIECE)
            copies.append(
                pltpu.make_async_copy(
                    blocks.at[:, piece, :], out.at[:, piece, :], done.at[len(copies)]
                )
            )
            copies[-1].start()
    for copy in copies:
        copy.wait()


def call(
    kernel,
    outs,
    flops,
    bytes_accessed,
    scratch=(),
    limit=40 * 1024 * 1024,
    place=jax.ShapeDtypeStruct,
    **specs,
):
    return pl.pallas_call(
        kernel,
        **specs,
        out_shape=[place(shape, dtype) for shape, dtype in outs],
        scratch_shapes=list(scratch),
        compiler_params=pltpu.CompilerParams(vmem_limit_bytes=limit),
        cost_estimate=pl.CostEstimate(flops=flops, bytes_accessed=bytes_accessed, transcendentals=0),
    )


def exchange_sums(array, sizes, flips):
    devices = range(sizes[0] * sizes[1] * sizes[2])
    return [array] + [lax.ppermute(array, AXES, [(i, i ^ flip) for i in devices]) for flip in flips]


def on_device(sizes, history, start, diagonal):
    fields, history_count = start.shape[0], history.shape[0]
    columns = fields * (STEPS + 1)
    all_fields = fields + 1
    count = dict(zip(AXES, sizes))
    ways = {axis: 1 if size == 2 else 2 for axis, size in count.items()}
    cells = Z * Y * X * sizes[0] * sizes[1] * sizes[2]
    tile = Y * X * 4

    ends = 1 if count["gx"] == 2 else 2
    there = pl.BlockSpec(memory_space=pltpu.HBM)
    anywhere = pl.BlockSpec(memory_space=pl.ANY)
    here = pl.BlockSpec(memory_space=pltpu.VMEM)

    with jax.named_scope("halo_y"):
        start, diagonal, *sends = call(
            functools.partial(pack_y, fields),
            [(start.shape, F32), (diagonal.shape, F32)]
            + [((4 * all_fields, Y, X), F32)] * ways["gy"],
            1000,
            start.size * 4,
            [pltpu.SemaphoreType.DMA((2,))],
            None,
            pltpu.VMEM,
            in_specs=[there, there],
        )(start, diagonal)
        received = swaps(sends, sizes, "gy")
    with jax.named_scope("load_history"):
        rows = call(
            load_history,
            [(history.shape, F32)],
            1000,
            history.size * 4,
            [pltpu.SemaphoreType.DMA],
            None,
            pltpu.VMEM,
            in_specs=[there],
        )(history)[0].reshape(history_count * CELLS, X)
    with jax.named_scope("history_at_ends"):
        history_ends = call(
            functools.partial(pack_history, history_count, count["gx"]),
            [((2 * HPAD, ends * Y * X), BF16)],
            1000,
            history.size * 2,
            [pltpu.VMEM((history_count * Y, X), F32)],
        )(rows)[0]
    with jax.named_scope("halo_z"):
        beyond, *sends = call(
            functools.partial(pack_z, fields, count["gy"], ways["gy"]),
            [((all_fields, Z, Y, X), F32)] + [((z_tiles(fields), Y, X), F32)] * ways["gz"],
            1000,
            start.size * 4,
            in_specs=[here, here, anywhere] + [here] * ways["gy"],
        )(start, diagonal, history_ends, *received)
        received = swaps(sends, sizes, "gz")
    with jax.named_scope("history_products"):
        history_split, history_gram = call(
            functools.partial(history_kernel, history_count),
            [((2 * HPAD, CELLS * X), BF16), ((HPAD, HPAD), F32)],
            2 * 128 * 128 * CELLS * X,
            history.size * 4,
        )(rows)
    with jax.named_scope("halo_x"):
        wide, *sends = call(
            functools.partial(pack_x, fields, count["gz"], ways["gz"]),
            [((all_fields, SLOTS, 2, Y, X), F32)]
            + [((x_tiles(fields), Y, X), F32)] * ways["gx"],
            1000,
            start.size * 4,
            in_specs=[here, here, anywhere, here] + [here] * ways["gz"],
        )(start, diagonal, history_gram, beyond, *received)
        received = swaps(sends, sizes, "gx")
    with jax.named_scope("matrix_powers"):
        center, own, sums = call(
            functools.partial(powers, fields, count["gx"]),
            [
                ((BROWS * CELLS, X), F32),
                ((ends, all_fields, 2, 2, Y, X), F32),
                ((ROWS, X), F32),
            ],
            2 * 192 * 64 * CELLS * X,
            start.size * 4,
            [
                pltpu.VMEM((STEPS - 1, fields, SLOTS, 2, Y, X), F32),
                pltpu.VMEM((SLOTS, 2, Y, X), F32),
                pltpu.VMEM((SLOTS, 2, Y, X), F32),
                pltpu.VMEM((2 * BPAD, CELLS * X), BF16),
            ],
        )(wide, history_split, history_gram)
    with jax.named_scope("powers_at_ends"):
        sums, patch = call(
            functools.partial(powers_at_ends, fields, count["gx"], ways["gx"]),
            [((ROWS, X), F32), ((ends, BROWS * Y, X), F32)],
            1000000,
            start.size * 4,
            [
                pltpu.VMEM((STEPS + 1, fields, 2, 2, Y, X), F32),
                pltpu.VMEM((2 * BPAD, ends * Y * X), BF16),
            ],
        )(own, history_ends, sums, *received)
    with jax.named_scope("whole_basis"):
        split = call(
            functools.partial(patch_and_split, fields, count["gx"]),
            [((2 * BPAD, CELLS * X), BF16)],
            1000,
            columns * CELLS * X * 4,
            [pltpu.VMEM((BROWS * CELLS, X), F32)],
        )(center, patch)[0]
    with jax.named_scope("sum_over_devices"):
        bits = []
        for axis, stride in (("gz", 1), ("gx", sizes[1] * sizes[2]), ("gy", sizes[2])):
            bits += [stride << b for b in range(count[axis].bit_length() - 1)]
        alone = 1 + (len(bits) - 1) % 2
        for bit in bits[:alone]:
            pair = exchange_sums(sums, sizes, [bit])
            sums = pair[0] + pair[1]
        for k in range(alone, len(bits), 2):
            if k > alone:
                sums = (parts[0] + parts[1]) + (parts[2] + parts[3])
            one, two = bits[k : k + 2]
            flips = [one, two ^ 1, one ^ two ^ 1] if k + 2 == len(bits) else [one ^ 1, two ^ 1, one ^ two]
            parts = exchange_sums(sums, sizes, flips)
    with jax.named_scope("orthonormalize"):
        out, factor = call(
            functools.partial(finish, columns, cells),
            [((columns, CELLS, X), F32), ((columns, columns), F32)],
            2 * 192 * 64 * CELLS * X,
            columns * CELLS * X * 4,
            [
                pltpu.VMEM((columns * CELLS, X), F32),
                pltpu.VMEM((columns, columns), F32),
                pltpu.SemaphoreType.DMA((CELLS // PIECE + 1,)),
            ],
            out_specs=[pl.BlockSpec(memory_space=pltpu.HBM)] * 2,
        )(history_split, split, *parts)
    return out.reshape(columns, Z, Y, X), factor


def solution(mesh):
    sizes = tuple(mesh.shape[axis] for axis in AXES)
    return jax.shard_map(
        functools.partial(on_device, sizes),
        mesh=mesh,
        in_specs=(P(None, "gz", "gy", "gx"), P(None, "gz", "gy", "gx"), P("gz", "gy", "gx")),
        out_specs=(P(None, "gz", "gy", "gx"), P()),
        check_vma=False,
    )
```

time: 37.6 us -> 36.8 us (0.979)
  waiting for transfers between devices: 10.3 us -> 8.88 us
  Pallas kernels: 11 us -> 11.7 us
    ppermute x5, waiting for transfers between devices: 3.02 us -> 1.37 us  [swaps(): lax.ppermute(a, AXES, pairs)]
    pallas_call x7 -> x8, Pallas kernels: 8.22 us -> 9 us  [the longest x1 2.16 us: on_device(): call(functools.partial(powers, fields, count['gx']), [((BROWS * CELLS, X)...]
  transfers between devices with their start and end apart: 12 -> 12, of which waited for: 9 -> 7; matrix products, arithmetic and copies ran while one was open for 0% -> 0% of each run, Pallas kernels for 12% -> 19%
where the time goes in v4:
time: 36.8 us; the launch traced here: 36.4 us
  starting transfers between devices  15 us (41%)
  Pallas kernels  11.7 us (32%)
  waiting for transfers between devices  8.88 us (24%)
  between operations  0.73 us (2%)
    ppermute x7, starting transfers between devices, exchange_sums(): lax.ppermute(array, AXES, [(i, i ^ flip) for i in devices])  7.93 us
    ppermute x7, waiting for transfers between devices, exchange_sums(): lax.ppermute(array, AXES, [(i, i ^ flip) for i in devices])  7.51 us
    ppermute x5, starting transfers between devices, swaps(): lax.ppermute(a, AXES, pairs)  7.07 us
    pallas_call x1, Pallas kernels, on_device(): call(functools.partial(finish, columns, cells), [((columns, CELLS, X), F3...  2.67 us
    pallas_call x1, Pallas kernels, on_device(): call(functools.partial(powers, fields, count['gx']), [((BROWS * CELLS, X)...  2.16 us
    pallas_call x1, Pallas kernels, on_device(): call(functools.partial(history_kernel, history_count), [((2 * HPAD, CELLS...  1.93 us
    pallas_call x1, Pallas kernels, on_device(): call(load_history, [(history.shape, F32)], 1000, history.size * 4, [pltpu...  1.51 us
    ppermute x5, waiting for transfers between devices, swaps(): lax.ppermute(a, AXES, pairs)  1.37 us
  transfers between devices with their start and end apart: 12, of which 7 were waited for; matrix products, arithmetic and copies ran while one was open for 0% of the time, Pallas kernels for 19%

profile of v4, /device:TPU:0, one launch (start us, length us, event | category | flops | bytes accessed | tf_op | source)
XLA Modules:
  0.0 36.4 jit_solution(12151272762168852070)
XLA Ops:
  0.6 0.9 %halo_y.1 = (f32[4,8,8,128]{3,2,1,0:T(8,128)S(1)}, f32[8,8,128]{2,1,0:T(8,128)S(1)}, f32[20,8,128]{2,1,0:T(8,128)S(1)}, f32[20,8,128]{2,1,0:T(8,128)S(1)}) custom-call(f32[4,8,8,128]{3,2,1,0:T(8,128)} %start_there.1, f32[8,8,128]{2,1,0:T(8,128)} %diagonal_there.1), custom_call_target="tpu_custom_call" | custom-call | flops 1000 | bytes 131072 | tf_op jit(solution)/shard_map/halo_y/pallas_call | solution.py:551
  1.6 3.1 %collective-permute-start = (f32[20,8,128]{2,1,0:T(8,128)S(1)}, f32[20,8,128]{2,1,0:T(8,128)S(1)}, u32[]{:S(2)}, u32[]{:S(2)}) collective-permute-start(f32[20,8,128]{2,1,0:T(8,128)S(1)} %get-tuple-element.24), channel_id=1, source_target_pairs={{0,4},{1,5},{2,6},{3,7},{4,0},{5,1},{6,2},{7,3},{8,12},{9,13},{10,... | collective-permute-start | bytes 245768 | tf_op jit(solution)/shard_map/halo_y/ppermute | solution.py:78
  4.7 0.0 collective-permute-start.1
  4.7 1.5 %load_history.1 = f32[56,8,8,128]{3,2,1,0:T(8,128)S(1)} custom-call(f32[56,8,8,128]{3,2,1,0:T(8,128)} %history.1), custom_call_target="tpu_custom_call" | custom-call | flops 1000 | bytes 1835008 | tf_op jit(solution)/shard_map/load_history/pallas_call | solution.py:564
  6.2 0.6 %history_at_ends.1._.history_ends = bf16[128,1024]{1,0:T(8,128)(2,1)S(1)} custom-call(f32[3584,128]{1,0:T(8,128)S(1)} %bitcast.2), custom_call_target="tpu_custom_call" | custom-call | flops 1000 | bytes 917504 | tf_op jit(solution)/shard_map/history_at_ends/pallas_call | solution.py:575
  6.8 0.3 collective-permute-done.refs_0_
  7.1 0.0 collective-permute-done.1.refs_1_
  7.1 0.1 halo_z.1
  7.2 0.3 collective-permute-start.2
  7.4 1.8 %collective-permute-start.3 = (f32[28,8,128]{2,1,0:T(8,128)S(1)}, f32[28,8,128]{2,1,0:T(8,128)S(1)}, u32[]{:S(2)}, u32[]{:S(2)}) collective-permute-start(f32[28,8,128]{2,1,0:T(8,128)S(1)} %get-tuple-element.28), channel_id=1, source_target_pairs={{0,16},{1,2},{2,1},{3,19},{4,20},{5,6},{6,5},{7,23},{8,24},{9,10},... | collective-permute-start | bytes 344072 | tf_op jit(solution)/shard_map/halo_z/ppermute | solution.py:78
  9.3 1.9 %history_products.1 = (bf16[128,8192]{1,0:T(8,128)(2,1)S(1)}, f32[64,64]{1,0:T(8,128)S(1)}) custom-call(f32[3584,128]{1,0:T(8,128)S(1)} %bitcast.3), custom_call_target="tpu_custom_call" | custom-call | flops 268435456 | bytes 1835008 | tf_op jit(solution)/shard_map/history_products/pallas_call | solution.py:592
  11.2 1.0 %collective-permute-done.3.refs_1_ = f32[28,8,128]{2,1,0:T(8,128)S(1)} collective-permute-done((f32[28,8,128]{2,1,0:T(8,128)S(1)}, f32[28,8,128]{2,1,0:T(8,128)S(1)}, u32[]{:S(2)}, u32[]{:S(2)}) %collective-permute-start.3) | collective-permute-done | bytes 114720 | tf_op jit(solution)/shard_map/halo_z/ppermute | solution.py:78
  12.2 0.2 halo_x.1
  12.5 1.9 %collective-permute-start.4 = (f32[6,8,128]{2,1,0:T(8,128)S(1)}, f32[6,8,128]{2,1,0:T(8,128)S(1)}, u32[]{:S(2)}, u32[]{:S(2)}) collective-permute-start(f32[6,8,128]{2,1,0:T(8,128)S(1)} %get-tuple-element.33), channel_id=1, source_target_pairs={{0,16},{1,17},{2,18},{3,19},{4,20},{5,21},{6,22},{7,23},{8,24},{9,... | collective-permute-start | bytes 73736 | tf_op jit(solution)/shard_map/halo_x/ppermute | solution.py:78
  14.4 2.2 %matrix_powers.1 = (f32[1536,128]{1,0:T(8,128)S(1)}, f32[1,5,2,2,8,128]{5,4,3,2,1,0:T(8,128)S(1)}, f32[56,128]{1,0:T(8,128)S(1)}) custom-call(f32[5,16,2,8,128]{4,3,2,1,0:T(8,128)S(1)} %get-tuple-element.29.wide, bf16[128,8192]{1,0:T(8,128)(2,1)S(1)} %get-tuple-element.20.history_split, f32[64,64]{1,0:T(8,128)S(1)} %get-tuple-element.23._.history_gram), custom_call_target="tpu_custom_call" | custom-call | flops 201326592 | bytes 131072 | tf_op jit(solution)/shard_map/matrix_powers/pallas_call | solution.py:609
  16.5 0.9 %powers_at_ends.1 = (f32[56,128]{1,0:T(8,128)S(1)}, f32[1,192,128]{2,1,0:T(8,128)S(1)}) custom-call(f32[1,5,2,2,8,128]{5,4,3,2,1,0:T(8,128)S(1)} %get-tuple-element.31.own, bf16[128,1024]{1,0:T(8,128)(2,1)S(1)} %history_at_ends.1._.history_ends, f32[56,128]{1,0:T(8,128)S(1)} %get-tuple-element.32.before, f32[6,8,128]{2,1,0:T(8,128)S(1)} %collective-permute-done.4.refs_0_), custom_call_target="tpu_custom_call" | custom-call | flops 1000000 | bytes 131072 | tf_op jit(solution)/shard_map/powers_at_ends/pallas_call | solution.py:626
  17.4 0.1 collective-permute-start.5
  17.5 1.2 %collective-permute-done.5 = f32[56,128]{1,0:T(8,128)S(1)} collective-permute-done((f32[56,128]{1,0:T(8,128)S(1)}, f32[56,128]{1,0:T(8,128)S(1)}, u32[]{:S(2)}, u32[]{:S(2)}) %collective-permute-start.5) | collective-permute-done | bytes 28704 | tf_op jit(solution)/shard_map/sum_over_devices/ppermute | solution.py:533
  18.7 1.4 %collective-permute-start.7 = (f32[56,128]{1,0:T(8,128)S(1)}, f32[56,128]{1,0:T(8,128)S(1)}, u32[]{:S(2)}, u32[]{:S(2)}) collective-permute-start(f32[56,128]{1,0:T(8,128)S(1)} %add.12), channel_id=1, source_target_pairs={{0,17},{1,16},{2,19},{3,18},{4,21},{5,20},{6,23},{7,22},{8,25},{9,... | collective-permute-start | bytes 86024 | tf_op jit(solution)/shard_map/sum_over_devices/ppermute | solution.py:533
  20.1 0.9 %collective-permute-start.8 = (f32[56,128]{1,0:T(8,128)S(1)}, f32[56,128]{1,0:T(8,128)S(1)}, u32[]{:S(2)}, u32[]{:S(2)}) collective-permute-start(f32[56,128]{1,0:T(8,128)S(1)} %add.12), channel_id=1, source_target_pairs={{0,18},{1,19},{2,16},{3,17},{4,22},{5,23},{6,20},{7,21},{8,26},{9,... | collective-permute-start | bytes 86024 | tf_op jit(solution)/shard_map/sum_over_devices/ppermute | solution.py:533
  20.9 0.7 %collective-permute-start.6 = (f32[56,128]{1,0:T(8,128)S(1)}, f32[56,128]{1,0:T(8,128)S(1)}, u32[]{:S(2)}, u32[]{:S(2)}) collective-permute-start(f32[56,128]{1,0:T(8,128)S(1)} %add.12), channel_id=1, source_target_pairs={{0,3},{1,2},{2,1},{3,0},{4,7},{5,6},{6,5},{7,4},{8,11},{9,10},{10,... | collective-permute-start | bytes 86024 | tf_op jit(solution)/shard_map/sum_over_devices/ppermute | solution.py:533
  21.6 0.4 %collective-permute-done.7 = f32[56,128]{1,0:T(8,128)S(1)} collective-permute-done((f32[56,128]{1,0:T(8,128)S(1)}, f32[56,128]{1,0:T(8,128)S(1)}, u32[]{:S(2)}, u32[]{:S(2)}) %collective-permute-start.7) | collective-permute-done | bytes 28704 | tf_op jit(solution)/shard_map/sum_over_devices/ppermute | solution.py:533
  22.0 2.9 %collective-permute-done.8 = f32[56,128]{1,0:T(8,128)S(1)} collective-permute-done((f32[56,128]{1,0:T(8,128)S(1)}, f32[56,128]{1,0:T(8,128)S(1)}, u32[]{:S(2)}, u32[]{:S(2)}) %collective-permute-start.8) | collective-permute-done | bytes 28704 | tf_op jit(solution)/shard_map/sum_over_devices/ppermute | solution.py:533
  24.9 0.0 collective-permute-done.6
  24.9 2.8 %collective-permute-start.9 = (f32[56,128]{1,0:T(8,128)S(1)}, f32[56,128]{1,0:T(8,128)S(1)}, u32[]{:S(2)}, u32[]{:S(2)}) collective-permute-start(f32[56,128]{1,0:T(8,128)S(1)} %add_add_fusion.refs_0_), channel_id=1, source_target_pairs={{0,4},{1,5},{2,6},{3,7},{4,0},{5,1},{6,2},{7,3},{8,12},{9,13},{10,... | collective-permute-start | bytes 86024 | tf_op jit(solution)/shard_map/sum_over_devices/ppermute | solution.py:533
  27.6 0.9 %collective-permute-start.10 = (f32[56,128]{1,0:T(8,128)S(1)}, f32[56,128]{1,0:T(8,128)S(1)}, u32[]{:S(2)}, u32[]{:S(2)}) collective-permute-start(f32[56,128]{1,0:T(8,128)S(1)} %add_add_fusion.refs_0_), channel_id=1, source_target_pairs={{0,9},{1,8},{2,11},{3,10},{4,13},{5,12},{6,15},{7,14},{8,1},{9,0},... | collective-permute-start | bytes 86024 | tf_op jit(solution)/shard_map/sum_over_devices/ppermute | solution.py:533
  28.6 1.2 %collective-permute-start.11 = (f32[56,128]{1,0:T(8,128)S(1)}, f32[56,128]{1,0:T(8,128)S(1)}, u32[]{:S(2)}, u32[]{:S(2)}) collective-permute-start(f32[56,128]{1,0:T(8,128)S(1)} %add_add_fusion.refs_0_), channel_id=1, source_target_pairs={{0,13},{1,12},{2,15},{3,14},{4,9},{5,8},{6,11},{7,10},{8,5},{9,4},... | collective-permute-start | bytes 86024 | tf_op jit(solution)/shard_map/sum_over_devices/ppermute | solution.py:533
  29.8 0.8 %whole_basis.1.split = bf16[64,8192]{1,0:T(8,128)(2,1)S(1)} custom-call(f32[1536,128]{1,0:T(8,128)S(1)} %get-tuple-element.30.center, f32[1,192,128]{2,1,0:T(8,128)S(1)} %get-tuple-element.34.patch), custom_call_target="tpu_custom_call" | custom-call | flops 1000 | bytes 655360 | tf_op jit(solution)/shard_map/whole_basis/pallas_call | solution.py:637
  30.6 0.0 collective-permute-done.9.refs_1_
  30.6 1.5 %collective-permute-done.10.refs_2_ = f32[56,128]{1,0:T(8,128)S(1)} collective-permute-done((f32[56,128]{1,0:T(8,128)S(1)}, f32[56,128]{1,0:T(8,128)S(1)}, u32[]{:S(2)}, u32[]{:S(2)}) %collective-permute-start.10) | collective-permute-done | bytes 28704 | tf_op jit(solution)/shard_map/sum_over_devices/ppermute | solution.py:533
  32.1 1.5 %collective-permute-done.11.refs_3_ = f32[56,128]{1,0:T(8,128)S(1)} collective-permute-done((f32[56,128]{1,0:T(8,128)S(1)}, f32[56,128]{1,0:T(8,128)S(1)}, u32[]{:S(2)}, u32[]{:S(2)}) %collective-permute-start.11) | collective-permute-done | bytes 28704 | tf_op jit(solution)/shard_map/sum_over_devices/ppermute | solution.py:533
  33.7 2.7 %orthonormalize.1 = (f32[20,64,128]{2,1,0:T(8,128)}, f32[20,20]{1,0:T(8,128)}) custom-call(bf16[128,8192]{1,0:T(8,128)(2,1)S(1)} %get-tuple-element.20.history_split, bf16[64,8192]{1,0:T(8,128)(2,1)S(1)} %whole_basis.1.split, f32[56,128]{1,0:T(8,128)S(1)} %add_add_fusion.refs_0_, f32[56,128]{1,0:T(8,128)S(1)} %collective-permute-done.9.refs_1_, ...), custom_call_target="tpu_custom_call" | custom-call | flops 201326592 | bytes 655360 | tf_op jit(solution)/shard_map/orthonormalize/pallas_call | solution.py:659
  (4 shorter events, 0.0 us)
Async XLA Ops:
  1.6 5.5 %collective-permute-start = (f32[20,8,128]{2,1,0:T(8,128)S(1)}, f32[20,8,128]{2,1,0:T(8,128)S(1)}, u32[]{:S(2)}, u32[]{:S(2)}) collective-permute-start(f32[20,8,128]{2,1,0:T(8,128)S(1)} %get-tuple-element.24), channel_id=1, source_target_pairs={{0,4},{1,5},{2,6},{3,7},{4,0},{5,1},{6,2},{7,3},{8,12},{9,13},{10,... | collective-permute-start | bytes 245768 | tf_op jit(solution)/shard_map/halo_y/ppermute | solution.py:78
  4.7 2.4 %collective-permute-start.1 = (f32[20,8,128]{2,1,0:T(8,128)S(1)}, f32[20,8,128]{2,1,0:T(8,128)S(1)}, u32[]{:S(2)}, u32[]{:S(2)}) collective-permute-start(f32[20,8,128]{2,1,0:T(8,128)S(1)} %get-tuple-element.25), channel_id=1, source_target_pairs={{0,1},{1,0},{2,3},{3,2},{4,8},{5,9},{6,10},{7,11},{8,4},{9,5},{10,... | collective-permute-start | bytes 245768 | tf_op jit(solution)/shard_map/halo_y/ppermute | solution.py:78
  7.2 4.0 %collective-permute-start.2 = (f32[28,8,128]{2,1,0:T(8,128)S(1)}, f32[28,8,128]{2,1,0:T(8,128)S(1)}, u32[]{:S(2)}, u32[]{:S(2)}) collective-permute-start(f32[28,8,128]{2,1,0:T(8,128)S(1)} %get-tuple-element.27), channel_id=1, source_target_pairs={{0,1},{1,0},{2,3},{3,2},{4,5},{5,4},{6,7},{7,6},{8,9},{9,8},{10,11... | collective-permute-start | bytes 344072 | tf_op jit(solution)/shard_map/halo_z/ppermute | solution.py:78
  7.4 4.8 %collective-permute-start.3 = (f32[28,8,128]{2,1,0:T(8,128)S(1)}, f32[28,8,128]{2,1,0:T(8,128)S(1)}, u32[]{:S(2)}, u32[]{:S(2)}) collective-permute-start(f32[28,8,128]{2,1,0:T(8,128)S(1)} %get-tuple-element.28), channel_id=1, source_target_pairs={{0,16},{1,2},{2,1},{3,19},{4,20},{5,6},{6,5},{7,23},{8,24},{9,10},... | collective-permute-start | bytes 344072 | tf_op jit(solution)/shard_map/halo_z/ppermute | solution.py:78
  12.5 4.1 %collective-permute-start.4 = (f32[6,8,128]{2,1,0:T(8,128)S(1)}, f32[6,8,128]{2,1,0:T(8,128)S(1)}, u32[]{:S(2)}, u32[]{:S(2)}) collective-permute-start(f32[6,8,128]{2,1,0:T(8,128)S(1)} %get-tuple-element.33), channel_id=1, source_target_pairs={{0,16},{1,17},{2,18},{3,19},{4,20},{5,21},{6,22},{7,23},{8,24},{9,... | collective-permute-start | bytes 73736 | tf_op jit(solution)/shard_map/halo_x/ppermute | solution.py:78
  17.4 1.3 %collective-permute-start.5 = (f32[56,128]{1,0:T(8,128)S(1)}, f32[56,128]{1,0:T(8,128)S(1)}, u32[]{:S(2)}, u32[]{:S(2)}) collective-permute-start(f32[56,128]{1,0:T(8,128)S(1)} %get-tuple-element.35), channel_id=1, source_target_pairs={{0,1},{1,0},{2,3},{3,2},{4,5},{5,4},{6,7},{7,6},{8,9},{9,8},{10,11... | collective-permute-start | bytes 86024 | tf_op jit(solution)/shard_map/sum_over_devices/ppermute | solution.py:533
  18.7 3.3 %collective-permute-start.7 = (f32[56,128]{1,0:T(8,128)S(1)}, f32[56,128]{1,0:T(8,128)S(1)}, u32[]{:S(2)}, u32[]{:S(2)}) collective-permute-start(f32[56,128]{1,0:T(8,128)S(1)} %add.12), channel_id=1, source_target_pairs={{0,17},{1,16},{2,19},{3,18},{4,21},{5,20},{6,23},{7,22},{8,25},{9,... | collective-permute-start | bytes 86024 | tf_op jit(solution)/shard_map/sum_over_devices/ppermute | solution.py:533
  20.1 4.8 %collective-permute-start.8 = (f32[56,128]{1,0:T(8,128)S(1)}, f32[56,128]{1,0:T(8,128)S(1)}, u32[]{:S(2)}, u32[]{:S(2)}) collective-permute-start(f32[56,128]{1,0:T(8,128)S(1)} %add.12), channel_id=1, source_target_pairs={{0,18},{1,19},{2,16},{3,17},{4,22},{5,23},{6,20},{7,21},{8,26},{9,... | collective-permute-start | bytes 86024 | tf_op jit(solution)/shard_map/sum_over_devices/ppermute | solution.py:533
  20.9 3.9 %collective-permute-start.6 = (f32[56,128]{1,0:T(8,128)S(1)}, f32[56,128]{1,0:T(8,128)S(1)}, u32[]{:S(2)}, u32[]{:S(2)}) collective-permute-start(f32[56,128]{1,0:T(8,128)S(1)} %add.12), channel_id=1, source_target_pairs={{0,3},{1,2},{2,1},{3,0},{4,7},{5,6},{6,5},{7,4},{8,11},{9,10},{10,... | collective-permute-start | bytes 86024 | tf_op jit(solution)/shard_map/sum_over_devices/ppermute | solution.py:533
  24.9 5.7 %collective-permute-start.9 = (f32[56,128]{1,0:T(8,128)S(1)}, f32[56,128]{1,0:T(8,128)S(1)}, u32[]{:S(2)}, u32[]{:S(2)}) collective-permute-start(f32[56,128]{1,0:T(8,128)S(1)} %add_add_fusion.refs_0_), channel_id=1, source_target_pairs={{0,4},{1,5},{2,6},{3,7},{4,0},{5,1},{6,2},{7,3},{8,12},{9,13},{10,... | collective-permute-start | bytes 86024 | tf_op jit(solution)/shard_map/sum_over_devices/ppermute | solution.py:533
  27.6 4.5 %collective-permute-start.10 = (f32[56,128]{1,0:T(8,128)S(1)}, f32[56,128]{1,0:T(8,128)S(1)}, u32[]{:S(2)}, u32[]{:S(2)}) collective-permute-start(f32[56,128]{1,0:T(8,128)S(1)} %add_add_fusion.refs_0_), channel_id=1, source_target_pairs={{0,9},{1,8},{2,11},{3,10},{4,13},{5,12},{6,15},{7,14},{8,1},{9,0},... | collective-permute-start | bytes 86024 | tf_op jit(solution)/shard_map/sum_over_devices/ppermute | solution.py:533
  28.6 5.1 %collective-permute-start.11 = (f32[56,128]{1,0:T(8,128)S(1)}, f32[56,128]{1,0:T(8,128)S(1)}, u32[]{:S(2)}, u32[]{:S(2)}) collective-permute-start(f32[56,128]{1,0:T(8,128)S(1)} %add_add_fusion.refs_0_), channel_id=1, source_target_pairs={{0,13},{1,12},{2,15},{3,14},{4,9},{5,8},{6,11},{7,10},{8,5},{9,4},... | collective-permute-start | bytes 86024 | tf_op jit(solution)/shard_map/sum_over_devices/ppermute | solution.py:533

commit v5 on v4

--- a/solution.py
+++ b/solution.py
@@ -16,6 +16,7 @@
 Z, Y, X = 8, 8, 128
 CELLS = Z * Y
 PIECE = 16
+WIDTH = 8
 SLOTS = 16
 BPAD = 32
 BROWS = 24
@@ -208,7 +209,7 @@
     )
 
 
-def powers(fields, count, wide, history_split, history_gram, center, own, sums, *refs):
+def powers(fields, count, wide, history_split, center, own, sums, *refs):
     halo, coef_a, coef_b, split = refs
     columns = fields * (STEPS + 1)
     _, lane = iotas()
@@ -268,8 +269,7 @@
         high, low = split_rows(rows, BPAD)
         split[0:BPAD, cell * X : (cell + 1) * X] = high
         split[BPAD : 2 * BPAD, cell * X : (cell + 1) * X] = low
-    write_sums(sums, split[...], history_split[...])
-    sums[:, 0:HPAD] = history_gram[0:ROWS]
+    sums[...] = inner_products(split[...], history_split[...])
 
     for e, right in enumerate(ends):
         for f in range(fields + 1):
@@ -286,16 +286,14 @@
                     own[e, f, part, t] = tiles[part][t]
 
 
-def write_sums(sums, split, history_split):
+def inner_products(split, history_split):
     basis = join_lanes(join(product(split, split), BPAD), BPAD)
     cross = join_lanes(join(product(split, history_split), BPAD), HPAD)
-    sums[0:BROWS, HPAD:] = cross[:BROWS]
-    sums[BROWS : 2 * BROWS, HPAD : HPAD + BPAD] = basis[:BROWS]
-    sums[BROWS : 2 * BROWS, HPAD + BPAD :] = jnp.zeros((BROWS, X - HPAD - BPAD), F32)
-    sums[2 * BROWS :, HPAD:] = jnp.zeros((ROWS - 2 * BROWS, X - HPAD), F32)
-
-
-def powers_at_ends(fields, count, ways, own, history_ends, before, *refs):
+    both = jnp.concatenate([cross, basis, jnp.zeros((BPAD, X - HPAD - BPAD), F32)], axis=1)
+    return both[:BROWS]
+
+
+def powers_at_ends(fields, count, ways, own, history_ends, before, history_gram, *refs):
     received, (sums, patch, work, split) = refs[:ways], refs[ways:]
     columns = fields * (STEPS + 1)
     _, lane = iotas()
@@ -350,9 +348,43 @@
             at = (e * Y + y) * X
             split[0:BPAD, at : at + X] = high
             split[BPAD : 2 * BPAD, at : at + X] = low
-    write_sums(sums, split[...], history_ends[...])
-    sums[:, 0:HPAD] = before[:, 0:HPAD]
-    sums[:, HPAD:] = sums[:, HPAD:] + before[:, HPAD:]
+    both = before[...] + inner_products(split[...], history_ends[...])
+    first, second, third = (both[k : k + Y] for k in range(0, BROWS, Y))
+    sums[0:8] = history_gram[0:8]
+    sums[8:16] = jnp.where(lane < 96, history_gram[8:16], roll(first, 32, 1))
+    sums[16:24] = jnp.where(lane < ROWS, first, roll(second, ROWS, 1))
+    sums[24:32] = jnp.where(
+        lane < ROWS, third, jnp.where(lane < 80, roll(second, -8, 1), roll(third, 16, 1))
+    )
+
+
+PACKED = ((0, 0), (0, 56), (1, 0), (1, 40), (0, 104), (1, 72), (1, 88))
+
+
+def pack_gram(gram):
+    _, lane = iotas()
+    gram = jnp.concatenate([gram, jnp.zeros((HPAD, X - HPAD), F32)], axis=1)
+    tiles = [jnp.zeros((Y, X), F32)] * 2
+    for i, (t, first) in enumerate(PACKED):
+        inside = (lane >= first) & (lane < first + ROWS - 8 * i)
+        tiles[t] = jnp.where(inside, roll(gram[8 * i : 8 * i + 8], first - 8 * i, 1), tiles[t])
+    return jnp.concatenate(tiles, axis=0)
+
+
+def unpack_sums(total):
+    _, lane = iotas()
+    tiles = [total[8 * k : 8 * k + 8] for k in range(4)]
+    rows = []
+    for i, (t, first) in enumerate(PACKED):
+        row = jnp.where((lane >= 8 * i) & (lane < ROWS), roll(tiles[t], 8 * i - first, 1), 0.0)
+        rows.append(jnp.where(lane < 8 * i + 8, 0.5 * row, row))
+    rows.append(jnp.zeros((Y, X), F32))
+    upper = jnp.concatenate(rows, axis=0)[:, :HPAD]
+    coef = [tiles[2], roll(tiles[2], -ROWS, 1), tiles[3]]
+    coef = jnp.concatenate([jnp.where(lane < ROWS, c, 0.0) for c in coef], axis=0)[:, :HPAD]
+    basis = [roll(tiles[1], -96, 1), roll(tiles[3], -ROWS, 1), roll(tiles[3], -80, 1)]
+    basis = jnp.concatenate([jnp.where(lane < BROWS, b, 0.0) for b in basis], axis=0)[:, :BPAD]
+    return upper, coef, basis
 
 
 def patch_and_split(fields, count, center, patch, split, whole):
@@ -419,7 +451,7 @@
         high, low = split_rows(history[pl.ds(cell, count, stride=CELLS), :], HPAD)
         split[0:HPAD, cell * X : (cell + 1) * X] = high
         split[HPAD : 2 * HPAD, cell * X : (cell + 1) * X] = low
-    gram[...] = join_lanes(join(product(split[...], split[...]), HPAD), HPAD)
+    gram[...] = pack_gram(join_lanes(join(product(split[...], split[...]), HPAD), HPAD))
 
 
 def split_matrix(matrix):
@@ -434,20 +466,39 @@
 
 
 def finish(columns, cells, history_split, split, *refs):
-    parts, (out, factor, staged, factor_staged, done) = refs[:-5], refs[-5:]
-    total = (parts[0][...] + parts[1][...]) + (parts[2][...] + parts[3][...])
-    total = total * (1.0 / cells)
-    history_gram = jnp.concatenate([total[:, 0:HPAD], jnp.zeros((HPAD - ROWS, HPAD), F32)], axis=0)
-    coef = total[0:BROWS, HPAD:]
-    basis_gram = total[BROWS : 2 * BROWS, HPAD : HPAD + BPAD]
-    inner = jnp.dot(coef, history_gram, precision=HIGHEST, preferred_element_type=F32) - 2.0 * coef
+    parts, (out, factor, staged, factor_staged, done, projected) = refs[:-6], refs[-6:]
+    total = (parts[0][...] + parts[1][...]) * (1.0 / cells)
+    upper, coef, basis_gram = unpack_sums(total)
+    inner = jnp.dot(coef, upper, precision=HIGHEST, preferred_element_type=F32)
+    inner = inner + lax.dot_general(
+        coef, upper, (((1,), (1,)), ((), ())), precision=HIGHEST, preferred_element_type=F32
+    )
+    inner = inner - 2.0 * coef
     inner = jnp.concatenate([inner, jnp.zeros((BPAD - BROWS, HPAD), F32)], axis=0)
     gram = basis_gram + lax.dot_general(
         coef, inner, (((1,), (1,)), ((), ())), precision=HIGHEST, preferred_element_type=F32
     )
+    coef_high, coef_low = split_matrix(-jnp.concatenate([coef, jnp.zeros((BPAD - BROWS, HPAD), F32)], axis=0))
+    one = jnp.where(
+        lax.broadcasted_iota(jnp.int32, (BPAD, BPAD), 0) == lax.broadcasted_iota(jnp.int32, (BPAD, BPAD), 1), 1.0, 0.0
+    ).astype(BF16)
+    basis_minus = jnp.concatenate(
+        [
+            jnp.concatenate([coef_high, coef_high, one, one], axis=1),
+            jnp.concatenate([coef_low, jnp.zeros((BPAD, HPAD + 2 * BPAD), BF16)], axis=1),
+        ],
+        axis=0,
+    )
+    width = WIDTH * X
+    for c in range(CELLS * X // width):
+        at = slice(c * width, (c + 1) * width)
+        right = jnp.concatenate([history_split[:, at], split[:, at]], axis=0)
+        high, low = split_matrix(join(jnp.dot(basis_minus, right, preferred_element_type=F32), BPAD))
+        projected[0:BPAD, at] = high
+        projected[BPAD:, at] = low
     row = lax.broadcasted_iota(jnp.int32, (BROWS, X), 0)
     lane = lax.broadcasted_iota(jnp.int32, (BROWS, X), 1)
-    work = jnp.concatenate([gram, jnp.zeros((BROWS, X - BPAD - HPAD), F32), coef], axis=1)
+    work = jnp.concatenate([gram, jnp.zeros((BROWS, X - BPAD), F32)], axis=1)
     work = jnp.where(lane == row + BPAD, 1.0, work)
     panel = columns
     for start in range(0, columns, panel):
@@ -468,29 +519,19 @@
     copies = [pltpu.make_async_copy(factor_staged, factor, done.at[0])]
     copies[0].start()
     work = jnp.concatenate([work, jnp.zeros((BPAD - BROWS, X), F32)], axis=0)
-    history_high, history_low = split_matrix(-work[:, X - HPAD :])
     basis_high, basis_low = split_matrix(work[:, BPAD : 2 * BPAD])
     left = jnp.concatenate(
         [
-            jnp.concatenate([history_high, history_high, basis_high, basis_high], axis=1),
-            jnp.concatenate(
-                [history_low, jnp.zeros_like(history_low), basis_low, jnp.zeros_like(basis_low)], axis=1
-            ),
+            jnp.concatenate([basis_high, basis_high], axis=1),
+            jnp.concatenate([basis_low, jnp.zeros_like(basis_low)], axis=1),
         ],
         axis=0,
     )
-    width = 4 * X
+    width = WIDTH * X
     inside = width // X
     blocks = staged.reshape(columns, CELLS, X)
     for c in range(CELLS // inside):
-        right = jnp.concatenate(
-            [
-                history_split[:, c * width : (c + 1) * width],
-                split[:, c * width : (c + 1) * width],
-            ],
-            axis=0,
-        )
-        result = join(jnp.dot(left, right, preferred_element_type=F32), BPAD)
+        result = join(jnp.dot(left, projected[:, c * width : (c + 1) * width], preferred_element_type=F32), BPAD)
         for j in range(inside):
             staged[pl.ds(c * inside + j, columns, stride=CELLS), :] = result[
                 0:columns, j * X : (j + 1) * X
@@ -528,9 +569,16 @@
     )
 
 
-def exchange_sums(array, sizes, flips):
+def sum_over_devices(array, sizes):
     devices = range(sizes[0] * sizes[1] * sizes[2])
-    return [array] + [lax.ppermute(array, AXES, [(i, i ^ flip) for i in devices]) for flip in flips]
+    bits = []
+    for axis, stride in ((2, 1), (0, sizes[1] * sizes[2]), (1, sizes[2])):
+        bits += [stride << b for b in range(sizes[axis].bit_length() - 1)]
+    others = None
+    for bit in bits:
+        array = array if others is None else array + others
+        others = lax.ppermute(array, AXES, [(i, i ^ (bit | 1)) for i in devices])
+    return [array, others]
 
 
 def on_device(sizes, history, start, diagonal):
@@ -591,7 +639,7 @@
     with jax.named_scope("history_products"):
         history_split, history_gram = call(
             functools.partial(history_kernel, history_count),
-            [((2 * HPAD, CELLS * X), BF16), ((HPAD, HPAD), F32)],
+            [((2 * HPAD, CELLS * X), BF16), ((2 * Y, X), F32)],
             2 * 128 * 128 * CELLS * X,
             history.size * 4,
         )(rows)
@@ -611,7 +659,7 @@
             [
                 ((BROWS * CELLS, X), F32),
                 ((ends, all_fields, 2, 2, Y, X), F32),
-                ((ROWS, X), F32),
+                ((BROWS, X), F32),
             ],
             2 * 192 * 64 * CELLS * X,
             start.size * 4,
@@ -621,18 +669,18 @@
                 pltpu.VMEM((SLOTS, 2, Y, X), F32),
                 pltpu.VMEM((2 * BPAD, CELLS * X), BF16),
             ],
-        )(wide, history_split, history_gram)
+        )(wide, history_split)
     with jax.named_scope("powers_at_ends"):
         sums, patch = call(
             functools.partial(powers_at_ends, fields, count["gx"], ways["gx"]),
-            [((ROWS, X), F32), ((ends, BROWS * Y, X), F32)],
+            [((4 * Y, X), F32), ((ends, BROWS * Y, X), F32)],
             1000000,
             start.size * 4,
             [
                 pltpu.VMEM((STEPS + 1, fields, 2, 2, Y, X), F32),
                 pltpu.VMEM((2 * BPAD, ends * Y * X), BF16),
             ],
-        )(own, history_ends, sums, *received)
+        )(own, history_ends, sums, history_gram, *received)
     with jax.named_scope("whole_basis"):
         split = call(
             functools.partial(patch_and_split, fields, count["gx"]),
@@ -642,19 +690,7 @@
             [pltpu.VMEM((BROWS * CELLS, X), F32)],
         )(center, patch)[0]
     with jax.named_scope("sum_over_devices"):
-        bits = []
-        for axis, stride in (("gz", 1), ("gx", sizes[1] * sizes[2]), ("gy", sizes[2])):
-            bits += [stride << b for b in range(count[axis].bit_length() - 1)]
-        alone = 1 + (len(bits) - 1) % 2
-        for bit in bits[:alone]:
-            pair = exchange_sums(sums, sizes, [bit])
-            sums = pair[0] + pair[1]
-        for k in range(alone, len(bits), 2):
-            if k > alone:
-                sums = (parts[0] + parts[1]) + (parts[2] + parts[3])
-            one, two = bits[k : k + 2]
-            flips = [one, two ^ 1, one ^ two ^ 1] if k + 2 == len(bits) else [one ^ 1, two ^ 1, one ^ two]
-            parts = exchange_sums(sums, sizes, flips)
+        parts = sum_over_devices(sums, sizes)
     with jax.named_scope("orthonormalize"):
         out, factor = call(
             functools.partial(finish, columns, cells),
@@ -665,6 +701,7 @@
                 pltpu.VMEM((columns * CELLS, X), F32),
                 pltpu.VMEM((columns, columns), F32),
                 pltpu.SemaphoreType.DMA((CELLS // PIECE + 1,)),
+                pltpu.VMEM((2 * BPAD, CELLS * X), BF16),
             ],
             out_specs=[pl.BlockSpec(memory_space=pltpu.HBM)] * 2,
         )(history_split, split, *parts)

time: 36.8 us -> 36.3 us (0.986)
    ppermute x7 -> x5, waiting for transfers between devices: 7.51 us -> 7.36 us  [sum_over_devices(): others = lax.ppermute(array, AXES, [(i, i ^ (bit | 1)) for i in devices])]
    ppermute x7 -> x5, starting transfers between devices: 7.93 us -> 8.06 us  [sum_over_devices(): others = lax.ppermute(array, AXES, [(i, i ^ (bit | 1)) for i in devices])]
  transfers between devices with their start and end apart: 12 -> 10, of which waited for: 7 -> 7; matrix products, arithmetic and copies ran while one was open for 0% -> 0% of each run, Pallas kernels for 19% -> 20%
where the time goes in v5:
time: 36.3 us; the launch traced here: 36.2 us
  starting transfers between devices  15.1 us (42%)
  Pallas kernels  11.7 us (32%)
  waiting for transfers between devices  8.64 us (24%)
  between operations  0.71 us (2%)
    ppermute x5, starting transfers between devices, sum_over_devices(): others = lax.ppermute(array, AXES, [(i, i ^ (bit | 1)) for i in devices])  8.06 us
    ppermute x5, waiting for transfers between devices, sum_over_devices(): others = lax.ppermute(array, AXES, [(i, i ^ (bit | 1)) for i in devices])  7.36 us
    ppermute x5, starting transfers between devices, swaps(): lax.ppermute(a, AXES, pairs)  7.07 us
    pallas_call x1, Pallas kernels, on_device(): call(functools.partial(finish, columns, cells), [((columns, CELLS, X), F3...  2.53 us
    pallas_call x1, Pallas kernels, on_device(): call(functools.partial(powers, fields, count['gx']), [((BROWS * CELLS, X)...  2.13 us
    pallas_call x1, Pallas kernels, on_device(): call(functools.partial(history_kernel, history_count), [((2 * HPAD, CELLS...  2.05 us
    pallas_call x1, Pallas kernels, on_device(): call(load_history, [(history.shape, F32)], 1000, history.size * 4, [pltpu...  1.51 us
    ppermute x5, waiting for transfers between devices, swaps(): lax.ppermute(a, AXES, pairs)  1.29 us
  transfers between devices with their start and end apart: 10, of which 7 were waited for; matrix products, arithmetic and copies ran while one was open for 0% of the time, Pallas kernels for 20%

profile of v5, /device:TPU:0, one launch (start us, length us, event | category | flops | bytes accessed | tf_op | source)
XLA Modules:
  0.0 36.2 jit_solution(1757028516597337486)
XLA Ops:
  0.6 0.9 %halo_y.1 = (f32[4,8,8,128]{3,2,1,0:T(8,128)S(1)}, f32[8,8,128]{2,1,0:T(8,128)S(1)}, f32[20,8,128]{2,1,0:T(8,128)S(1)}, f32[20,8,128]{2,1,0:T(8,128)S(1)}) custom-call(f32[4,8,8,128]{3,2,1,0:T(8,128)} %start_there.1, f32[8,8,128]{2,1,0:T(8,128)} %diagonal_there.1), custom_call_target="tpu_custom_call" | custom-call | flops 1000 | bytes 131072 | tf_op jit(solution)/shard_map/halo_y/pallas_call | solution.py:599
  1.6 3.1 %collective-permute-start = (f32[20,8,128]{2,1,0:T(8,128)S(1)}, f32[20,8,128]{2,1,0:T(8,128)S(1)}, u32[]{:S(2)}, u32[]{:S(2)}) collective-permute-start(f32[20,8,128]{2,1,0:T(8,128)S(1)} %get-tuple-element.24), channel_id=1, source_target_pairs={{0,4},{1,5},{2,6},{3,7},{4,0},{5,1},{6,2},{7,3},{8,12},{9,13},{10,... | collective-permute-start | bytes 245768 | tf_op jit(solution)/shard_map/halo_y/ppermute | solution.py:79
  4.7 0.0 collective-permute-start.1
  4.7 1.5 %load_history.1 = f32[56,8,8,128]{3,2,1,0:T(8,128)S(1)} custom-call(f32[56,8,8,128]{3,2,1,0:T(8,128)} %history.1), custom_call_target="tpu_custom_call" | custom-call | flops 1000 | bytes 1835008 | tf_op jit(solution)/shard_map/load_history/pallas_call | solution.py:612
  6.2 0.6 %history_at_ends.1._.history_ends = bf16[128,1024]{1,0:T(8,128)(2,1)S(1)} custom-call(f32[3584,128]{1,0:T(8,128)S(1)} %bitcast.2), custom_call_target="tpu_custom_call" | custom-call | flops 1000 | bytes 917504 | tf_op jit(solution)/shard_map/history_at_ends/pallas_call | solution.py:623
  6.8 0.3 collective-permute-done.refs_0_
  7.1 0.0 collective-permute-done.1.refs_1_
  7.1 0.1 halo_z.1
  7.2 0.3 collective-permute-start.2
  7.4 1.8 %collective-permute-start.3 = (f32[28,8,128]{2,1,0:T(8,128)S(1)}, f32[28,8,128]{2,1,0:T(8,128)S(1)}, u32[]{:S(2)}, u32[]{:S(2)}) collective-permute-start(f32[28,8,128]{2,1,0:T(8,128)S(1)} %get-tuple-element.28), channel_id=1, source_target_pairs={{0,16},{1,2},{2,1},{3,19},{4,20},{5,6},{6,5},{7,23},{8,24},{9,10},... | collective-permute-start | bytes 344072 | tf_op jit(solution)/shard_map/halo_z/ppermute | solution.py:79
  9.3 2.0 %history_products.1 = (bf16[128,8192]{1,0:T(8,128)(2,1)S(1)}, f32[16,128]{1,0:T(8,128)S(1)}) custom-call(f32[3584,128]{1,0:T(8,128)S(1)} %bitcast.3), custom_call_target="tpu_custom_call" | custom-call | flops 268435456 | bytes 1835008 | tf_op jit(solution)/shard_map/history_products/pallas_call | solution.py:640
  11.3 0.0 collective-permute-done.2.refs_0_
  11.3 0.9 %collective-permute-done.3.refs_1_ = f32[28,8,128]{2,1,0:T(8,128)S(1)} collective-permute-done((f32[28,8,128]{2,1,0:T(8,128)S(1)}, f32[28,8,128]{2,1,0:T(8,128)S(1)}, u32[]{:S(2)}, u32[]{:S(2)}) %collective-permute-start.3) | collective-permute-done | bytes 114720 | tf_op jit(solution)/shard_map/halo_z/ppermute | solution.py:79
  12.2 0.2 halo_x.1
  12.5 1.9 %collective-permute-start.4 = (f32[6,8,128]{2,1,0:T(8,128)S(1)}, f32[6,8,128]{2,1,0:T(8,128)S(1)}, u32[]{:S(2)}, u32[]{:S(2)}) collective-permute-start(f32[6,8,128]{2,1,0:T(8,128)S(1)} %get-tuple-element.33), channel_id=1, source_target_pairs={{0,16},{1,17},{2,18},{3,19},{4,20},{5,21},{6,22},{7,23},{8,24},{9,... | collective-permute-start | bytes 73736 | tf_op jit(solution)/shard_map/halo_x/ppermute | solution.py:79
  14.4 2.1 %matrix_powers.1 = (f32[1536,128]{1,0:T(8,128)S(1)}, f32[1,5,2,2,8,128]{5,4,3,2,1,0:T(8,128)S(1)}, f32[24,128]{1,0:T(8,128)S(1)}) custom-call(f32[5,16,2,8,128]{4,3,2,1,0:T(8,128)S(1)} %get-tuple-element.29.wide, bf16[128,8192]{1,0:T(8,128)(2,1)S(1)} %get-tuple-element.20.history_split), custom_call_target="tpu_custom_call" | custom-call | flops 201326592 | bytes 131072 | tf_op jit(solution)/shard_map/matrix_powers/pallas_call | solution.py:657
  16.5 0.0 collective-permute-done.4.refs_0_
  16.5 0.9 %powers_at_ends.1 = (f32[32,128]{1,0:T(8,128)S(1)}, f32[1,192,128]{2,1,0:T(8,128)S(1)}) custom-call(f32[1,5,2,2,8,128]{5,4,3,2,1,0:T(8,128)S(1)} %get-tuple-element.31.own, bf16[128,1024]{1,0:T(8,128)(2,1)S(1)} %history_at_ends.1._.history_ends, f32[24,128]{1,0:T(8,128)S(1)} %get-tuple-element.32.before, f32[16,128]{1,0:T(8,128)S(1)} %get-tuple-element.23._.history_gram, ...), custom_call_target="tpu_custom_call" | custom-call | flops 1000000 | bytes 131072 | tf_op jit(solution)/shard_map/powers_at_ends/pallas_call | solution.py:674
  17.4 0.1 collective-permute-start.5
  17.5 1.2 %collective-permute-done.5 = f32[32,128]{1,0:T(8,128)S(1)} collective-permute-done((f32[32,128]{1,0:T(8,128)S(1)}, f32[32,128]{1,0:T(8,128)S(1)}, u32[]{:S(2)}, u32[]{:S(2)}) %collective-permute-start.5) | collective-permute-done | bytes 16416 | tf_op jit(solution)/shard_map/sum_over_devices/ppermute | solution.py:580
  18.6 0.8 %collective-permute-start.6 = (f32[32,128]{1,0:T(8,128)S(1)}, f32[32,128]{1,0:T(8,128)S(1)}, u32[]{:S(2)}, u32[]{:S(2)}) collective-permute-start(f32[32,128]{1,0:T(8,128)S(1)} %add.12), channel_id=1, source_target_pairs={{0,3},{1,2},{2,1},{3,0},{4,7},{5,6},{6,5},{7,4},{8,11},{9,10},{10,... | collective-permute-start | bytes 49160 | tf_op jit(solution)/shard_map/sum_over_devices/ppermute | solution.py:580
  19.5 2.4 %collective-permute-done.6 = f32[32,128]{1,0:T(8,128)S(1)} collective-permute-done((f32[32,128]{1,0:T(8,128)S(1)}, f32[32,128]{1,0:T(8,128)S(1)}, u32[]{:S(2)}, u32[]{:S(2)}) %collective-permute-start.6) | collective-permute-done | bytes 16416 | tf_op jit(solution)/shard_map/sum_over_devices/ppermute | solution.py:580
  21.8 1.4 %collective-permute-start.7 = (f32[32,128]{1,0:T(8,128)S(1)}, f32[32,128]{1,0:T(8,128)S(1)}, u32[]{:S(2)}, u32[]{:S(2)}) collective-permute-start(f32[32,128]{1,0:T(8,128)S(1)} %add.13), channel_id=1, source_target_pairs={{0,17},{1,16},{2,19},{3,18},{4,21},{5,20},{6,23},{7,22},{8,25},{9,... | collective-permute-start | bytes 49160 | tf_op jit(solution)/shard_map/sum_over_devices/ppermute | solution.py:580
  23.2 1.8 %collective-permute-done.7 = f32[32,128]{1,0:T(8,128)S(1)} collective-permute-done((f32[32,128]{1,0:T(8,128)S(1)}, f32[32,128]{1,0:T(8,128)S(1)}, u32[]{:S(2)}, u32[]{:S(2)}) %collective-permute-start.7) | collective-permute-done | bytes 16416 | tf_op jit(solution)/shard_map/sum_over_devices/ppermute | solution.py:580
  25.0 2.6 %collective-permute-start.8 = (f32[32,128]{1,0:T(8,128)S(1)}, f32[32,128]{1,0:T(8,128)S(1)}, u32[]{:S(2)}, u32[]{:S(2)}) collective-permute-start(f32[32,128]{1,0:T(8,128)S(1)} %add.14), channel_id=1, source_target_pairs={{0,5},{1,4},{2,7},{3,6},{4,1},{5,0},{6,3},{7,2},{8,13},{9,12},{10,... | collective-permute-start | bytes 49160 | tf_op jit(solution)/shard_map/sum_over_devices/ppermute | solution.py:580
  27.6 1.4 %collective-permute-done.8 = f32[32,128]{1,0:T(8,128)S(1)} collective-permute-done((f32[32,128]{1,0:T(8,128)S(1)}, f32[32,128]{1,0:T(8,128)S(1)}, u32[]{:S(2)}, u32[]{:S(2)}) %collective-permute-start.8) | collective-permute-done | bytes 16416 | tf_op jit(solution)/shard_map/sum_over_devices/ppermute | solution.py:580
  29.0 3.2 %collective-permute-start.9 = (f32[32,128]{1,0:T(8,128)S(1)}, f32[32,128]{1,0:T(8,128)S(1)}, u32[]{:S(2)}, u32[]{:S(2)}) collective-permute-start(f32[32,128]{1,0:T(8,128)S(1)} %add.15.refs_0_), channel_id=1, source_target_pairs={{0,9},{1,8},{2,11},{3,10},{4,13},{5,12},{6,15},{7,14},{8,1},{9,0},... | collective-permute-start | bytes 49160 | tf_op jit(solution)/shard_map/sum_over_devices/ppermute | solution.py:580
  32.2 0.8 %whole_basis.1.split = bf16[64,8192]{1,0:T(8,128)(2,1)S(1)} custom-call(f32[1536,128]{1,0:T(8,128)S(1)} %get-tuple-element.30.center, f32[1,192,128]{2,1,0:T(8,128)S(1)} %get-tuple-element.34.patch), custom_call_target="tpu_custom_call" | custom-call | flops 1000 | bytes 655360 | tf_op jit(solution)/shard_map/whole_basis/pallas_call | solution.py:685
  33.0 0.6 %collective-permute-done.9.refs_1_ = f32[32,128]{1,0:T(8,128)S(1)} collective-permute-done((f32[32,128]{1,0:T(8,128)S(1)}, f32[32,128]{1,0:T(8,128)S(1)}, u32[]{:S(2)}, u32[]{:S(2)}) %collective-permute-start.9) | collective-permute-done | bytes 16416 | tf_op jit(solution)/shard_map/sum_over_devices/ppermute | solution.py:580
  33.7 2.5 %orthonormalize.1 = (f32[20,64,128]{2,1,0:T(8,128)}, f32[20,20]{1,0:T(8,128)}) custom-call(bf16[128,8192]{1,0:T(8,128)(2,1)S(1)} %get-tuple-element.20.history_split, bf16[64,8192]{1,0:T(8,128)(2,1)S(1)} %whole_basis.1.split, f32[32,128]{1,0:T(8,128)S(1)} %add.15.refs_0_, f32[32,128]{1,0:T(8,128)S(1)} %collective-permute-done.9.refs_1_), custom_call_target="tpu_custom_call" | custom-call | flops 201326592 | bytes 655360 | tf_op jit(solution)/shard_map/orthonormalize/pallas_call | solution.py:695
  (4 shorter events, 0.0 us)
Async XLA Ops:
  1.6 5.5 %collective-permute-start = (f32[20,8,128]{2,1,0:T(8,128)S(1)}, f32[20,8,128]{2,1,0:T(8,128)S(1)}, u32[]{:S(2)}, u32[]{:S(2)}) collective-permute-start(f32[20,8,128]{2,1,0:T(8,128)S(1)} %get-tuple-element.24), channel_id=1, source_target_pairs={{0,4},{1,5},{2,6},{3,7},{4,0},{5,1},{6,2},{7,3},{8,12},{9,13},{10,... | collective-permute-start | bytes 245768 | tf_op jit(solution)/shard_map/halo_y/ppermute | solution.py:79
  4.7 2.4 %collective-permute-start.1 = (f32[20,8,128]{2,1,0:T(8,128)S(1)}, f32[20,8,128]{2,1,0:T(8,128)S(1)}, u32[]{:S(2)}, u32[]{:S(2)}) collective-permute-start(f32[20,8,128]{2,1,0:T(8,128)S(1)} %get-tuple-element.25), channel_id=1, source_target_pairs={{0,1},{1,0},{2,3},{3,2},{4,8},{5,9},{6,10},{7,11},{8,4},{9,5},{10,... | collective-permute-start | bytes 245768 | tf_op jit(solution)/shard_map/halo_y/ppermute | solution.py:79
  7.2 4.1 %collective-permute-start.2 = (f32[28,8,128]{2,1,0:T(8,128)S(1)}, f32[28,8,128]{2,1,0:T(8,128)S(1)}, u32[]{:S(2)}, u32[]{:S(2)}) collective-permute-start(f32[28,8,128]{2,1,0:T(8,128)S(1)} %get-tuple-element.27), channel_id=1, source_target_pairs={{0,1},{1,0},{2,3},{3,2},{4,5},{5,4},{6,7},{7,6},{8,9},{9,8},{10,11... | collective-permute-start | bytes 344072 | tf_op jit(solution)/shard_map/halo_z/ppermute | solution.py:79
  7.4 4.8 %collective-permute-start.3 = (f32[28,8,128]{2,1,0:T(8,128)S(1)}, f32[28,8,128]{2,1,0:T(8,128)S(1)}, u32[]{:S(2)}, u32[]{:S(2)}) collective-permute-start(f32[28,8,128]{2,1,0:T(8,128)S(1)} %get-tuple-element.28), channel_id=1, source_target_pairs={{0,16},{1,2},{2,1},{3,19},{4,20},{5,6},{6,5},{7,23},{8,24},{9,10},... | collective-permute-start | bytes 344072 | tf_op jit(solution)/shard_map/halo_z/ppermute | solution.py:79
  12.5 4.1 %collective-permute-start.4 = (f32[6,8,128]{2,1,0:T(8,128)S(1)}, f32[6,8,128]{2,1,0:T(8,128)S(1)}, u32[]{:S(2)}, u32[]{:S(2)}) collective-permute-start(f32[6,8,128]{2,1,0:T(8,128)S(1)} %get-tuple-element.33), channel_id=1, source_target_pairs={{0,16},{1,17},{2,18},{3,19},{4,20},{5,21},{6,22},{7,23},{8,24},{9,... | collective-permute-start | bytes 73736 | tf_op jit(solution)/shard_map/halo_x/ppermute | solution.py:79
  17.4 1.2 %collective-permute-start.5 = (f32[32,128]{1,0:T(8,128)S(1)}, f32[32,128]{1,0:T(8,128)S(1)}, u32[]{:S(2)}, u32[]{:S(2)}) collective-permute-start(f32[32,128]{1,0:T(8,128)S(1)} %get-tuple-element.35), channel_id=1, source_target_pairs={{0,1},{1,0},{2,3},{3,2},{4,5},{5,4},{6,7},{7,6},{8,9},{9,8},{10,11... | collective-permute-start | bytes 49160 | tf_op jit(solution)/shard_map/sum_over_devices/ppermute | solution.py:580
  18.6 3.2 %collective-permute-start.6 = (f32[32,128]{1,0:T(8,128)S(1)}, f32[32,128]{1,0:T(8,128)S(1)}, u32[]{:S(2)}, u32[]{:S(2)}) collective-permute-start(f32[32,128]{1,0:T(8,128)S(1)} %add.12), channel_id=1, source_target_pairs={{0,3},{1,2},{2,1},{3,0},{4,7},{5,6},{6,5},{7,4},{8,11},{9,10},{10,... | collective-permute-start | bytes 49160 | tf_op jit(solution)/shard_map/sum_over_devices/ppermute | solution.py:580
  21.8 3.2 %collective-permute-start.7 = (f32[32,128]{1,0:T(8,128)S(1)}, f32[32,128]{1,0:T(8,128)S(1)}, u32[]{:S(2)}, u32[]{:S(2)}) collective-permute-start(f32[32,128]{1,0:T(8,128)S(1)} %add.13), channel_id=1, source_target_pairs={{0,17},{1,16},{2,19},{3,18},{4,21},{5,20},{6,23},{7,22},{8,25},{9,... | collective-permute-start | bytes 49160 | tf_op jit(solution)/shard_map/sum_over_devices/ppermute | solution.py:580
  25.0 4.0 %collective-permute-start.8 = (f32[32,128]{1,0:T(8,128)S(1)}, f32[32,128]{1,0:T(8,128)S(1)}, u32[]{:S(2)}, u32[]{:S(2)}) collective-permute-start(f32[32,128]{1,0:T(8,128)S(1)} %add.14), channel_id=1, source_target_pairs={{0,5},{1,4},{2,7},{3,6},{4,1},{5,0},{6,3},{7,2},{8,13},{9,12},{10,... | collective-permute-start | bytes 49160 | tf_op jit(solution)/shard_map/sum_over_devices/ppermute | solution.py:580
  29.0 4.6 %collective-permute-start.9 = (f32[32,128]{1,0:T(8,128)S(1)}, f32[32,128]{1,0:T(8,128)S(1)}, u32[]{:S(2)}, u32[]{:S(2)}) collective-permute-start(f32[32,128]{1,0:T(8,128)S(1)} %add.15.refs_0_), channel_id=1, source_target_pairs={{0,9},{1,8},{2,11},{3,10},{4,13},{5,12},{6,15},{7,14},{8,1},{9,0},... | collective-permute-start | bytes 49160 | tf_op jit(solution)/shard_map/sum_over_devices/ppermute | solution.py:580

commit v6 on v5

--- a/solution.py
+++ b/solution.py
@@ -96,16 +96,15 @@
 def pack_y(fields, start_there, diagonal_there, start, diagonal, *refs):
     sends, done = refs[:-1], refs[-1]
     copies = [
-        pltpu.make_async_copy(start_there, start, done.at[0]),
-        pltpu.make_async_copy(diagonal_there, diagonal, done.at[1]),
+        pltpu.make_async_copy(start_there.at[f], start.at[f], done.at[f]) for f in range(fields)
     ]
+    copies.append(pltpu.make_async_copy(diagonal_there, diagonal, done.at[fields]))
     for copy in copies:
         copy.start()
-    for copy in copies:
-        copy.wait()
     row, _ = iotas()
     even = is_even("gy")
     for f in range(fields + 1):
+        copies[f].wait()
         for p in range(4):
             one, two = (start[f, z] if f < fields else diagonal[z] for z in (p, p + 4))
             to_high = jnp.where(row < 4, roll(one, 4, 0), two)
@@ -155,38 +154,61 @@
             yield at % SLOTS, part
 
 
-def pack_x(fields, count, ways, start, diagonal, _, beyond, *refs):
+def end_columns(fields, up, tile_of, halo):
+    _, lane = iotas()
+    tiles = [jnp.zeros((Y, X), F32)] * x_tiles(fields)
+    for f in range(fields + 1):
+        for z, part in known(fields, f):
+            if (z >= Z) != halo:
+                continue
+            index, column = divmod(2 * f + part, 4)
+            base = 16 * (z % 8) + 4 * column
+            moved = turn(tile_of(f, z, part), up, base + 4, base)
+            k = 2 * index + z // 8
+            tiles[k] = jnp.where((lane >= base) & (lane < base + 4), moved, tiles[k])
+    return tiles
+
+
+def pack_x_own(fields, start, diagonal, beyond, *sends):
+    def tile_of(f, z, part):
+        if part:
+            return beyond[f, z]
+        return start[f, z] if f < fields else diagonal[z]
+
+    even = is_even("gx")
+    for which, ref in enumerate(sends):
+        tiles = end_columns(fields, even if which == 0 else jnp.logical_not(even), tile_of, False)
+        for k, tile in enumerate(tiles):
+            ref[k] = tile
+
+
+def pack_x(fields, count, ways, x_ways, *refs):
+    owns, refs = refs[:x_ways], refs[x_ways + 1 :]
     received, (wide, *sends) = refs[:ways], refs[ways:]
-    _, lane = iotas()
     pick = facing("gz", count, received)
     even = is_even("gx")
+    found = {}
     k = 0
     for f in range(fields + 1):
         depth = 4 if f < fields else 3
-        for z in range(Z):
-            wide[f, z, 0] = start[f, z] if f < fields else diagonal[z]
-            wide[f, z, 1] = beyond[f, z]
         for d in range(1, depth + 1):
-            wide[f, SLOTS - d, 0], wide[f, Z - 1 + d, 0] = pick(k)
+            found[f, SLOTS - d, 0], found[f, Z - 1 + d, 0] = pick(k)
             k += 1
         if f < fields:
-            wide[f, SLOTS - 1, 1], wide[f, Z, 1] = pick(k)
+            found[f, SLOTS - 1, 1], found[f, Z, 1] = pick(k)
             k += 1
         low, high = pick(k)
         k += 1
-        wide[f, SLOTS - depth + 2, 1], wide[f, Z + depth - 3, 1] = low, high
-        wide[f, SLOTS - depth + 1, 1], wide[f, Z + depth - 2, 1] = roll(low, -3, 0), roll(high, -3, 0)
+        found[f, SLOTS - depth + 2, 1], found[f, Z + depth - 3, 1] = low, high
+        found[f, SLOTS - depth + 1, 1] = roll(low, -3, 0)
+        found[f, Z + depth - 2, 1] = roll(high, -3, 0)
+    for (f, z, part), tile in found.items():
+        wide[f, z - Z, part] = tile
     for which, ref in enumerate(sends):
         up = even if which == 0 else jnp.logical_not(even)
-        for k in range(x_tiles(fields)):
-            ref[k] = jnp.zeros((Y, X), F32)
-        for f in range(fields + 1):
-            for z, part in known(fields, f):
-                index, column = divmod(2 * f + part, 4)
-                base = 16 * (z % 8) + 4 * column
-                moved = turn(wide[f, z, part], up, base + 4, base)
-                k = 2 * index + z // 8
-                ref[k] = jnp.where((lane >= base) & (lane < base + 4), moved, ref[k])
+        tiles = end_columns(fields, up, lambda f, z, part: found[f, z, part], True)
+        for k, tile in enumerate(tiles):
+            ref[k] = tile + owns[which][k]
 
 
 def x_tiles(fields):
@@ -209,29 +231,36 @@
     )
 
 
-def powers(fields, count, wide, history_split, center, own, sums, *refs):
+def powers(fields, count, start, diagonal, beyond, wide, history_split, center, own, sums, *refs):
     halo, coef_a, coef_b, split = refs
     columns = fields * (STEPS + 1)
     _, lane = iotas()
     inside = set(range(Z))
     ends = ends_of(count)
 
+    def given(f, z, part):
+        if z >= Z:
+            return wide[f, z - Z, part]
+        if part:
+            return beyond[f, z]
+        return start[f, z] if f < fields else diagonal[z]
+
     for z, part in known(fields, fields):
         if part == 0 and z in inside:
-            coef_a[z, 0] = (wide[fields, z, 0] - 1.0) * (1.0 / 7.0)
+            coef_a[z, 0] = (diagonal[z] - 1.0) * (1.0 / 7.0)
         else:
-            coef_a[z, part], coef_b[z, part] = coefficients(wide[fields, z, part])
+            coef_a[z, part], coef_b[z, part] = coefficients(given(fields, z, part))
 
     def read(level, f, z, part):
         if level == 0:
-            return wide[f, z, part]
+            return given(f, z, part)
         if part == 0 and z in inside:
             return center[pl.ds((fields * level + f) * CELLS + z * Y, Y), :]
         return halo[level - 1, f, z, part]
 
     for f in range(fields):
         for z in range(Z):
-            center[pl.ds(f * CELLS + z * Y, Y), :] = wide[f, z, 0]
+            center[pl.ds(f * CELLS + z * Y, Y), :] = start[f, z]
     for level in range(1, STEPS + 1):
         reach = STEPS - level
         for f in range(fields):
@@ -277,7 +306,7 @@
             for z, part in known(fields, f):
                 base = 16 * (z % 8)
                 first = choose(right, base, base + 4)
-                moved = turn(wide[f, z, part], right, base + 8, base + 4)
+                moved = turn(given(f, z, part), right, base + 8, base + 4)
                 tiles[part][z // 8] = jnp.where(
                     (lane >= first) & (lane < first + 8), moved, tiles[part][z // 8]
                 )
@@ -520,18 +549,14 @@
     copies[0].start()
     work = jnp.concatenate([work, jnp.zeros((BPAD - BROWS, X), F32)], axis=0)
     basis_high, basis_low = split_matrix(work[:, BPAD : 2 * BPAD])
-    left = jnp.concatenate(
-        [
-            jnp.concatenate([basis_high, basis_high], axis=1),
-            jnp.concatenate([basis_low, jnp.zeros_like(basis_low)], axis=1),
-        ],
-        axis=0,
-    )
+    left = jnp.concatenate([basis_high, basis_high, basis_low], axis=1)
     width = WIDTH * X
     inside = width // X
-    blocks = staged.reshape(columns, CELLS, X)
+    blocks = staged.reshape(BROWS, CELLS, X)
     for c in range(CELLS // inside):
-        result = join(jnp.dot(left, projected[:, c * width : (c + 1) * width], preferred_element_type=F32), BPAD)
+        right = projected[:, c * width : (c + 1) * width]
+        right = jnp.concatenate([right, right[:BPAD]], axis=0)
+        result = jnp.dot(left, right, preferred_element_type=F32)
         for j in range(inside):
             staged[pl.ds(c * inside + j, columns, stride=CELLS), :] = result[
                 0:columns, j * X : (j + 1) * X
@@ -541,7 +566,7 @@
             piece = pl.ds(cells_done - PIECE, PIECE)
             copies.append(
                 pltpu.make_async_copy(
-                    blocks.at[:, piece, :], out.at[:, piece, :], done.at[len(copies)]
+                    blocks.at[pl.ds(0, columns), piece, :], out.at[:, piece, :], done.at[len(copies)]
                 )
             )
             copies[-1].start()
@@ -602,7 +627,7 @@
             + [((4 * all_fields, Y, X), F32)] * ways["gy"],
             1000,
             start.size * 4,
-            [pltpu.SemaphoreType.DMA((2,))],
+            [pltpu.SemaphoreType.DMA((all_fields,))],
             None,
             pltpu.VMEM,
             in_specs=[there, there],
@@ -644,14 +669,17 @@
             history.size * 4,
         )(rows)
     with jax.named_scope("halo_x"):
+        x_shapes = [((x_tiles(fields), Y, X), F32)] * ways["gx"]
+        owns = call(functools.partial(pack_x_own, fields), x_shapes, 1000, start.size * 4)(
+            start, diagonal, beyond
+        )
         wide, *sends = call(
-            functools.partial(pack_x, fields, count["gz"], ways["gz"]),
-            [((all_fields, SLOTS, 2, Y, X), F32)]
-            + [((x_tiles(fields), Y, X), F32)] * ways["gx"],
+            functools.partial(pack_x, fields, count["gz"], ways["gz"], ways["gx"]),
+            [((all_fields, SLOTS - Z, 2, Y, X), F32)] + x_shapes,
             1000,
             start.size * 4,
-            in_specs=[here, here, anywhere, here] + [here] * ways["gz"],
-        )(start, diagonal, history_gram, beyond, *received)
+            in_specs=[here] * ways["gx"] + [anywhere] + [here] * ways["gz"],
+        )(*owns, history_gram, *received)
         received = swaps(sends, sizes, "gx")
     with jax.named_scope("matrix_powers"):
         center, own, sums = call(
@@ -669,7 +697,7 @@
                 pltpu.VMEM((SLOTS, 2, Y, X), F32),
                 pltpu.VMEM((2 * BPAD, CELLS * X), BF16),
             ],
-        )(wide, history_split)
+        )(start, diagonal, beyond, wide, history_split)
     with jax.named_scope("powers_at_ends"):
         sums, patch = call(
             functools.partial(powers_at_ends, fields, count["gx"], ways["gx"]),
@@ -698,7 +726,7 @@
             2 * 192 * 64 * CELLS * X,
             columns * CELLS * X * 4,
             [
-                pltpu.VMEM((columns * CELLS, X), F32),
+                pltpu.VMEM((BROWS * CELLS, X), F32),
                 pltpu.VMEM((columns, columns), F32),
                 pltpu.SemaphoreType.DMA((CELLS // PIECE + 1,)),
                 pltpu.VMEM((2 * BPAD, CELLS * X), BF16),

time: 36.3 us -> 36.2 us (level)
  no operation moved by 1% of the time
where the time goes in v6:
time: 36.2 us; the launch traced here: 36 us
  starting transfers between devices  15.2 us (42%)
  Pallas kernels  11.6 us (32%)
  waiting for transfers between devices  8.4 us (23%)
  between operations  0.71 us (2%)
    ppermute x5, starting transfers between devices, sum_over_devices(): others = lax.ppermute(array, AXES, [(i, i ^ (bit | 1)) for i in devices])  8.17 us
    ppermute x5, waiting for transfers between devices, sum_over_devices(): others = lax.ppermute(array, AXES, [(i, i ^ (bit | 1)) for i in devices])  7.29 us
    ppermute x5, starting transfers between devices, swaps(): lax.ppermute(a, AXES, pairs)  7.07 us
    pallas_call x1, Pallas kernels, on_device(): call(functools.partial(finish, columns, cells), [((columns, CELLS, X), F3...  2.51 us
    pallas_call x1, Pallas kernels, on_device(): call(functools.partial(powers, fields, count['gx']), [((BROWS * CELLS, X)...  2.09 us
    pallas_call x1, Pallas kernels, on_device(): call(functools.partial(history_kernel, history_count), [((2 * HPAD, CELLS...  2.05 us
    pallas_call x1, Pallas kernels, on_device(): call(load_history, [(history.shape, F32)], 1000, history.size * 4, [pltpu...  1.51 us
    ppermute x5, waiting for transfers between devices, swaps(): lax.ppermute(a, AXES, pairs)  1.12 us
  transfers between devices with their start and end apart: 10, of which 7 were waited for; matrix products, arithmetic and copies ran while one was open for 0% of the time, Pallas kernels for 20%

profile of v6, /device:TPU:0, one launch (start us, length us, event | category | flops | bytes accessed | tf_op | source)
XLA Modules:
  0.0 36.0 jit_solution(6463220276001588944)
XLA Ops:
  0.6 0.9 %halo_y.1 = (f32[4,8,8,128]{3,2,1,0:T(8,128)S(1)}, f32[8,8,128]{2,1,0:T(8,128)S(1)}, f32[20,8,128]{2,1,0:T(8,128)S(1)}, f32[20,8,128]{2,1,0:T(8,128)S(1)}) custom-call(f32[4,8,8,128]{3,2,1,0:T(8,128)} %start_there.1, f32[8,8,128]{2,1,0:T(8,128)} %diagonal_there.1), custom_call_target="tpu_custom_call" | custom-call | flops 1000 | bytes 131072 | tf_op jit(solution)/shard_map/halo_y/pallas_call | solution.py:624
  1.5 3.1 %collective-permute-start = (f32[20,8,128]{2,1,0:T(8,128)S(1)}, f32[20,8,128]{2,1,0:T(8,128)S(1)}, u32[]{:S(2)}, u32[]{:S(2)}) collective-permute-start(f32[20,8,128]{2,1,0:T(8,128)S(1)} %get-tuple-element.23), channel_id=1, source_target_pairs={{0,4},{1,5},{2,6},{3,7},{4,0},{5,1},{6,2},{7,3},{8,12},{9,13},{10,... | collective-permute-start | bytes 245768 | tf_op jit(solution)/shard_map/halo_y/ppermute | solution.py:79
  4.6 0.0 collective-permute-start.1
  4.6 1.5 %load_history.1 = f32[56,8,8,128]{3,2,1,0:T(8,128)S(1)} custom-call(f32[56,8,8,128]{3,2,1,0:T(8,128)} %history.1), custom_call_target="tpu_custom_call" | custom-call | flops 1000 | bytes 1835008 | tf_op jit(solution)/shard_map/load_history/pallas_call | solution.py:637
  6.1 0.6 %history_at_ends.1._.history_ends = bf16[128,1024]{1,0:T(8,128)(2,1)S(1)} custom-call(f32[3584,128]{1,0:T(8,128)S(1)} %bitcast.2), custom_call_target="tpu_custom_call" | custom-call | flops 1000 | bytes 917504 | tf_op jit(solution)/shard_map/history_at_ends/pallas_call | solution.py:648
  6.7 0.3 collective-permute-done.refs_0_
  7.0 0.0 collective-permute-done.1.refs_1_
  7.0 0.1 halo_z.1
  7.1 0.3 collective-permute-start.2
  7.4 1.8 %collective-permute-start.3 = (f32[28,8,128]{2,1,0:T(8,128)S(1)}, f32[28,8,128]{2,1,0:T(8,128)S(1)}, u32[]{:S(2)}, u32[]{:S(2)}) collective-permute-start(f32[28,8,128]{2,1,0:T(8,128)S(1)} %get-tuple-element.28), channel_id=1, source_target_pairs={{0,16},{1,2},{2,1},{3,19},{4,20},{5,6},{6,5},{7,23},{8,24},{9,10},... | collective-permute-start | bytes 344072 | tf_op jit(solution)/shard_map/halo_z/ppermute | solution.py:79
  9.2 2.1 %history_products.1 = (bf16[128,8192]{1,0:T(8,128)(2,1)S(1)}, f32[16,128]{1,0:T(8,128)S(1)}) custom-call(f32[3584,128]{1,0:T(8,128)S(1)} %bitcast.3), custom_call_target="tpu_custom_call" | custom-call | flops 268435456 | bytes 1835008 | tf_op jit(solution)/shard_map/history_products/pallas_call | solution.py:665
  11.2 0.2 halo_x.2.refs_0_
  11.4 0.0 collective-permute-done.2.refs_2_
  11.4 0.7 %collective-permute-done.3.refs_3_ = f32[28,8,128]{2,1,0:T(8,128)S(1)} collective-permute-done((f32[28,8,128]{2,1,0:T(8,128)S(1)}, f32[28,8,128]{2,1,0:T(8,128)S(1)}, u32[]{:S(2)}, u32[]{:S(2)}) %collective-permute-start.3) | collective-permute-done | bytes 114720 | tf_op jit(solution)/shard_map/halo_z/ppermute | solution.py:79
  12.2 0.1 halo_x.3
  12.3 1.9 %collective-permute-start.4 = (f32[6,8,128]{2,1,0:T(8,128)S(1)}, f32[6,8,128]{2,1,0:T(8,128)S(1)}, u32[]{:S(2)}, u32[]{:S(2)}) collective-permute-start(f32[6,8,128]{2,1,0:T(8,128)S(1)} %get-tuple-element.33), channel_id=1, source_target_pairs={{0,16},{1,17},{2,18},{3,19},{4,20},{5,21},{6,22},{7,23},{8,24},{9,... | collective-permute-start | bytes 73736 | tf_op jit(solution)/shard_map/halo_x/ppermute | solution.py:79
  14.2 2.1 %matrix_powers.1 = (f32[1536,128]{1,0:T(8,128)S(1)}, f32[1,5,2,2,8,128]{5,4,3,2,1,0:T(8,128)S(1)}, f32[24,128]{1,0:T(8,128)S(1)}) custom-call(f32[4,8,8,128]{3,2,1,0:T(8,128)S(1)} %get-tuple-element.21.start, f32[8,8,128]{2,1,0:T(8,128)S(1)} %get-tuple-element.22.diagonal, f32[5,8,8,128]{3,2,1,0:T(8,128)S(1)} %get-tuple-element.25.beyond, ...), custom_call_target="tpu_custom_call" | custom-call | flops 201326592 | bytes 131072 | tf_op jit(solution)/shard_map/matrix_powers/pallas_call | solution.py:685
  16.3 0.0 collective-permute-done.4.refs_0_
  16.3 0.9 %powers_at_ends.1 = (f32[32,128]{1,0:T(8,128)S(1)}, f32[1,192,128]{2,1,0:T(8,128)S(1)}) custom-call(f32[1,5,2,2,8,128]{5,4,3,2,1,0:T(8,128)S(1)} %get-tuple-element.31.own, bf16[128,1024]{1,0:T(8,128)(2,1)S(1)} %history_at_ends.1._.history_ends, f32[24,128]{1,0:T(8,128)S(1)} %get-tuple-element.32.before, ...), custom_call_target="tpu_custom_call" | custom-call | flops 1000000 | bytes 131072 | tf_op jit(solution)/shard_map/powers_at_ends/pallas_call | solution.py:702
  17.2 0.1 collective-permute-start.5
  17.3 1.2 %collective-permute-done.5 = f32[32,128]{1,0:T(8,128)S(1)} collective-permute-done((f32[32,128]{1,0:T(8,128)S(1)}, f32[32,128]{1,0:T(8,128)S(1)}, u32[]{:S(2)}, u32[]{:S(2)}) %collective-permute-start.5) | collective-permute-done | bytes 16416 | tf_op jit(solution)/shard_map/sum_over_devices/ppermute | solution.py:605
  18.4 0.8 %collective-permute-start.6 = (f32[32,128]{1,0:T(8,128)S(1)}, f32[32,128]{1,0:T(8,128)S(1)}, u32[]{:S(2)}, u32[]{:S(2)}) collective-permute-start(f32[32,128]{1,0:T(8,128)S(1)} %add.12), channel_id=1, source_target_pairs={{0,3},{1,2},{2,1},{3,0},{4,7},{5,6},{6,5},{7,4},{8,11},{9,10},{10,... | collective-permute-start | bytes 49160 | tf_op jit(solution)/shard_map/sum_over_devices/ppermute | solution.py:605
  19.3 2.3 %collective-permute-done.6 = f32[32,128]{1,0:T(8,128)S(1)} collective-permute-done((f32[32,128]{1,0:T(8,128)S(1)}, f32[32,128]{1,0:T(8,128)S(1)}, u32[]{:S(2)}, u32[]{:S(2)}) %collective-permute-start.6) | collective-permute-done | bytes 16416 | tf_op jit(solution)/shard_map/sum_over_devices/ppermute | solution.py:605
  21.6 1.4 %collective-permute-start.7 = (f32[32,128]{1,0:T(8,128)S(1)}, f32[32,128]{1,0:T(8,128)S(1)}, u32[]{:S(2)}, u32[]{:S(2)}) collective-permute-start(f32[32,128]{1,0:T(8,128)S(1)} %add.13), channel_id=1, source_target_pairs={{0,17},{1,16},{2,19},{3,18},{4,21},{5,20},{6,23},{7,22},{8,25},{9,... | collective-permute-start | bytes 49160 | tf_op jit(solution)/shard_map/sum_over_devices/ppermute | solution.py:605
  23.1 1.7 %collective-permute-done.7 = f32[32,128]{1,0:T(8,128)S(1)} collective-permute-done((f32[32,128]{1,0:T(8,128)S(1)}, f32[32,128]{1,0:T(8,128)S(1)}, u32[]{:S(2)}, u32[]{:S(2)}) %collective-permute-start.7) | collective-permute-done | bytes 16416 | tf_op jit(solution)/shard_map/sum_over_devices/ppermute | solution.py:605
  24.8 2.6 %collective-permute-start.8 = (f32[32,128]{1,0:T(8,128)S(1)}, f32[32,128]{1,0:T(8,128)S(1)}, u32[]{:S(2)}, u32[]{:S(2)}) collective-permute-start(f32[32,128]{1,0:T(8,128)S(1)} %add.14), channel_id=1, source_target_pairs={{0,5},{1,4},{2,7},{3,6},{4,1},{5,0},{6,3},{7,2},{8,13},{9,12},{10,... | collective-permute-start | bytes 49160 | tf_op jit(solution)/shard_map/sum_over_devices/ppermute | solution.py:605
  27.4 1.4 %collective-permute-done.8 = f32[32,128]{1,0:T(8,128)S(1)} collective-permute-done((f32[32,128]{1,0:T(8,128)S(1)}, f32[32,128]{1,0:T(8,128)S(1)}, u32[]{:S(2)}, u32[]{:S(2)}) %collective-permute-start.8) | collective-permute-done | bytes 16416 | tf_op jit(solution)/shard_map/sum_over_devices/ppermute | solution.py:605
  28.9 3.2 %collective-permute-start.9 = (f32[32,128]{1,0:T(8,128)S(1)}, f32[32,128]{1,0:T(8,128)S(1)}, u32[]{:S(2)}, u32[]{:S(2)}) collective-permute-start(f32[32,128]{1,0:T(8,128)S(1)} %add.15.refs_0_), channel_id=1, source_target_pairs={{0,9},{1,8},{2,11},{3,10},{4,13},{5,12},{6,15},{7,14},{8,1},{9,0},... | collective-permute-start | bytes 49160 | tf_op jit(solution)/shard_map/sum_over_devices/ppermute | solution.py:605
  32.0 0.8 %whole_basis.1.split = bf16[64,8192]{1,0:T(8,128)(2,1)S(1)} custom-call(f32[1536,128]{1,0:T(8,128)S(1)} %get-tuple-element.30.center, f32[1,192,128]{2,1,0:T(8,128)S(1)} %get-tuple-element.34.patch), custom_call_target="tpu_custom_call" | custom-call | flops 1000 | bytes 655360 | tf_op jit(solution)/shard_map/whole_basis/pallas_call | solution.py:713
  32.9 0.6 %collective-permute-done.9.refs_1_ = f32[32,128]{1,0:T(8,128)S(1)} collective-permute-done((f32[32,128]{1,0:T(8,128)S(1)}, f32[32,128]{1,0:T(8,128)S(1)}, u32[]{:S(2)}, u32[]{:S(2)}) %collective-permute-start.9) | collective-permute-done | bytes 16416 | tf_op jit(solution)/shard_map/sum_over_devices/ppermute | solution.py:605
  33.5 2.5 %orthonormalize.1 = (f32[20,64,128]{2,1,0:T(8,128)}, f32[20,20]{1,0:T(8,128)}) custom-call(bf16[128,8192]{1,0:T(8,128)(2,1)S(1)} %get-tuple-element.20.history_split, bf16[64,8192]{1,0:T(8,128)(2,1)S(1)} %whole_basis.1.split, f32[32,128]{1,0:T(8,128)S(1)} %add.15.refs_0_, f32[32,128]{1,0:T(8,128)S(1)} %collective-permute-done.9.refs_1_), custom_call_target="tpu_custom_call" | custom-call | flops 201326592 | bytes 655360 | tf_op jit(solution)/shard_map/orthonormalize/pallas_call | solution.py:723
  (4 shorter events, 0.0 us)
Async XLA Ops:
  1.5 5.5 %collective-permute-start = (f32[20,8,128]{2,1,0:T(8,128)S(1)}, f32[20,8,128]{2,1,0:T(8,128)S(1)}, u32[]{:S(2)}, u32[]{:S(2)}) collective-permute-start(f32[20,8,128]{2,1,0:T(8,128)S(1)} %get-tuple-element.23), channel_id=1, source_target_pairs={{0,4},{1,5},{2,6},{3,7},{4,0},{5,1},{6,2},{7,3},{8,12},{9,13},{10,... | collective-permute-start | bytes 245768 | tf_op jit(solution)/shard_map/halo_y/ppermute | solution.py:79
  4.6 2.4 %collective-permute-start.1 = (f32[20,8,128]{2,1,0:T(8,128)S(1)}, f32[20,8,128]{2,1,0:T(8,128)S(1)}, u32[]{:S(2)}, u32[]{:S(2)}) collective-permute-start(f32[20,8,128]{2,1,0:T(8,128)S(1)} %get-tuple-element.24), channel_id=1, source_target_pairs={{0,1},{1,0},{2,3},{3,2},{4,8},{5,9},{6,10},{7,11},{8,4},{9,5},{10,... | collective-permute-start | bytes 245768 | tf_op jit(solution)/shard_map/halo_y/ppermute | solution.py:79
  7.1 4.3 %collective-permute-start.2 = (f32[28,8,128]{2,1,0:T(8,128)S(1)}, f32[28,8,128]{2,1,0:T(8,128)S(1)}, u32[]{:S(2)}, u32[]{:S(2)}) collective-permute-start(f32[28,8,128]{2,1,0:T(8,128)S(1)} %get-tuple-element.27), channel_id=1, source_target_pairs={{0,1},{1,0},{2,3},{3,2},{4,5},{5,4},{6,7},{7,6},{8,9},{9,8},{10,11... | collective-permute-start | bytes 344072 | tf_op jit(solution)/shard_map/halo_z/ppermute | solution.py:79
  7.4 4.8 %collective-permute-start.3 = (f32[28,8,128]{2,1,0:T(8,128)S(1)}, f32[28,8,128]{2,1,0:T(8,128)S(1)}, u32[]{:S(2)}, u32[]{:S(2)}) collective-permute-start(f32[28,8,128]{2,1,0:T(8,128)S(1)} %get-tuple-element.28), channel_id=1, source_target_pairs={{0,16},{1,2},{2,1},{3,19},{4,20},{5,6},{6,5},{7,23},{8,24},{9,10},... | collective-permute-start | bytes 344072 | tf_op jit(solution)/shard_map/halo_z/ppermute | solution.py:79
  12.3 4.0 %collective-permute-start.4 = (f32[6,8,128]{2,1,0:T(8,128)S(1)}, f32[6,8,128]{2,1,0:T(8,128)S(1)}, u32[]{:S(2)}, u32[]{:S(2)}) collective-permute-start(f32[6,8,128]{2,1,0:T(8,128)S(1)} %get-tuple-element.33), channel_id=1, source_target_pairs={{0,16},{1,17},{2,18},{3,19},{4,20},{5,21},{6,22},{7,23},{8,24},{9,... | collective-permute-start | bytes 73736 | tf_op jit(solution)/shard_map/halo_x/ppermute | solution.py:79
  17.2 1.2 %collective-permute-start.5 = (f32[32,128]{1,0:T(8,128)S(1)}, f32[32,128]{1,0:T(8,128)S(1)}, u32[]{:S(2)}, u32[]{:S(2)}) collective-permute-start(f32[32,128]{1,0:T(8,128)S(1)} %get-tuple-element.35), channel_id=1, source_target_pairs={{0,1},{1,0},{2,3},{3,2},{4,5},{5,4},{6,7},{7,6},{8,9},{9,8},{10,11... | collective-permute-start | bytes 49160 | tf_op jit(solution)/shard_map/sum_over_devices/ppermute | solution.py:605
  18.4 3.2 %collective-permute-start.6 = (f32[32,128]{1,0:T(8,128)S(1)}, f32[32,128]{1,0:T(8,128)S(1)}, u32[]{:S(2)}, u32[]{:S(2)}) collective-permute-start(f32[32,128]{1,0:T(8,128)S(1)} %add.12), channel_id=1, source_target_pairs={{0,3},{1,2},{2,1},{3,0},{4,7},{5,6},{6,5},{7,4},{8,11},{9,10},{10,... | collective-permute-start | bytes 49160 | tf_op jit(solution)/shard_map/sum_over_devices/ppermute | solution.py:605
  21.6 3.2 %collective-permute-start.7 = (f32[32,128]{1,0:T(8,128)S(1)}, f32[32,128]{1,0:T(8,128)S(1)}, u32[]{:S(2)}, u32[]{:S(2)}) collective-permute-start(f32[32,128]{1,0:T(8,128)S(1)} %add.13), channel_id=1, source_target_pairs={{0,17},{1,16},{2,19},{3,18},{4,21},{5,20},{6,23},{7,22},{8,25},{9,... | collective-permute-start | bytes 49160 | tf_op jit(solution)/shard_map/sum_over_devices/ppermute | solution.py:605
  24.8 4.1 %collective-permute-start.8 = (f32[32,128]{1,0:T(8,128)S(1)}, f32[32,128]{1,0:T(8,128)S(1)}, u32[]{:S(2)}, u32[]{:S(2)}) collective-permute-start(f32[32,128]{1,0:T(8,128)S(1)} %add.14), channel_id=1, source_target_pairs={{0,5},{1,4},{2,7},{3,6},{4,1},{5,0},{6,3},{7,2},{8,13},{9,12},{10,... | collective-permute-start | bytes 49160 | tf_op jit(solution)/shard_map/sum_over_devices/ppermute | solution.py:605
  28.9 4.6 %collective-permute-start.9 = (f32[32,128]{1,0:T(8,128)S(1)}, f32[32,128]{1,0:T(8,128)S(1)}, u32[]{:S(2)}, u32[]{:S(2)}) collective-permute-start(f32[32,128]{1,0:T(8,128)S(1)} %add.15.refs_0_), channel_id=1, source_target_pairs={{0,9},{1,8},{2,11},{3,10},{4,13},{5,12},{6,15},{7,14},{8,1},{9,0},... | collective-permute-start | bytes 49160 | tf_op jit(solution)/shard_map/sum_over_devices/ppermute | solution.py:605

commit v7 on v6

--- a/solution.py
+++ b/solution.py
@@ -133,9 +133,15 @@
             for d in range(1, 5):
                 ref[k] = start[f, at[d]]
                 k += 1
-            ref[k] = beyond[f, at[1]]
-            ref[k + 1] = jnp.where(inner, roll(beyond[f, at[3]], 3, 0), beyond[f, at[2]])
-            k += 2
+            far = beyond[f, at[3]]
+            ref[k] = jnp.where(
+                row == 3, roll(far, 3, 0), jnp.where(row == 4, roll(far, -3, 0), beyond[f, at[1]])
+            )
+            k += 1
+        for f in range(0, fields, 2):
+            shared = roll(beyond[min(f + 1, fields - 1), at[2]], 4, 0)
+            ref[k] = jnp.where((row >= 2) & (row < 6), shared, beyond[f, at[2]])
+            k += 1
         for d in range(1, 4):
             ref[k] = diagonal[at[d]]
             k += 1
@@ -143,7 +149,7 @@
 
 
 def z_tiles(fields):
-    return 6 * fields + 4
+    return 5 * fields + (fields + 1) // 2 + 4
 
 
 def known(fields, f):
@@ -185,6 +191,7 @@
 def pack_x(fields, count, ways, x_ways, *refs):
     owns, refs = refs[:x_ways], refs[x_ways + 1 :]
     received, (wide, *sends) = refs[:ways], refs[ways:]
+    row, _ = iotas()
     pick = facing("gz", count, received)
     even = is_even("gx")
     found = {}
@@ -195,13 +202,20 @@
             found[f, SLOTS - d, 0], found[f, Z - 1 + d, 0] = pick(k)
             k += 1
         if f < fields:
-            found[f, SLOTS - 1, 1], found[f, Z, 1] = pick(k)
+            for z, far_z, tile in zip((SLOTS - 1, Z), (SLOTS - 3, Z + 2), pick(k)):
+                found[f, z, 1] = tile
+                found[f, far_z, 1] = jnp.where(row < 4, roll(tile, -3, 0), roll(tile, 3, 0))
             k += 1
-        low, high = pick(k)
-        k += 1
-        found[f, SLOTS - depth + 2, 1], found[f, Z + depth - 3, 1] = low, high
-        found[f, SLOTS - depth + 1, 1] = roll(low, -3, 0)
-        found[f, Z + depth - 2, 1] = roll(high, -3, 0)
+            if f == fields - 1:
+                for g in range(fields):
+                    shared = pick(k + g // 2)
+                    found[g, SLOTS - 2, 1], found[g, Z + 1, 1] = (roll(t, 4 * (g % 2), 0) for t in shared)
+                k += (fields + 1) // 2
+        else:
+            low, high = pick(k)
+            k += 1
+            found[f, SLOTS - 1, 1], found[f, Z, 1] = low, high
+            found[f, SLOTS - 2, 1], found[f, Z + 1, 1] = roll(low, -3, 0), roll(high, -3, 0)
     for (f, z, part), tile in found.items():
         wide[f, z - Z, part] = tile
     for which, ref in enumerate(sends):

time: 36.2 us -> 36.1 us (level)
  no operation moved by 1% of the time
where the time goes in v7:
time: 36.1 us; the launch traced here: 35.9 us
  starting transfers between devices  15.2 us (42%)
  Pallas kernels  11.6 us (32%)
  waiting for transfers between devices  8.31 us (23%)
  between operations  0.72 us (2%)
    ppermute x5, starting transfers between devices, sum_over_devices(): others = lax.ppermute(array, AXES, [(i, i ^ (bit | 1)) for i in devices])  8.18 us
    ppermute x5, waiting for transfers between devices, sum_over_devices(): others = lax.ppermute(array, AXES, [(i, i ^ (bit | 1)) for i in devices])  7.27 us
    ppermute x5, starting transfers between devices, swaps(): lax.ppermute(a, AXES, pairs)  7.06 us
    pallas_call x1, Pallas kernels, on_device(): call(functools.partial(finish, columns, cells), [((columns, CELLS, X), F3...  2.51 us
    pallas_call x1, Pallas kernels, on_device(): call(functools.partial(powers, fields, count['gx']), [((BROWS * CELLS, X)...  2.09 us
    pallas_call x1, Pallas kernels, on_device(): call(functools.partial(history_kernel, history_count), [((2 * HPAD, CELLS...  2.05 us
    pallas_call x1, Pallas kernels, on_device(): call(load_history, [(history.shape, F32)], 1000, history.size * 4, [pltpu...  1.51 us
    ppermute x5, waiting for transfers between devices, swaps(): lax.ppermute(a, AXES, pairs)  1.03 us
  transfers between devices with their start and end apart: 10, of which 7 were waited for; matrix products, arithmetic and copies ran while one was open for 0% of the time, Pallas kernels for 20%

profile of v7, /device:TPU:0, one launch (start us, length us, event | category | flops | bytes accessed | tf_op | source)
XLA Modules:
  0.0 35.9 jit_solution(11472050471557347580)
XLA Ops:
  0.6 0.9 %halo_y.1 = (f32[4,8,8,128]{3,2,1,0:T(8,128)S(1)}, f32[8,8,128]{2,1,0:T(8,128)S(1)}, f32[20,8,128]{2,1,0:T(8,128)S(1)}, f32[20,8,128]{2,1,0:T(8,128)S(1)}) custom-call(f32[4,8,8,128]{3,2,1,0:T(8,128)} %start_there.1, f32[8,8,128]{2,1,0:T(8,128)} %diagonal_there.1), custom_call_target="tpu_custom_call" | custom-call | flops 1000 | bytes 131072 | tf_op jit(solution)/shard_map/halo_y/pallas_call | solution.py:638
  1.5 3.1 %collective-permute-start = (f32[20,8,128]{2,1,0:T(8,128)S(1)}, f32[20,8,128]{2,1,0:T(8,128)S(1)}, u32[]{:S(2)}, u32[]{:S(2)}) collective-permute-start(f32[20,8,128]{2,1,0:T(8,128)S(1)} %get-tuple-element.23), channel_id=1, source_target_pairs={{0,4},{1,5},{2,6},{3,7},{4,0},{5,1},{6,2},{7,3},{8,12},{9,13},{10,... | collective-permute-start | bytes 245768 | tf_op jit(solution)/shard_map/halo_y/ppermute | solution.py:79
  4.6 0.0 collective-permute-start.1
  4.6 1.5 %load_history.1 = f32[56,8,8,128]{3,2,1,0:T(8,128)S(1)} custom-call(f32[56,8,8,128]{3,2,1,0:T(8,128)} %history.1), custom_call_target="tpu_custom_call" | custom-call | flops 1000 | bytes 1835008 | tf_op jit(solution)/shard_map/load_history/pallas_call | solution.py:651
  6.1 0.6 %history_at_ends.1._.history_ends = bf16[128,1024]{1,0:T(8,128)(2,1)S(1)} custom-call(f32[3584,128]{1,0:T(8,128)S(1)} %bitcast.2), custom_call_target="tpu_custom_call" | custom-call | flops 1000 | bytes 917504 | tf_op jit(solution)/shard_map/history_at_ends/pallas_call | solution.py:662
  6.7 0.3 collective-permute-done.refs_0_
  7.0 0.0 collective-permute-done.1.refs_1_
  7.0 0.1 halo_z.1
  7.1 0.3 collective-permute-start.2
  7.4 1.8 %collective-permute-start.3 = (f32[26,8,128]{2,1,0:T(8,128)S(1)}, f32[26,8,128]{2,1,0:T(8,128)S(1)}, u32[]{:S(2)}, u32[]{:S(2)}) collective-permute-start(f32[26,8,128]{2,1,0:T(8,128)S(1)} %get-tuple-element.28), channel_id=1, source_target_pairs={{0,16},{1,2},{2,1},{3,19},{4,20},{5,6},{6,5},{7,23},{8,24},{9,10},... | collective-permute-start | bytes 319496 | tf_op jit(solution)/shard_map/halo_z/ppermute | solution.py:79
  9.2 2.1 %history_products.1 = (bf16[128,8192]{1,0:T(8,128)(2,1)S(1)}, f32[16,128]{1,0:T(8,128)S(1)}) custom-call(f32[3584,128]{1,0:T(8,128)S(1)} %bitcast.3), custom_call_target="tpu_custom_call" | custom-call | flops 268435456 | bytes 1835008 | tf_op jit(solution)/shard_map/history_products/pallas_call | solution.py:679
  11.2 0.2 halo_x.2.refs_0_
  11.4 0.0 collective-permute-done.2.refs_2_
  11.4 0.6 %collective-permute-done.3.refs_3_ = f32[26,8,128]{2,1,0:T(8,128)S(1)} collective-permute-done((f32[26,8,128]{2,1,0:T(8,128)S(1)}, f32[26,8,128]{2,1,0:T(8,128)S(1)}, u32[]{:S(2)}, u32[]{:S(2)}) %collective-permute-start.3) | collective-permute-done | bytes 106528 | tf_op jit(solution)/shard_map/halo_z/ppermute | solution.py:79
  12.1 0.1 halo_x.3
  12.2 1.9 %collective-permute-start.4 = (f32[6,8,128]{2,1,0:T(8,128)S(1)}, f32[6,8,128]{2,1,0:T(8,128)S(1)}, u32[]{:S(2)}, u32[]{:S(2)}) collective-permute-start(f32[6,8,128]{2,1,0:T(8,128)S(1)} %get-tuple-element.33), channel_id=1, source_target_pairs={{0,16},{1,17},{2,18},{3,19},{4,20},{5,21},{6,22},{7,23},{8,24},{9,... | collective-permute-start | bytes 73736 | tf_op jit(solution)/shard_map/halo_x/ppermute | solution.py:79
  14.1 2.1 %matrix_powers.1 = (f32[1536,128]{1,0:T(8,128)S(1)}, f32[1,5,2,2,8,128]{5,4,3,2,1,0:T(8,128)S(1)}, f32[24,128]{1,0:T(8,128)S(1)}) custom-call(f32[4,8,8,128]{3,2,1,0:T(8,128)S(1)} %get-tuple-element.21.start, f32[8,8,128]{2,1,0:T(8,128)S(1)} %get-tuple-element.22.diagonal, f32[5,8,8,128]{3,2,1,0:T(8,128)S(1)} %get-tuple-element.25.beyond, ...), custom_call_target="tpu_custom_call" | custom-call | flops 201326592 | bytes 131072 | tf_op jit(solution)/shard_map/matrix_powers/pallas_call | solution.py:699
  16.2 0.0 collective-permute-done.4.refs_0_
  16.3 0.9 %powers_at_ends.1 = (f32[32,128]{1,0:T(8,128)S(1)}, f32[1,192,128]{2,1,0:T(8,128)S(1)}) custom-call(f32[1,5,2,2,8,128]{5,4,3,2,1,0:T(8,128)S(1)} %get-tuple-element.31.own, bf16[128,1024]{1,0:T(8,128)(2,1)S(1)} %history_at_ends.1._.history_ends, f32[24,128]{1,0:T(8,128)S(1)} %get-tuple-element.32.before, ...), custom_call_target="tpu_custom_call" | custom-call | flops 1000000 | bytes 131072 | tf_op jit(solution)/shard_map/powers_at_ends/pallas_call | solution.py:716
  17.1 0.1 collective-permute-start.5
  17.2 1.2 %collective-permute-done.5 = f32[32,128]{1,0:T(8,128)S(1)} collective-permute-done((f32[32,128]{1,0:T(8,128)S(1)}, f32[32,128]{1,0:T(8,128)S(1)}, u32[]{:S(2)}, u32[]{:S(2)}) %collective-permute-start.5) | collective-permute-done | bytes 16416 | tf_op jit(solution)/shard_map/sum_over_devices/ppermute | solution.py:619
  18.4 0.8 %collective-permute-start.6 = (f32[32,128]{1,0:T(8,128)S(1)}, f32[32,128]{1,0:T(8,128)S(1)}, u32[]{:S(2)}, u32[]{:S(2)}) collective-permute-start(f32[32,128]{1,0:T(8,128)S(1)} %add.12), channel_id=1, source_target_pairs={{0,3},{1,2},{2,1},{3,0},{4,7},{5,6},{6,5},{7,4},{8,11},{9,10},{10,... | collective-permute-start | bytes 49160 | tf_op jit(solution)/shard_map/sum_over_devices/ppermute | solution.py:619
  19.2 2.3 %collective-permute-done.6 = f32[32,128]{1,0:T(8,128)S(1)} collective-permute-done((f32[32,128]{1,0:T(8,128)S(1)}, f32[32,128]{1,0:T(8,128)S(1)}, u32[]{:S(2)}, u32[]{:S(2)}) %collective-permute-start.6) | collective-permute-done | bytes 16416 | tf_op jit(solution)/shard_map/sum_over_devices/ppermute | solution.py:619
  21.5 1.5 %collective-permute-start.7 = (f32[32,128]{1,0:T(8,128)S(1)}, f32[32,128]{1,0:T(8,128)S(1)}, u32[]{:S(2)}, u32[]{:S(2)}) collective-permute-start(f32[32,128]{1,0:T(8,128)S(1)} %add.13), channel_id=1, source_target_pairs={{0,17},{1,16},{2,19},{3,18},{4,21},{5,20},{6,23},{7,22},{8,25},{9,... | collective-permute-start | bytes 49160 | tf_op jit(solution)/shard_map/sum_over_devices/ppermute | solution.py:619
  23.0 1.7 %collective-permute-done.7 = f32[32,128]{1,0:T(8,128)S(1)} collective-permute-done((f32[32,128]{1,0:T(8,128)S(1)}, f32[32,128]{1,0:T(8,128)S(1)}, u32[]{:S(2)}, u32[]{:S(2)}) %collective-permute-start.7) | collective-permute-done | bytes 16416 | tf_op jit(solution)/shard_map/sum_over_devices/ppermute | solution.py:619
  24.7 2.6 %collective-permute-start.8 = (f32[32,128]{1,0:T(8,128)S(1)}, f32[32,128]{1,0:T(8,128)S(1)}, u32[]{:S(2)}, u32[]{:S(2)}) collective-permute-start(f32[32,128]{1,0:T(8,128)S(1)} %add.14), channel_id=1, source_target_pairs={{0,5},{1,4},{2,7},{3,6},{4,1},{5,0},{6,3},{7,2},{8,13},{9,12},{10,... | collective-permute-start | bytes 49160 | tf_op jit(solution)/shard_map/sum_over_devices/ppermute | solution.py:619
  27.3 1.4 %collective-permute-done.8 = f32[32,128]{1,0:T(8,128)S(1)} collective-permute-done((f32[32,128]{1,0:T(8,128)S(1)}, f32[32,128]{1,0:T(8,128)S(1)}, u32[]{:S(2)}, u32[]{:S(2)}) %collective-permute-start.8) | collective-permute-done | bytes 16416 | tf_op jit(solution)/shard_map/sum_over_devices/ppermute | solution.py:619
  28.8 3.2 %collective-permute-start.9 = (f32[32,128]{1,0:T(8,128)S(1)}, f32[32,128]{1,0:T(8,128)S(1)}, u32[]{:S(2)}, u32[]{:S(2)}) collective-permute-start(f32[32,128]{1,0:T(8,128)S(1)} %add.15.refs_0_), channel_id=1, source_target_pairs={{0,9},{1,8},{2,11},{3,10},{4,13},{5,12},{6,15},{7,14},{8,1},{9,0},... | collective-permute-start | bytes 49160 | tf_op jit(solution)/shard_map/sum_over_devices/ppermute | solution.py:619
  32.0 0.8 %whole_basis.1.split = bf16[64,8192]{1,0:T(8,128)(2,1)S(1)} custom-call(f32[1536,128]{1,0:T(8,128)S(1)} %get-tuple-element.30.center, f32[1,192,128]{2,1,0:T(8,128)S(1)} %get-tuple-element.34.patch), custom_call_target="tpu_custom_call" | custom-call | flops 1000 | bytes 655360 | tf_op jit(solution)/shard_map/whole_basis/pallas_call | solution.py:727
  32.8 0.6 %collective-permute-done.9.refs_1_ = f32[32,128]{1,0:T(8,128)S(1)} collective-permute-done((f32[32,128]{1,0:T(8,128)S(1)}, f32[32,128]{1,0:T(8,128)S(1)}, u32[]{:S(2)}, u32[]{:S(2)}) %collective-permute-start.9) | collective-permute-done | bytes 16416 | tf_op jit(solution)/shard_map/sum_over_devices/ppermute | solution.py:619
  33.4 2.5 %orthonormalize.1 = (f32[20,64,128]{2,1,0:T(8,128)}, f32[20,20]{1,0:T(8,128)}) custom-call(bf16[128,8192]{1,0:T(8,128)(2,1)S(1)} %get-tuple-element.20.history_split, bf16[64,8192]{1,0:T(8,128)(2,1)S(1)} %whole_basis.1.split, f32[32,128]{1,0:T(8,128)S(1)} %add.15.refs_0_, f32[32,128]{1,0:T(8,128)S(1)} %collective-permute-done.9.refs_1_), custom_call_target="tpu_custom_call" | custom-call | flops 201326592 | bytes 655360 | tf_op jit(solution)/shard_map/orthonormalize/pallas_call | solution.py:737
  (4 shorter events, 0.0 us)
Async XLA Ops:
  1.5 5.5 %collective-permute-start = (f32[20,8,128]{2,1,0:T(8,128)S(1)}, f32[20,8,128]{2,1,0:T(8,128)S(1)}, u32[]{:S(2)}, u32[]{:S(2)}) collective-permute-start(f32[20,8,128]{2,1,0:T(8,128)S(1)} %get-tuple-element.23), channel_id=1, source_target_pairs={{0,4},{1,5},{2,6},{3,7},{4,0},{5,1},{6,2},{7,3},{8,12},{9,13},{10,... | collective-permute-start | bytes 245768 | tf_op jit(solution)/shard_map/halo_y/ppermute | solution.py:79
  4.6 2.4 %collective-permute-start.1 = (f32[20,8,128]{2,1,0:T(8,128)S(1)}, f32[20,8,128]{2,1,0:T(8,128)S(1)}, u32[]{:S(2)}, u32[]{:S(2)}) collective-permute-start(f32[20,8,128]{2,1,0:T(8,128)S(1)} %get-tuple-element.24), channel_id=1, source_target_pairs={{0,1},{1,0},{2,3},{3,2},{4,8},{5,9},{6,10},{7,11},{8,4},{9,5},{10,... | collective-permute-start | bytes 245768 | tf_op jit(solution)/shard_map/halo_y/ppermute | solution.py:79
  7.1 4.3 %collective-permute-start.2 = (f32[26,8,128]{2,1,0:T(8,128)S(1)}, f32[26,8,128]{2,1,0:T(8,128)S(1)}, u32[]{:S(2)}, u32[]{:S(2)}) collective-permute-start(f32[26,8,128]{2,1,0:T(8,128)S(1)} %get-tuple-element.27), channel_id=1, source_target_pairs={{0,1},{1,0},{2,3},{3,2},{4,5},{5,4},{6,7},{7,6},{8,9},{9,8},{10,11... | collective-permute-start | bytes 319496 | tf_op jit(solution)/shard_map/halo_z/ppermute | solution.py:79
  7.4 4.7 %collective-permute-start.3 = (f32[26,8,128]{2,1,0:T(8,128)S(1)}, f32[26,8,128]{2,1,0:T(8,128)S(1)}, u32[]{:S(2)}, u32[]{:S(2)}) collective-permute-start(f32[26,8,128]{2,1,0:T(8,128)S(1)} %get-tuple-element.28), channel_id=1, source_target_pairs={{0,16},{1,2},{2,1},{3,19},{4,20},{5,6},{6,5},{7,23},{8,24},{9,10},... | collective-permute-start | bytes 319496 | tf_op jit(solution)/shard_map/halo_z/ppermute | solution.py:79
  12.2 4.0 %collective-permute-start.4 = (f32[6,8,128]{2,1,0:T(8,128)S(1)}, f32[6,8,128]{2,1,0:T(8,128)S(1)}, u32[]{:S(2)}, u32[]{:S(2)}) collective-permute-start(f32[6,8,128]{2,1,0:T(8,128)S(1)} %get-tuple-element.33), channel_id=1, source_target_pairs={{0,16},{1,17},{2,18},{3,19},{4,20},{5,21},{6,22},{7,23},{8,24},{9,... | collective-permute-start | bytes 73736 | tf_op jit(solution)/shard_map/halo_x/ppermute | solution.py:79
  17.1 1.2 %collective-permute-start.5 = (f32[32,128]{1,0:T(8,128)S(1)}, f32[32,128]{1,0:T(8,128)S(1)}, u32[]{:S(2)}, u32[]{:S(2)}) collective-permute-start(f32[32,128]{1,0:T(8,128)S(1)} %get-tuple-element.35), channel_id=1, source_target_pairs={{0,1},{1,0},{2,3},{3,2},{4,5},{5,4},{6,7},{7,6},{8,9},{9,8},{10,11... | collective-permute-start | bytes 49160 | tf_op jit(solution)/shard_map/sum_over_devices/ppermute | solution.py:619
  18.4 3.2 %collective-permute-start.6 = (f32[32,128]{1,0:T(8,128)S(1)}, f32[32,128]{1,0:T(8,128)S(1)}, u32[]{:S(2)}, u32[]{:S(2)}) collective-permute-start(f32[32,128]{1,0:T(8,128)S(1)} %add.12), channel_id=1, source_target_pairs={{0,3},{1,2},{2,1},{3,0},{4,7},{5,6},{6,5},{7,4},{8,11},{9,10},{10,... | collective-permute-start | bytes 49160 | tf_op jit(solution)/shard_map/sum_over_devices/ppermute | solution.py:619
  21.5 3.2 %collective-permute-start.7 = (f32[32,128]{1,0:T(8,128)S(1)}, f32[32,128]{1,0:T(8,128)S(1)}, u32[]{:S(2)}, u32[]{:S(2)}) collective-permute-start(f32[32,128]{1,0:T(8,128)S(1)} %add.13), channel_id=1, source_target_pairs={{0,17},{1,16},{2,19},{3,18},{4,21},{5,20},{6,23},{7,22},{8,25},{9,... | collective-permute-start | bytes 49160 | tf_op jit(solution)/shard_map/sum_over_devices/ppermute | solution.py:619
  24.7 4.1 %collective-permute-start.8 = (f32[32,128]{1,0:T(8,128)S(1)}, f32[32,128]{1,0:T(8,128)S(1)}, u32[]{:S(2)}, u32[]{:S(2)}) collective-permute-start(f32[32,128]{1,0:T(8,128)S(1)} %add.14), channel_id=1, source_target_pairs={{0,5},{1,4},{2,7},{3,6},{4,1},{5,0},{6,3},{7,2},{8,13},{9,12},{10,... | collective-permute-start | bytes 49160 | tf_op jit(solution)/shard_map/sum_over_devices/ppermute | solution.py:619
  28.8 4.6 %collective-permute-start.9 = (f32[32,128]{1,0:T(8,128)S(1)}, f32[32,128]{1,0:T(8,128)S(1)}, u32[]{:S(2)}, u32[]{:S(2)}) collective-permute-start(f32[32,128]{1,0:T(8,128)S(1)} %add.15.refs_0_), channel_id=1, source_target_pairs={{0,9},{1,8},{2,11},{3,10},{4,13},{5,12},{6,15},{7,14},{8,1},{9,0},... | collective-permute-start | bytes 49160 | tf_op jit(solution)/shard_map/sum_over_devices/ppermute | solution.py:619

commit v8 on v7

--- a/solution.py
+++ b/solution.py
@@ -103,15 +103,22 @@
         copy.start()
     row, _ = iotas()
     even = is_even("gy")
+    highs, lows = [], []
     for f in range(fields + 1):
         copies[f].wait()
         for p in range(4):
             one, two = (start[f, z] if f < fields else diagonal[z] for z in (p, p + 4))
-            to_high = jnp.where(row < 4, roll(one, 4, 0), two)
-            to_low = jnp.where(row < 4, one, roll(two, 4, 0))
-            sends[0][4 * f + p] = jnp.where(even, to_high, to_low)
-            if len(sends) > 1:
-                sends[1][4 * f + p] = jnp.where(even, to_low, to_high)
+            highs.append(jnp.where(row < 4, roll(one, 4, 0), two))
+            lows.append(jnp.where(row < 4, one, roll(two, 4, 0)))
+    last_high, last_low = highs.pop(), lows.pop()
+    for p in range(3):
+        k = 4 * fields + p
+        highs[k] = jnp.where((row & 3) == 0, roll(last_high, -1 - p, 0), highs[k])
+        lows[k] = jnp.where((row & 3) == 3, roll(last_low, 3 - p, 0), lows[k])
+    for k, (to_high, to_low) in enumerate(zip(highs, lows)):
+        sends[0][k] = jnp.where(even, to_high, to_low)
+        if len(sends) > 1:
+            sends[1][k] = jnp.where(even, to_low, to_high)
 
 
 def pack_z(fields, count, ways, start, diagonal, _, *refs):
@@ -121,7 +128,13 @@
     even = is_even("gz")
     for f in range(fields + 1):
         for p in range(4):
-            low, high = pick(4 * f + p)
+            if f == fields and p == 3:
+                low = high = jnp.zeros((Y, X), F32)
+                for q, (from_low, from_high) in enumerate(pick(4 * f + i) for i in range(3)):
+                    low = jnp.where((row & 3) == q + 1, roll(from_low, q + 1, 0), low)
+                    high = jnp.where((row & 3) == q, roll(from_high, q - 3, 0), high)
+            else:
+                low, high = pick(4 * f + p)
             beyond[f, p] = jnp.where(row < 4, high, roll(low, 4, 0))
             beyond[f, p + 4] = jnp.where(row < 4, roll(high, 4, 0), low)
     inner = (row == 2) | (row == 3)
@@ -638,7 +651,7 @@
         start, diagonal, *sends = call(
             functools.partial(pack_y, fields),
             [(start.shape, F32), (diagonal.shape, F32)]
-            + [((4 * all_fields, Y, X), F32)] * ways["gy"],
+            + [((4 * all_fields - 1, Y, X), F32)] * ways["gy"],
             1000,
             start.size * 4,
             [pltpu.SemaphoreType.DMA((all_fields,))],

time: 36.1 us -> 36.1 us (level)
  no operation moved by 1% of the time
where the time goes in v8:
time: 36.1 us; the launch traced here: 35.9 us
  starting transfers between devices  15.2 us (42%)
  Pallas kernels  11.7 us (32%)
  waiting for transfers between devices  8.32 us (23%)
  between operations  0.72 us (2%)
    ppermute x5, starting transfers between devices, sum_over_devices(): others = lax.ppermute(array, AXES, [(i, i ^ (bit | 1)) for i in devices])  8.12 us
    ppermute x5, waiting for transfers between devices, sum_over_devices(): others = lax.ppermute(array, AXES, [(i, i ^ (bit | 1)) for i in devices])  7.31 us
    ppermute x5, starting transfers between devices, swaps(): lax.ppermute(a, AXES, pairs)  7.05 us
    pallas_call x1, Pallas kernels, on_device(): call(functools.partial(finish, columns, cells), [((columns, CELLS, X), F3...  2.51 us
    pallas_call x1, Pallas kernels, on_device(): call(functools.partial(powers, fields, count['gx']), [((BROWS * CELLS, X)...  2.11 us
    pallas_call x1, Pallas kernels, on_device(): call(functools.partial(history_kernel, history_count), [((2 * HPAD, CELLS...  2.05 us
    pallas_call x1, Pallas kernels, on_device(): call(load_history, [(history.shape, F32)], 1000, history.size * 4, [pltpu...  1.51 us
    ppermute x5, waiting for transfers between devices, swaps(): lax.ppermute(a, AXES, pairs)  1 us
  transfers between devices with their start and end apart: 10, of which 7 were waited for; matrix products, arithmetic and copies ran while one was open for 0% of the time, Pallas kernels for 20%

profile of v8, /device:TPU:0, one launch (start us, length us, event | category | flops | bytes accessed | tf_op | source)
XLA Modules:
  0.0 35.9 jit_solution(9809411614901002522)
XLA Ops:
  0.6 0.9 %halo_y.1 = (f32[4,8,8,128]{3,2,1,0:T(8,128)S(1)}, f32[8,8,128]{2,1,0:T(8,128)S(1)}, f32[19,8,128]{2,1,0:T(8,128)S(1)}, f32[19,8,128]{2,1,0:T(8,128)S(1)}) custom-call(f32[4,8,8,128]{3,2,1,0:T(8,128)} %start_there.1, f32[8,8,128]{2,1,0:T(8,128)} %diagonal_there.1), custom_call_target="tpu_custom_call" | custom-call | flops 1000 | bytes 131072 | tf_op jit(solution)/shard_map/halo_y/pallas_call | solution.py:651
  1.5 3.1 %collective-permute-start = (f32[19,8,128]{2,1,0:T(8,128)S(1)}, f32[19,8,128]{2,1,0:T(8,128)S(1)}, u32[]{:S(2)}, u32[]{:S(2)}) collective-permute-start(f32[19,8,128]{2,1,0:T(8,128)S(1)} %get-tuple-element.23), channel_id=1, source_target_pairs={{0,4},{1,5},{2,6},{3,7},{4,0},{5,1},{6,2},{7,3},{8,12},{9,13},{10,... | collective-permute-start | bytes 233480 | tf_op jit(solution)/shard_map/halo_y/ppermute | solution.py:79
  4.6 0.0 collective-permute-start.1
  4.6 1.5 %load_history.1 = f32[56,8,8,128]{3,2,1,0:T(8,128)S(1)} custom-call(f32[56,8,8,128]{3,2,1,0:T(8,128)} %history.1), custom_call_target="tpu_custom_call" | custom-call | flops 1000 | bytes 1835008 | tf_op jit(solution)/shard_map/load_history/pallas_call | solution.py:664
  6.1 0.6 %history_at_ends.1._.history_ends = bf16[128,1024]{1,0:T(8,128)(2,1)S(1)} custom-call(f32[3584,128]{1,0:T(8,128)S(1)} %bitcast.2), custom_call_target="tpu_custom_call" | custom-call | flops 1000 | bytes 917504 | tf_op jit(solution)/shard_map/history_at_ends/pallas_call | solution.py:675
  6.7 0.3 collective-permute-done.refs_0_
  7.0 0.0 collective-permute-done.1.refs_1_
  7.0 0.1 halo_z.1
  7.1 0.3 collective-permute-start.2
  7.4 1.8 %collective-permute-start.3 = (f32[26,8,128]{2,1,0:T(8,128)S(1)}, f32[26,8,128]{2,1,0:T(8,128)S(1)}, u32[]{:S(2)}, u32[]{:S(2)}) collective-permute-start(f32[26,8,128]{2,1,0:T(8,128)S(1)} %get-tuple-element.28), channel_id=1, source_target_pairs={{0,16},{1,2},{2,1},{3,19},{4,20},{5,6},{6,5},{7,23},{8,24},{9,10},... | collective-permute-start | bytes 319496 | tf_op jit(solution)/shard_map/halo_z/ppermute | solution.py:79
  9.2 2.0 %history_products.1 = (bf16[128,8192]{1,0:T(8,128)(2,1)S(1)}, f32[16,128]{1,0:T(8,128)S(1)}) custom-call(f32[3584,128]{1,0:T(8,128)S(1)} %bitcast.3), custom_call_target="tpu_custom_call" | custom-call | flops 268435456 | bytes 1835008 | tf_op jit(solution)/shard_map/history_products/pallas_call | solution.py:692
  11.2 0.2 halo_x.2.refs_0_
  11.4 0.0 collective-permute-done.2.refs_2_
  11.4 0.7 %collective-permute-done.3.refs_3_ = f32[26,8,128]{2,1,0:T(8,128)S(1)} collective-permute-done((f32[26,8,128]{2,1,0:T(8,128)S(1)}, f32[26,8,128]{2,1,0:T(8,128)S(1)}, u32[]{:S(2)}, u32[]{:S(2)}) %collective-permute-start.3) | collective-permute-done | bytes 106528 | tf_op jit(solution)/shard_map/halo_z/ppermute | solution.py:79
  12.1 0.1 halo_x.3
  12.2 1.8 %collective-permute-start.4 = (f32[6,8,128]{2,1,0:T(8,128)S(1)}, f32[6,8,128]{2,1,0:T(8,128)S(1)}, u32[]{:S(2)}, u32[]{:S(2)}) collective-permute-start(f32[6,8,128]{2,1,0:T(8,128)S(1)} %get-tuple-element.33), channel_id=1, source_target_pairs={{0,16},{1,17},{2,18},{3,19},{4,20},{5,21},{6,22},{7,23},{8,24},{9,... | collective-permute-start | bytes 73736 | tf_op jit(solution)/shard_map/halo_x/ppermute | solution.py:79
  14.1 2.1 %matrix_powers.1 = (f32[1536,128]{1,0:T(8,128)S(1)}, f32[1,5,2,2,8,128]{5,4,3,2,1,0:T(8,128)S(1)}, f32[24,128]{1,0:T(8,128)S(1)}) custom-call(f32[4,8,8,128]{3,2,1,0:T(8,128)S(1)} %get-tuple-element.21.start, f32[8,8,128]{2,1,0:T(8,128)S(1)} %get-tuple-element.22.diagonal, f32[5,8,8,128]{3,2,1,0:T(8,128)S(1)} %get-tuple-element.25.beyond, ...), custom_call_target="tpu_custom_call" | custom-call | flops 201326592 | bytes 131072 | tf_op jit(solution)/shard_map/matrix_powers/pallas_call | solution.py:712
  16.2 0.0 collective-permute-done.4.refs_0_
  16.2 0.9 %powers_at_ends.1 = (f32[32,128]{1,0:T(8,128)S(1)}, f32[1,192,128]{2,1,0:T(8,128)S(1)}) custom-call(f32[1,5,2,2,8,128]{5,4,3,2,1,0:T(8,128)S(1)} %get-tuple-element.31.own, bf16[128,1024]{1,0:T(8,128)(2,1)S(1)} %history_at_ends.1._.history_ends, f32[24,128]{1,0:T(8,128)S(1)} %get-tuple-element.32.before, ...), custom_call_target="tpu_custom_call" | custom-call | flops 1000000 | bytes 131072 | tf_op jit(solution)/shard_map/powers_at_ends/pallas_call | solution.py:729
  17.1 0.1 collective-permute-start.5
  17.2 1.2 %collective-permute-done.5 = f32[32,128]{1,0:T(8,128)S(1)} collective-permute-done((f32[32,128]{1,0:T(8,128)S(1)}, f32[32,128]{1,0:T(8,128)S(1)}, u32[]{:S(2)}, u32[]{:S(2)}) %collective-permute-start.5) | collective-permute-done | bytes 16416 | tf_op jit(solution)/shard_map/sum_over_devices/ppermute | solution.py:632
  18.3 0.8 %collective-permute-start.6 = (f32[32,128]{1,0:T(8,128)S(1)}, f32[32,128]{1,0:T(8,128)S(1)}, u32[]{:S(2)}, u32[]{:S(2)}) collective-permute-start(f32[32,128]{1,0:T(8,128)S(1)} %add.12), channel_id=1, source_target_pairs={{0,3},{1,2},{2,1},{3,0},{4,7},{5,6},{6,5},{7,4},{8,11},{9,10},{10,... | collective-permute-start | bytes 49160 | tf_op jit(solution)/shard_map/sum_over_devices/ppermute | solution.py:632
  19.2 2.3 %collective-permute-done.6 = f32[32,128]{1,0:T(8,128)S(1)} collective-permute-done((f32[32,128]{1,0:T(8,128)S(1)}, f32[32,128]{1,0:T(8,128)S(1)}, u32[]{:S(2)}, u32[]{:S(2)}) %collective-permute-start.6) | collective-permute-done | bytes 16416 | tf_op jit(solution)/shard_map/sum_over_devices/ppermute | solution.py:632
  21.5 1.4 %collective-permute-start.7 = (f32[32,128]{1,0:T(8,128)S(1)}, f32[32,128]{1,0:T(8,128)S(1)}, u32[]{:S(2)}, u32[]{:S(2)}) collective-permute-start(f32[32,128]{1,0:T(8,128)S(1)} %add.13), channel_id=1, source_target_pairs={{0,17},{1,16},{2,19},{3,18},{4,21},{5,20},{6,23},{7,22},{8,25},{9,... | collective-permute-start | bytes 49160 | tf_op jit(solution)/shard_map/sum_over_devices/ppermute | solution.py:632
  23.0 1.7 %collective-permute-done.7 = f32[32,128]{1,0:T(8,128)S(1)} collective-permute-done((f32[32,128]{1,0:T(8,128)S(1)}, f32[32,128]{1,0:T(8,128)S(1)}, u32[]{:S(2)}, u32[]{:S(2)}) %collective-permute-start.7) | collective-permute-done | bytes 16416 | tf_op jit(solution)/shard_map/sum_over_devices/ppermute | solution.py:632
  24.7 2.6 %collective-permute-start.8 = (f32[32,128]{1,0:T(8,128)S(1)}, f32[32,128]{1,0:T(8,128)S(1)}, u32[]{:S(2)}, u32[]{:S(2)}) collective-permute-start(f32[32,128]{1,0:T(8,128)S(1)} %add.14), channel_id=1, source_target_pairs={{0,5},{1,4},{2,7},{3,6},{4,1},{5,0},{6,3},{7,2},{8,13},{9,12},{10,... | collective-permute-start | bytes 49160 | tf_op jit(solution)/shard_map/sum_over_devices/ppermute | solution.py:632
  27.3 1.4 %collective-permute-done.8 = f32[32,128]{1,0:T(8,128)S(1)} collective-permute-done((f32[32,128]{1,0:T(8,128)S(1)}, f32[32,128]{1,0:T(8,128)S(1)}, u32[]{:S(2)}, u32[]{:S(2)}) %collective-permute-start.8) | collective-permute-done | bytes 16416 | tf_op jit(solution)/shard_map/sum_over_devices/ppermute | solution.py:632
  28.7 3.2 %collective-permute-start.9 = (f32[32,128]{1,0:T(8,128)S(1)}, f32[32,128]{1,0:T(8,128)S(1)}, u32[]{:S(2)}, u32[]{:S(2)}) collective-permute-start(f32[32,128]{1,0:T(8,128)S(1)} %add.15.refs_0_), channel_id=1, source_target_pairs={{0,9},{1,8},{2,11},{3,10},{4,13},{5,12},{6,15},{7,14},{8,1},{9,0},... | collective-permute-start | bytes 49160 | tf_op jit(solution)/shard_map/sum_over_devices/ppermute | solution.py:632
  31.9 0.8 %whole_basis.1.split = bf16[64,8192]{1,0:T(8,128)(2,1)S(1)} custom-call(f32[1536,128]{1,0:T(8,128)S(1)} %get-tuple-element.30.center, f32[1,192,128]{2,1,0:T(8,128)S(1)} %get-tuple-element.34.patch), custom_call_target="tpu_custom_call" | custom-call | flops 1000 | bytes 655360 | tf_op jit(solution)/shard_map/whole_basis/pallas_call | solution.py:740
  32.7 0.6 %collective-permute-done.9.refs_1_ = f32[32,128]{1,0:T(8,128)S(1)} collective-permute-done((f32[32,128]{1,0:T(8,128)S(1)}, f32[32,128]{1,0:T(8,128)S(1)}, u32[]{:S(2)}, u32[]{:S(2)}) %collective-permute-start.9) | collective-permute-done | bytes 16416 | tf_op jit(solution)/shard_map/sum_over_devices/ppermute | solution.py:632
  33.4 2.5 %orthonormalize.1 = (f32[20,64,128]{2,1,0:T(8,128)}, f32[20,20]{1,0:T(8,128)}) custom-call(bf16[128,8192]{1,0:T(8,128)(2,1)S(1)} %get-tuple-element.20.history_split, bf16[64,8192]{1,0:T(8,128)(2,1)S(1)} %whole_basis.1.split, f32[32,128]{1,0:T(8,128)S(1)} %add.15.refs_0_, f32[32,128]{1,0:T(8,128)S(1)} %collective-permute-done.9.refs_1_), custom_call_target="tpu_custom_call" | custom-call | flops 201326592 | bytes 655360 | tf_op jit(solution)/shard_map/orthonormalize/pallas_call | solution.py:750
  (4 shorter events, 0.0 us)
Async XLA Ops:
  1.5 5.5 %collective-permute-start = (f32[19,8,128]{2,1,0:T(8,128)S(1)}, f32[19,8,128]{2,1,0:T(8,128)S(1)}, u32[]{:S(2)}, u32[]{:S(2)}) collective-permute-start(f32[19,8,128]{2,1,0:T(8,128)S(1)} %get-tuple-element.23), channel_id=1, source_target_pairs={{0,4},{1,5},{2,6},{3,7},{4,0},{5,1},{6,2},{7,3},{8,12},{9,13},{10,... | collective-permute-start | bytes 233480 | tf_op jit(solution)/shard_map/halo_y/ppermute | solution.py:79
  4.6 2.4 %collective-permute-start.1 = (f32[19,8,128]{2,1,0:T(8,128)S(1)}, f32[19,8,128]{2,1,0:T(8,128)S(1)}, u32[]{:S(2)}, u32[]{:S(2)}) collective-permute-start(f32[19,8,128]{2,1,0:T(8,128)S(1)} %get-tuple-element.24), channel_id=1, source_target_pairs={{0,1},{1,0},{2,3},{3,2},{4,8},{5,9},{6,10},{7,11},{8,4},{9,5},{10,... | collective-permute-start | bytes 233480 | tf_op jit(solution)/shard_map/halo_y/ppermute | solution.py:79
  7.1 4.3 %collective-permute-start.2 = (f32[26,8,128]{2,1,0:T(8,128)S(1)}, f32[26,8,128]{2,1,0:T(8,128)S(1)}, u32[]{:S(2)}, u32[]{:S(2)}) collective-permute-start(f32[26,8,128]{2,1,0:T(8,128)S(1)} %get-tuple-element.27), channel_id=1, source_target_pairs={{0,1},{1,0},{2,3},{3,2},{4,5},{5,4},{6,7},{7,6},{8,9},{9,8},{10,11... | collective-permute-start | bytes 319496 | tf_op jit(solution)/shard_map/halo_z/ppermute | solution.py:79
  7.4 4.7 %collective-permute-start.3 = (f32[26,8,128]{2,1,0:T(8,128)S(1)}, f32[26,8,128]{2,1,0:T(8,128)S(1)}, u32[]{:S(2)}, u32[]{:S(2)}) collective-permute-start(f32[26,8,128]{2,1,0:T(8,128)S(1)} %get-tuple-element.28), channel_id=1, source_target_pairs={{0,16},{1,2},{2,1},{3,19},{4,20},{5,6},{6,5},{7,23},{8,24},{9,10},... | collective-permute-start | bytes 319496 | tf_op jit(solution)/shard_map/halo_z/ppermute | solution.py:79
  12.2 4.0 %collective-permute-start.4 = (f32[6,8,128]{2,1,0:T(8,128)S(1)}, f32[6,8,128]{2,1,0:T(8,128)S(1)}, u32[]{:S(2)}, u32[]{:S(2)}) collective-permute-start(f32[6,8,128]{2,1,0:T(8,128)S(1)} %get-tuple-element.33), channel_id=1, source_target_pairs={{0,16},{1,17},{2,18},{3,19},{4,20},{5,21},{6,22},{7,23},{8,24},{9,... | collective-permute-start | bytes 73736 | tf_op jit(solution)/shard_map/halo_x/ppermute | solution.py:79
  17.1 1.2 %collective-permute-start.5 = (f32[32,128]{1,0:T(8,128)S(1)}, f32[32,128]{1,0:T(8,128)S(1)}, u32[]{:S(2)}, u32[]{:S(2)}) collective-permute-start(f32[32,128]{1,0:T(8,128)S(1)} %get-tuple-element.35), channel_id=1, source_target_pairs={{0,1},{1,0},{2,3},{3,2},{4,5},{5,4},{6,7},{7,6},{8,9},{9,8},{10,11... | collective-permute-start | bytes 49160 | tf_op jit(solution)/shard_map/sum_over_devices/ppermute | solution.py:632
  18.3 3.2 %collective-permute-start.6 = (f32[32,128]{1,0:T(8,128)S(1)}, f32[32,128]{1,0:T(8,128)S(1)}, u32[]{:S(2)}, u32[]{:S(2)}) collective-permute-start(f32[32,128]{1,0:T(8,128)S(1)} %add.12), channel_id=1, source_target_pairs={{0,3},{1,2},{2,1},{3,0},{4,7},{5,6},{6,5},{7,4},{8,11},{9,10},{10,... | collective-permute-start | bytes 49160 | tf_op jit(solution)/shard_map/sum_over_devices/ppermute | solution.py:632
  21.5 3.2 %collective-permute-start.7 = (f32[32,128]{1,0:T(8,128)S(1)}, f32[32,128]{1,0:T(8,128)S(1)}, u32[]{:S(2)}, u32[]{:S(2)}) collective-permute-start(f32[32,128]{1,0:T(8,128)S(1)} %add.13), channel_id=1, source_target_pairs={{0,17},{1,16},{2,19},{3,18},{4,21},{5,20},{6,23},{7,22},{8,25},{9,... | collective-permute-start | bytes 49160 | tf_op jit(solution)/shard_map/sum_over_devices/ppermute | solution.py:632
  24.7 4.1 %collective-permute-start.8 = (f32[32,128]{1,0:T(8,128)S(1)}, f32[32,128]{1,0:T(8,128)S(1)}, u32[]{:S(2)}, u32[]{:S(2)}) collective-permute-start(f32[32,128]{1,0:T(8,128)S(1)} %add.14), channel_id=1, source_target_pairs={{0,5},{1,4},{2,7},{3,6},{4,1},{5,0},{6,3},{7,2},{8,13},{9,12},{10,... | collective-permute-start | bytes 49160 | tf_op jit(solution)/shard_map/sum_over_devices/ppermute | solution.py:632
  28.7 4.6 %collective-permute-start.9 = (f32[32,128]{1,0:T(8,128)S(1)}, f32[32,128]{1,0:T(8,128)S(1)}, u32[]{:S(2)}, u32[]{:S(2)}) collective-permute-start(f32[32,128]{1,0:T(8,128)S(1)} %add.15.refs_0_), channel_id=1, source_target_pairs={{0,9},{1,8},{2,11},{3,10},{4,13},{5,12},{6,15},{7,14},{8,1},{9,0},... | collective-permute-start | bytes 49160 | tf_op jit(solution)/shard_map/sum_over_devices/ppermute | solution.py:632
